TPU v7x, 512 devices: a whole 4x8x8 slice. The times are simulated.
512 devices in a mesh: dp: 64 (over z, y), tensor: 8 (over x, core).
Axes of the slice: x: 4, y: 8, z: 8, core: 2. Of those that a mesh axis runs over, the one named last changes fastest.
Arguments:
- tokens: bfloat16 [32768, 4096], P(('dp', 'tensor')), may hold values from -6 to 6
- repack_plan: int32 [32768], P(('dp', 'tensor')), may hold values from 0 to 32767, as said below
- document_ids: int32 [32768], P(('dp', 'tensor')), may hold values from 0 to 255, never falling along the last dimension, each value on 1 to 512 neighbouring positions
- norm_gain: float32 [4096], replicated, may hold values from 0.1 to 1.9
- w_query: bfloat16 [4096, 4096], P('dp', 'tensor'), may hold values from -0.328125 to 0.328125
- w_key: bfloat16 [4096, 1024], P('dp', 'tensor'), may hold values from -0.328125 to 0.328125
- w_value: bfloat16 [4096, 1024], P('dp', 'tensor'), may hold values from -0.09375 to 0.09375
- w_out: bfloat16 [4096, 4096], P('tensor', 'dp'), may hold values from -0.1875 to 0.1875
Outputs:
- attended_out: bfloat16 [32768, 4096], P(('dp', 'tensor'))
Inputs may be any that keep to these rules, and one draw needn't show every extreme that they name: A permutation of the rows of the packed array. Token r of the device at dp index i and tensor index t goes to the pack repack_plan[r] // 512, within it to the block of tensor index t (so (repack_plan[r] % 512) // 64 == t); every block of 64 rows of a pack receives one token for each of its rows; of the 64 tokens of one device at most 2 go to one pack, and some device sends exactly 2 to some pack.
All inputs are finite; a program needn't handle non-finite values.
Results may differ from a plain program's by a relative error of at most 0.025.
The roundings to bfloat16 on the way count: a program that leaves them out, or rounds other values in their place, can miss the bound.
Values may be sent and summed in bfloat16 or wider, within the bound.
No kernel may reach another device: no remote copies, remote signals or barrier semaphores. Data moves between devices by JAX's collectives and lax.ppermute only.
A program may use at most 64 MiB of HBM per device.

v0:
```python
import jax
import jax.numpy as jnp
from jax import lax
from jax.sharding import PartitionSpec as P

HEAD_DIM = 128


def rms_rows(states, norm_gain):
    floats = states.astype(jnp.float32)
    mean_square = jnp.mean(floats * floats, axis=-1, keepdims=True)
    return (floats * lax.rsqrt(mean_square + 1e-05) * norm_gain).astype(jnp.bfloat16)


def attend_pack(query, key_rows, value_rows, doc_rows):
    count = query.shape[0]
    kv_count = key_rows.shape[1] // HEAD_DIM
    group = query.shape[1] // HEAD_DIM // kv_count
    queries = query.reshape(count, kv_count, group, HEAD_DIM)
    keys_view = key_rows.reshape(count, kv_count, HEAD_DIM)
    values_view = value_rows.reshape(count, kv_count, HEAD_DIM)
    scores = jnp.einsum("thgd,shd->hgts", queries, keys_view, preferred_element_type=jnp.float32)
    scores = scores / jnp.sqrt(jnp.float32(HEAD_DIM))
    positions = jnp.arange(count, dtype=jnp.int32)
    allowed = (doc_rows[:, None] == doc_rows[None, :]) & (positions[:, None] >= positions[None, :])
    scores = jnp.where(allowed, scores, jnp.float32(-1e30))
    highest = jnp.max(scores, axis=-1, keepdims=True)
    weights = jnp.where(allowed, jnp.exp(scores - highest), jnp.float32(0.0))
    probs = (weights / jnp.sum(weights, axis=-1, keepdims=True)).astype(jnp.bfloat16)
    mixed = jnp.einsum("hgts,shd->thgd", probs, values_view, preferred_element_type=jnp.float32)
    return mixed.reshape(count, kv_count * group * HEAD_DIM).astype(jnp.bfloat16)


def on_device(tokens, repack_plan, document_ids, norm_gain, w_query, w_key, w_value, w_out):
    row_count = tokens.shape[0]
    peer_count = lax.axis_size("dp")
    pack_rows = row_count * lax.axis_size("tensor")
    capacity = max(2, 2 * row_count // peer_count)
    slot_count = peer_count * capacity
    target = repack_plan // pack_rows
    landing = repack_plan % row_count
    positions = jnp.arange(row_count, dtype=jnp.int32)
    same_pack = target[:, None] == target[None, :]
    earlier = positions[None, :] < positions[:, None]
    slot_rank = jnp.sum(jnp.where(same_pack & earlier, 1, 0), axis=1).astype(jnp.int32)
    slot_of = target * capacity + slot_rank
    selector = slot_of[None, :] == jnp.arange(slot_count, dtype=jnp.int32)[:, None]
    outgoing = jnp.dot(
        selector.astype(jnp.bfloat16), tokens, preferred_element_type=jnp.float32
    ).astype(jnp.bfloat16)
    landing_marks = jnp.sum(jnp.where(selector, landing[None, :] + 1, 0), axis=1)
    arrived, arrived_marks = (
        lax.all_to_all(outgoing, "dp", split_axis=0, concat_axis=0, tiled=True),
        lax.all_to_all(landing_marks, "dp", split_axis=0, concat_axis=0, tiled=True),
    )
    settle = arrived_marks[None, :] == positions[:, None] + 1
    owned = jnp.dot(
        settle.astype(jnp.bfloat16), arrived, preferred_element_type=jnp.float32
    ).astype(jnp.bfloat16)
    whole_pack, doc_rows = (
        lax.all_gather(owned, "tensor", axis=0, tiled=True),
        lax.all_gather(document_ids, "tensor", axis=0, tiled=True),
    )
    normed = rms_rows(whole_pack, norm_gain)
    query_sum = jnp.dot(
        normed,
        lax.all_gather(w_query, "dp", axis=0, tiled=True),
        preferred_element_type=jnp.float32,
    )
    key_sum = jnp.dot(
        normed, lax.all_gather(w_key, "dp", axis=0, tiled=True), preferred_element_type=jnp.float32
    )
    value_sum = jnp.dot(
        normed,
        lax.all_gather(w_value, "dp", axis=0, tiled=True),
        preferred_element_type=jnp.float32,
    )
    attended = attend_pack(
        query_sum.astype(jnp.bfloat16),
        key_sum.astype(jnp.bfloat16),
        value_sum.astype(jnp.bfloat16),
        doc_rows,
    )
    out_full = lax.all_gather(w_out, "dp", axis=1, tiled=True)
    return lax.psum_scatter(
        jnp.dot(attended, out_full, preferred_element_type=jnp.float32).astype(jnp.bfloat16),
        "tensor",
        scatter_dimension=0,
        tiled=True,
    )


def solution(mesh):
    return jax.shard_map(
        on_device,
        mesh=mesh,
        in_specs=(
            P(("dp", "tensor"), None),
            P(("dp", "tensor")),
            P(("dp", "tensor")),
            P(),
            P("dp", "tensor"),
            P("dp", "tensor"),
            P("dp", "tensor"),
            P("tensor", "dp"),
        ),
        out_specs=P(("dp", "tensor"), None),
        check_vma=False,
    )
```

profile of v0, /device:TPU:1, one launch (start us, length us, event | category | flops | bytes accessed | tf_op | source)
XLA Modules:
  0.0 496.6 jit_solution(16805036724890042220)
XLA Ops:
  6.5 0.7 fusion.20
  7.6 0.8 all_to_all.14
  8.3 17.1 %all-to-all-start = ((s32[64,2,1]{1,2,0:T(1,128)}), s32[64,2,1]{1,2,0:T(1,128)S(1)}, u32[]{:S(2)}, u32[]{:S(2)}) async-start(s32[64,2,1]{1,2,0:T(1,128)} %bitcast), calls=%async_computation | async-start | bytes 65536 | tf_op jit(solution)/shard_map/all_to_all | solution.py:54
  25.5 0.5 convolution_convert_fusion.1
  26.0 1.5 all_to_all.16
  27.5 8.7 %all-to-all-done = s32[64,2,1]{1,2,0:T(1,128)S(1)} async-done(((s32[64,2,1]{1,2,0:T(1,128)}), s32[64,2,1]{1,2,0:T(1,128)S(1)}, u32[]{:S(2)}, u32[]{:S(2)}) %all-to-all-start) | async-done | bytes 544 | tf_op jit(solution)/shard_map/all_to_all | solution.py:54
  36.2 4.7 all-to-all-start.1
  40.9 0.5 broadcast.55
  41.5 0.7 reduce.5
  42.3 24.2 %all-to-all-done.1 = bf16[64,2,4096]{2,1,0:T(2,128)(2,1)S(1)} async-done(((bf16[64,2,4096]{2,1,0:T(2,128)(2,1)}), bf16[64,2,4096]{2,1,0:T(2,128)(2,1)S(1)}, u32[]{:S(2)}, u32[]{:S(2)}) %all-to-all-start.1) | async-done | bytes 1048608 | tf_op jit(solution)/shard_map/all_to_all | solution.py:53
  66.6 0.4 all_to_all.18
  67.0 1.1 convolution_convert_fusion.2
  68.2 0.7 all-gather.12.cloned.1.call-update
  69.0 0.7 all-gather.10.cloned.1.call-update
  69.7 0.5 all-gather.8.cloned.1.call-update
  70.3 0.5 all-gather.14.cloned.1.call-update
  70.9 1.3 dynamic-slice
  72.9 0.2 dynamic-update-slice
  73.2 12.1 %all-reduce = s32[512]{0:T(512)S(1)} all-reduce(s32[512]{0:T(512)S(1)} %dynamic-update-slice), channel_id=1, replica_groups=mesh['dp'=64,'tensor'=8] {'tensor'}, use_global_device_ids=true, to_apply=%add | all-reduce | flops 512 | bytes 4096
  85.3 0.2 fusion.14
  85.5 19.5 %all-gather.6.cloned.1.call-done = bf16[512,4096]{1,0:T(8,128)(2,1)} async-done(((bf16[64,4096]{1,0:T(8,128)(2,1)}), bf16[512,4096]{1,0:T(8,128)(2,1)}) %all-gather.6.cloned.1.call-update) | async-done | bytes 4194320 | tf_op jit(solution)/shard_map/all_gather | solution.py:61
  105.0 3.1 fusion
  108.1 82.8 %all-gather.12.cloned.1.call-done = bf16[4096,512]{1,0:T(8,128)(2,1)} async-done(((bf16[64,512]{1,0:T(8,128)(2,1)}), bf16[4096,512]{1,0:T(8,128)(2,1)}) %all-gather.12.cloned.1.call-update) | async-done | bytes 4194320 | tf_op jit(solution)/shard_map/all_gather | solution.py:67
  190.9 5.9 %convolution_convert_fusion.3 = bf16[512,512]{0,1:T(8,128)(2,1)S(1)} fusion(bf16[4096,512]{1,0:T(8,128)(2,1)} %all-gather.12.cloned.1.call-done, bf16[512,4096]{1,0:T(8,128)(2,1)} %all-gather.6.cloned.1.call-done, f32[4096]{0:T(1024)S(1)} %copy-done.1, f32[512]{0:T(512)S(1)} %add_rsqrt_fusion), kind=kOutput, calls=%fused_computation.16 | convolution fusion | flops 2156134400 | bytes 8931328 | tf_op jit(solution)/shard_map/dot_general | solution.py:65
  196.9 75.3 %all-gather.10.cloned.1.call-done = bf16[4096,128]{1,0:T(8,128)(2,1)} async-done(((bf16[64,128]{1,0:T(8,128)(2,1)}), bf16[4096,128]{1,0:T(8,128)(2,1)}) %all-gather.10.cloned.1.call-update) | async-done | bytes 1048592 | tf_op jit(solution)/shard_map/all_gather | solution.py:71
  272.1 7.4 %fusion.3 = (f32[4,512]{1,0:T(4,128)S(1)}, f32[512,512,4]{1,0,2:T(8,128)}) fusion(pred[512,512]{0,1:T(8,128)(4,1)S(1)} %fusion.14, bf16[512,4,128]{0,2,1:T(8,128)(2,1)S(1)} %bitcast.50, bf16[4096,128]{1,0:T(8,128)(2,1)} %all-gather.10.cloned.1.call-done, bf16[512,4096]{1,0:T(8,128)(2,1)} %all-gather.6.cloned.1.call-done, f32[4096]{0:T(1024)S(1)} %copy-done.1, ...), kind=kOutput, calls=%fused_computation.11 | convolution fusion | flops 816904192 | bytes 10250240 | tf_op jit(solution)/shard_map/thgd,shd->hgts/dot_general | solution.py:22
  279.5 3.2 fusion.4
  282.7 71.2 %all-gather.8.cloned.1.call-done = bf16[4096,128]{1,0:T(8,128)(2,1)} async-done(((bf16[64,128]{1,0:T(8,128)(2,1)}), bf16[4096,128]{1,0:T(8,128)(2,1)}) %all-gather.8.cloned.1.call-update) | async-done | bytes 1048592 | tf_op jit(solution)/shard_map/all_gather | solution.py:75
  353.9 6.6 %fusion.8 = bf16[128,4,512]{2,0,1:T(8,128)(2,1)S(1)} fusion(f32[4,512]{1,0:T(4,128)S(1)} %fusion.4, f32[4,512]{1,0:T(4,128)S(1)} %get-tuple-element.7, f32[512,512,4]{1,0,2:T(8,128)} %get-tuple-element.8, pred[512,512]{0,1:T(8,128)(4,1)S(1)} %fusion.14, bf16[4096,128]{1,0:T(8,128)(2,1)} %all-gather.8.cloned.1.call-done, ...), kind=kOutput, calls=%fused_computation.17 | convolution fusion | flops 820314112 | bytes 10258432 | tf_op jit(solution)/shard_map/hgts,shd->thgd/dot_general | solution.py:30
  360.6 80.9 %all-gather.14.cloned.1.call-done = bf16[512,4096]{0,1:T(8,128)(2,1)} async-done(((bf16[512,64]{0,1:T(8,128)(2,1)}), bf16[512,4096]{0,1:T(8,128)(2,1)}) %all-gather.14.cloned.1.call-update) | async-done | bytes 4194320 | tf_op jit(solution)/shard_map/all_gather | solution.py:84
  441.5 6.6 %convolution_convert_fusion = bf16[512,4096]{1,0:T(8,128)(2,1)} fusion(bf16[512,512]{0,1:T(8,128)(2,1)S(1)} %bitcast.49, bf16[512,4096]{0,1:T(8,128)(2,1)} %all-gather.14.cloned.1.call-done), kind=kOutput, calls=%fused_computation.5 | convolution fusion | flops 2149580800 | bytes 8912896 | tf_op jit(solution)/shard_map/dot_general | solution.py:86
  448.0 41.7 %reduce-scatter.2.cloned.1.call-done = bf16[64,4096]{1,0:T(8,128)(2,1)} async-done(((bf16[512,4096]{1,0:T(8,128)(2,1)}), bf16[64,4096]{1,0:T(8,128)(2,1)}) %reduce-scatter.2.cloned.1.call-update) | async-done | bytes 524304 | tf_op jit(solution)/shard_map/reduce_scatter | solution.py:85
  (21 shorter events, 0.7 us)
Async XLA Ops:
  6.5 18.9 %copy-start = (bf16[64,4096]{1,0:T(8,128)(2,1)S(1)}, bf16[64,4096]{1,0:T(8,128)(2,1)}, u32[]{:S(2)}) copy-start(bf16[64,4096]{1,0:T(8,128)(2,1)} %param.8) | copy-start | bytes 1572868
  8.3 27.9 %all-to-all-start = ((s32[64,2,1]{1,2,0:T(1,128)}), s32[64,2,1]{1,2,0:T(1,128)S(1)}, u32[]{:S(2)}, u32[]{:S(2)}) async-start(s32[64,2,1]{1,2,0:T(1,128)} %bitcast), calls=%async_computation | async-start | bytes 65536 | tf_op jit(solution)/shard_map/all_to_all | solution.py:54
  26.0 46.9 %copy-start.2 = (s32[64]{0:T(128)S(1)}, s32[64]{0:T(128)}, u32[]{:S(2)}) copy-start(s32[64]{0:T(128)} %param.10) | copy-start | bytes 772
  36.2 30.4 %all-to-all-start.1 = ((bf16[64,2,4096]{2,1,0:T(2,128)(2,1)}), bf16[64,2,4096]{2,1,0:T(2,128)(2,1)S(1)}, u32[]{:S(2)}, u32[]{:S(2)}) async-start(bf16[64,2,4096]{2,1,0:T(2,128)(2,1)} %all_to_all.16), calls=%async_computation.1 | async-start | bytes 2097152 | tf_op jit(solution)/shard_map/all_to_all | solution.py:53
  40.9 64.1 %all-gather.6.cloned.1.call-start = ((), (), s32[]{:S(2)}) async-start(), calls=%async_computation.3 | async-start | bytes 4718592 | tf_op jit(solution)/shard_map/all_gather | solution.py:61
  42.3 148.6 %copy-start.1 = (f32[4096]{0:T(1024)S(1)}, f32[4096]{0:T(1024)}, u32[]{:S(2)}) copy-start(f32[4096]{0:T(1024)} %param.11) | copy-start | bytes 49156
  68.2 122.7 %all-gather.12.cloned.1.call-start = ((), (), s32[]{:S(2)}) async-start(), calls=%async_computation.6 | async-start | bytes 4259840 | tf_op jit(solution)/shard_map/all_gather | solution.py:67
  68.9 203.2 %all-gather.10.cloned.1.call-start = ((), (), s32[]{:S(2)}) async-start(), calls=%async_computation.5 | async-start | bytes 1064960 | tf_op jit(solution)/shard_map/all_gather | solution.py:71
  69.7 284.3 %all-gather.8.cloned.1.call-start = ((), (), s32[]{:S(2)}) async-start(), calls=%async_computation.4 | async-start | bytes 1064960 | tf_op jit(solution)/shard_map/all_gather | solution.py:75
  70.2 371.2 %all-gather.14.cloned.1.call-start = ((), (), s32[]{:S(2)}) async-start(), calls=%async_computation.7 | async-start | bytes 4259840 | tf_op jit(solution)/shard_map/all_gather | solution.py:84
  70.8 418.9 %reduce-scatter.2.cloned.1.call-start = ((), (), s32[]{:S(2)}) async-start(), calls=%async_computation.8 | async-start | bytes 4718592 | tf_op jit(solution)/shard_map/reduce_scatter | solution.py:85
Sparse Core Ops, SparseCore 0:
  68.3 36.6 all-gather.5
  108.1 82.7 all-gather.11
  194.0 78.1 all-gather.9
  275.1 78.8 all-gather.7
  356.9 84.5 all-gather.13
  448.2 41.5 reduce-scatter.1
where the time goes:
time: 498 us; the launch traced here: 497 us
  waiting for transfers between devices  407 us (82%)
  matrix products  28.2 us (6%)
  starting transfers between devices  22 us (4%)
  between operations  14.3 us (3%)
  blocking collectives  12.1 us (2%)
  other arithmetic  8.27 us (2%)
    all_gather x1, waiting for transfers between devices, on_device(): lax.all_gather(w_query, 'dp', axis=0, tiled=True)  82.8 us
    all_gather x1, waiting for transfers between devices, on_device(): out_full = lax.all_gather(w_out, 'dp', axis=1, tiled=True)  80.9 us
    all_gather x1, waiting for transfers between devices, on_device(): lax.all_gather(w_key, 'dp', axis=0, tiled=True)  75.3 us
    all_gather x1, waiting for transfers between devices, on_device(): lax.all_gather(w_value, 'dp', axis=0, tiled=True)  71.2 us
    reduce_scatter x1, waiting for transfers between devices, on_device(): lax.psum_scatter(jnp.dot(attended, out_full, preferred_element_type=jnp.f...  41.7 us
    all_to_all x1, waiting for transfers between devices, on_device(): lax.all_to_all(outgoing, 'dp', split_axis=0, concat_axis=0, tiled=True)  24.2 us
    all_gather x1, waiting for transfers between devices, on_device(): lax.all_gather(owned, 'tensor', axis=0, tiled=True)  19.5 us
    all_to_all x1, starting transfers between devices, on_device(): lax.all_to_all(landing_marks, 'dp', split_axis=0, concat_axis=0, tiled=True)  17.1 us
  transfers between devices with their start and end apart: 8, of which 8 were waited for; matrix products, arithmetic and copies ran while one was open for 6% of the time, Pallas kernels for 0%

commit v1 on v0

v1 whole, which is shorter than its diff:
```python
import jax
import jax.numpy as jnp
from jax import lax
from jax.sharding import Mesh, PartitionSpec as P

HEAD_DIM = 128
LANES = 128


def rms_rows(states, norm_gain):
    floats = states.astype(jnp.float32)
    mean_square = jnp.mean(floats * floats, axis=-1, keepdims=True)
    return (floats * lax.rsqrt(mean_square + 1e-05) * norm_gain).astype(jnp.bfloat16)


def attend_pack(query, key_rows, value_rows, doc_rows, positions):
    count = query.shape[0]
    group = query.shape[1] // HEAD_DIM
    queries = query.reshape(count, group, HEAD_DIM)
    scores = jnp.einsum("tgd,sd->gts", queries, key_rows, preferred_element_type=jnp.float32)
    scores = scores / jnp.sqrt(jnp.float32(HEAD_DIM))
    allowed = (doc_rows[:, None] == doc_rows[None, :]) & (positions[:, None] >= positions[None, :])
    scores = jnp.where(allowed, scores, jnp.float32(-1e30))
    highest = jnp.max(scores, axis=-1, keepdims=True)
    weights = jnp.where(allowed, jnp.exp(scores - highest), jnp.float32(0.0))
    probs = (weights / jnp.sum(weights, axis=-1, keepdims=True)).astype(jnp.bfloat16)
    mixed = jnp.einsum("gts,sd->tgd", probs, value_rows, preferred_element_type=jnp.float32)
    return mixed.reshape(count, group * HEAD_DIM).astype(jnp.bfloat16)


def shift(array, axis, step, size):
    return lax.ppermute(array, axis, [(i, (i + step) % size) for i in range(size)])


def on_device(tokens, repack_plan, document_ids, norm_gain, w_query, w_key, w_value, w_out):
    dp = ("z", "y")
    row_count, width = tokens.shape
    x_count = lax.axis_size("x")
    peer_count = lax.axis_size("z") * lax.axis_size("y")
    x_index = lax.axis_index("x")
    core_index = lax.axis_index("core")
    pack_rows = row_count * x_count * 2
    projection = w_query.shape[1] + w_key.shape[1] + w_value.shape[1]

    with jax.named_scope("weights"):
        own_weights = jnp.concatenate([w_query, w_key, w_value, w_out.T], axis=1)
        weights = lax.all_gather(own_weights, dp, axis=0, tiled=True)

    with jax.named_scope("dispatch"):
        capacity = 2
        slot_count = peer_count * capacity
        target = repack_plan // pack_rows
        landing = repack_plan % row_count
        positions = jnp.arange(row_count, dtype=jnp.int32)
        same_pack = target[:, None] == target[None, :]
        earlier = positions[None, :] < positions[:, None]
        slot_rank = jnp.sum(jnp.where(same_pack & earlier, 1, 0), axis=1).astype(jnp.int32)
        slot_of = target * capacity + slot_rank
        selector = slot_of[None, :] == jnp.arange(slot_count, dtype=jnp.int32)[:, None]
        marks = jnp.broadcast_to((landing + 1)[:, None], (row_count, LANES)).astype(jnp.bfloat16)
        outgoing = jnp.dot(
            selector.astype(jnp.bfloat16),
            jnp.concatenate([tokens, marks], axis=1),
            preferred_element_type=jnp.float32,
        ).astype(jnp.bfloat16)
        arrived = lax.all_to_all(outgoing, dp, split_axis=0, concat_axis=0, tiled=True)
        arrived_marks = arrived[:, width].astype(jnp.int32)
        settle = arrived_marks[None, :] == positions[:, None] + 1
        owned = jnp.dot(
            settle.astype(jnp.bfloat16), arrived[:, :width], preferred_element_type=jnp.float32
        ).astype(jnp.bfloat16)
        normed_own = rms_rows(owned, norm_gain)

    with jax.named_scope("pack_rows"):
        docs = lax.all_gather(document_ids, ("x", "core"), axis=0, tiled=False)
        rings = [normed_own] + [shift(normed_own, "x", -k, x_count) for k in range(1, x_count)]
        near = jnp.concatenate(rings, axis=0)
        far = shift(near, "core", 1, 2)
        normed = jnp.concatenate([near, far], axis=0)
        ring_of = (x_index + jnp.arange(x_count, dtype=jnp.int32)) % x_count
        block_of = jnp.concatenate([ring_of * 2 + core_index, ring_of * 2 + 1 - core_index])
        doc_rows = docs[block_of].reshape(pack_rows)
        pack_positions = (block_of[:, None] * row_count + positions[None, :]).reshape(pack_rows)

    with jax.named_scope("attention"):
        sums = jnp.dot(normed, weights[:, :projection], preferred_element_type=jnp.float32)
        sums = sums.astype(jnp.bfloat16)
        q_end = w_query.shape[1]
        k_end = q_end + w_key.shape[1]
        attended = attend_pack(
            sums[:, :q_end], sums[:, q_end:k_end], sums[:, k_end:], doc_rows, pack_positions
        )

    with jax.named_scope("output"):
        halves = attended.reshape(2, x_count, row_count, -1)
        ordered = jnp.roll(halves, x_index, axis=1).reshape(2, x_count * row_count, -1)
        out_rows = weights[:, projection:]
        dims = (((1,), (1,)), ((), ()))
        theirs = lax.dot_general(ordered[1], out_rows, dims, preferred_element_type=jnp.float32)
        received = shift(theirs.astype(jnp.bfloat16), "core", 1, 2)
        ours = lax.dot_general(ordered[0], out_rows, dims, preferred_element_type=jnp.float32)
        both = (ours + received.astype(jnp.float32)).astype(jnp.bfloat16)
        return lax.psum_scatter(both, "x", scatter_dimension=0, tiled=True)


def solution(mesh):
    grid = Mesh(mesh.devices.reshape(8, 8, 4, 2), ("z", "y", "x", "core"))
    dp, tensor, rows = ("z", "y"), ("x", "core"), ("z", "y", "x", "core")
    return jax.shard_map(
        on_device,
        mesh=grid,
        in_specs=(
            P(rows, None),
            P(rows),
            P(rows),
            P(),
            P(dp, tensor),
            P(dp, tensor),
            P(dp, tensor),
            P(tensor, dp),
        ),
        out_specs=P(rows, None),
        check_vma=False,
    )
```

time: 498 us -> 207 us (0.42)
  waiting for transfers between devices: 407 us -> 114 us
  starting transfers between devices: 22 us -> 31.7 us
  matrix products: 28.2 us -> 19.1 us
  local copies, waits for them, and re-layouts: 4.92 us -> 13.1 us
  blocking collectives: 12.1 us -> 5.79 us
    all_gather x5 -> x1, waiting for transfers between devices: 330 us -> 24.3 us  [on_device(): weights = lax.all_gather(own_weights, dp, axis=0, tiled=True)]
    ppermute x0 -> x5, waiting for transfers between devices: none -> 26.5 us  [shift(): lax.ppermute(array, axis, [(i, (i + step) % size) for i in range(size)])]
    ppermute x0 -> x5, starting transfers between devices: none -> 14.6 us  [shift(): lax.ppermute(array, axis, [(i, (i + step) % size) for i in range(size)])]
    dot_general x6 -> x7, matrix products: 28.2 us -> 19.1 us  [the longest x1 7.46 us: on_device(): jnp.dot(normed, weights[:, :projection], preferred_element_type=jnp.float32)]
    reduce_scatter x1, waiting for transfers between devices: 41.7 us -> 33 us  [on_device(): return lax.psum_scatter(both, 'x', scatter_dimension=0, tiled=True)]
    reduce_sum x3 -> x0, other arithmetic: 6.42 us -> none  [the longest x1 3.24 us: attend_pack(): jnp.sum(weights, axis=-1, keepdims=True)]
    unnamed x1, blocking collectives: 12.1 us -> 5.79 us
    unnamed x9 -> x12, local copies, waits for them, and re-layouts: 1.61 us -> 6.9 us
  transfers between devices with their start and end apart: 8 -> 8, of which waited for: 8 -> 7; matrix products, arithmetic and copies ran while one was open for 6% -> 8% of each run, Pallas kernels for 0% -> 0%
where the time goes in v1:
time: 207 us; the launch traced here: 206 us
  waiting for transfers between devices  114 us (55%)
  starting transfers between devices  31.7 us (15%)
  matrix products  19.1 us (9%)
  between operations  14.2 us (7%)
  local copies, waits for them, and re-layouts  13.1 us (6%)
  other arithmetic  8 us (4%)
  blocking collectives  5.79 us (3%)
    reduce_scatter x1, waiting for transfers between devices, on_device(): return lax.psum_scatter(both, 'x', scatter_dimension=0, tiled=True)  33 us
    all_to_all x1, waiting for transfers between devices, on_device(): lax.all_to_all(outgoing, dp, split_axis=0, concat_axis=0, tiled=True)  30.6 us
    ppermute x5, waiting for transfers between devices, shift(): lax.ppermute(array, axis, [(i, (i + step) % size) for i in range(size)])  26.5 us
    all_gather x1, waiting for transfers between devices, on_device(): weights = lax.all_gather(own_weights, dp, axis=0, tiled=True)  24.3 us
    all_to_all x1, starting transfers between devices, on_device(): lax.all_to_all(outgoing, dp, split_axis=0, concat_axis=0, tiled=True)  17.1 us
    ppermute x5, starting transfers between devices, shift(): lax.ppermute(array, axis, [(i, (i + step) % size) for i in range(size)])  14.6 us
    dot_general x1, matrix products, on_device(): jnp.dot(normed, weights[:, :projection], preferred_element_type=jnp.float32)  7.46 us
    unnamed x12, local copies, waits for them, and re-layouts  6.9 us
  transfers between devices with their start and end apart: 8, of which 7 were waited for; matrix products, arithmetic and copies ran while one was open for 8% of the time, Pallas kernels for 0%

profile of v1, /device:TPU:1, one launch (start us, length us, event | category | flops | bytes accessed | tf_op | source)
XLA Modules:
  0.0 206.3 jit_solution(16243518511375113926)
XLA Ops:
  6.5 1.6 pad_maximum_fusion.1
  8.1 0.7 and_select_fusion.2
  9.1 1.5 convolution_convert_fusion
  10.6 1.2 all_to_all.8
  11.8 17.1 %all-to-all-start = ((bf16[64,2,4224]{2,1,0:T(2,128)(2,1)}), bf16[64,2,4224]{2,1,0:T(2,128)(2,1)S(1)}, u32[]{:S(2)}, u32[]{:S(2)}) async-start(bf16[64,2,4224]{2,1,0:T(2,128)(2,1)} %all_to_all.8), calls=%async_computation | async-start | bytes 2162688 | tf_op jit(solution)/shard_map/dispatch/all_to_all | solution.py:66
  29.0 30.6 %all-to-all-done = bf16[64,2,4224]{2,1,0:T(2,128)(2,1)S(1)} async-done(((bf16[64,2,4224]{2,1,0:T(2,128)(2,1)}), bf16[64,2,4224]{2,1,0:T(2,128)(2,1)S(1)}, u32[]{:S(2)}, u32[]{:S(2)}) %all-to-all-start) | async-done | bytes 1081376 | tf_op jit(solution)/shard_map/dispatch/all_to_all | solution.py:66
  60.6 1.0 constant_dynamic-update-slice_fusion.4
  61.6 4.5 %collective-permute-start = (bf16[64,4096]{1,0:T(8,128)(2,1)S(1)}, bf16[64,4096]{1,0:T(8,128)(2,1)S(1)}, u32[]{:S(2)}, u32[]{:S(2)}) collective-permute-start(bf16[64,4096]{1,0:T(8,128)(2,1)S(1)} %get-tuple-element.6), channel_id=1, source_target_pairs={{0,6},{2,0},{4,2},{6,4},{1,7},{3,1},{5,3},{7,5},{8,14},{10,8},{12,... | collective-permute-start | bytes 1572872 | tf_op jit(solution)/shard_map/pack_rows/ppermute | solution.py:32
  66.1 2.5 %collective-permute-start.1 = (bf16[64,4096]{1,0:T(8,128)(2,1)S(1)}, bf16[64,4096]{1,0:T(8,128)(2,1)S(1)}, u32[]{:S(2)}, u32[]{:S(2)}) collective-permute-start(bf16[64,4096]{1,0:T(8,128)(2,1)S(1)} %get-tuple-element.6), channel_id=1, source_target_pairs={{0,4},{2,6},{4,0},{6,2},{1,5},{3,7},{5,1},{7,3},{8,12},{10,14},{12... | collective-permute-start | bytes 1572872 | tf_op jit(solution)/shard_map/pack_rows/ppermute | solution.py:32
  68.6 2.4 %collective-permute-start.2 = (bf16[64,4096]{1,0:T(8,128)(2,1)S(1)}, bf16[64,4096]{1,0:T(8,128)(2,1)}, u32[]{:S(2)}, u32[]{:S(2)}) collective-permute-start(bf16[64,4096]{1,0:T(8,128)(2,1)S(1)} %get-tuple-element.6), channel_id=1, source_target_pairs={{0,2},{2,4},{4,6},{6,0},{1,3},{3,5},{5,7},{7,1},{8,10},{10,12},{12... | collective-permute-start | bytes 1572872 | tf_op jit(solution)/shard_map/pack_rows/ppermute | solution.py:32
  71.0 3.5 %collective-permute-done = bf16[64,4096]{1,0:T(8,128)(2,1)S(1)} collective-permute-done((bf16[64,4096]{1,0:T(8,128)(2,1)S(1)}, bf16[64,4096]{1,0:T(8,128)(2,1)S(1)}, u32[]{:S(2)}, u32[]{:S(2)}) %collective-permute-start) | collective-permute-done | bytes 524320 | tf_op jit(solution)/shard_map/pack_rows/ppermute | solution.py:32
  74.6 4.3 %collective-permute-done.1 = bf16[64,4096]{1,0:T(8,128)(2,1)S(1)} collective-permute-done((bf16[64,4096]{1,0:T(8,128)(2,1)S(1)}, bf16[64,4096]{1,0:T(8,128)(2,1)S(1)}, u32[]{:S(2)}, u32[]{:S(2)}) %collective-permute-start.1) | collective-permute-done | bytes 524320 | tf_op jit(solution)/shard_map/pack_rows/ppermute | solution.py:32
  78.9 0.8 copy-done
  79.7 14.9 %collective-permute-done.2 = bf16[64,4096]{1,0:T(8,128)(2,1)} collective-permute-done((bf16[64,4096]{1,0:T(8,128)(2,1)S(1)}, bf16[64,4096]{1,0:T(8,128)(2,1)}, u32[]{:S(2)}, u32[]{:S(2)}) %collective-permute-start.2) | collective-permute-done | bytes 524320 | tf_op jit(solution)/shard_map/pack_rows/ppermute | solution.py:32
  94.6 1.4 pad_maximum_fusion
  95.9 2.6 %collective-permute-start.3 = (bf16[256,4096]{1,0:T(8,128)(2,1)S(1)}, bf16[256,4096]{1,0:T(8,128)(2,1)}, u32[]{:S(2)}, u32[]{:S(2)}) collective-permute-start(bf16[256,4096]{1,0:T(8,128)(2,1)S(1)} %pad_maximum_fusion), channel_id=1, source_target_pairs={{0,1},{1,0},{2,3},{3,2},{4,5},{5,4},{6,7},{7,6},{8,9},{9,8},{10,11... | collective-permute-start | bytes 6291464 | tf_op jit(solution)/shard_map/pack_rows/ppermute | solution.py:32
  98.6 1.3 dynamic-slice
  100.8 5.8 %all-reduce = s32[512]{0:T(512)S(1)} all-reduce(s32[512]{0:T(512)S(1)} %dynamic-update-slice), channel_id=2, replica_groups=mesh['z'=8,'y'=8,'x'=4,'core'=2] {'x','core'}, use_global_device_ids=true, to_apply=%add | all-reduce | flops 512 | bytes 4096
  106.6 0.6 gather_fusion
  107.8 0.8 constant_dynamic-update-slice_fusion.3
  108.6 1.9 constant_dynamic-update-slice_fusion.2
  110.5 1.9 constant_dynamic-update-slice_fusion.1
  112.4 3.1 %constant_dynamic-update-slice_fusion = bf16[512,4096]{1,0:T(8,128)(2,1)} fusion(bf16[512,4096]{1,0:T(8,128)(2,1)} %constant_dynamic-update-slice_fusion.1, bf16[256,4096]{1,0:T(8,128)(2,1)} %collective-permute-done.3), kind=kLoop, calls=%fused_computation.50 | loop fusion | bytes 4194304 | tf_op jit(solution)/shard_map/pack_rows/concatenate | solution.py:79
  115.5 24.3 %all-gather.3.cloned.1.call-done = bf16[4096,1280]{1,0:T(8,128)(2,1)} async-done(((bf16[64,1280]{1,0:T(8,128)(2,1)}), bf16[4096,1280]{1,0:T(8,128)(2,1)}) %all-gather.3.cloned.1.call-update) | async-done | bytes 10485776 | tf_op jit(solution)/shard_map/weights/all_gather | solution.py:47
  139.8 7.5 %fusion.14 = bf16[512,768]{1,0:T(8,128)(2,1)S(1)} fusion(bf16[512,4096]{1,0:T(8,128)(2,1)} %constant_dynamic-update-slice_fusion, bf16[4096,1280]{1,0:T(8,128)(2,1)} %all-gather.3.cloned.1.call-done), kind=kOutput, calls=%fused_computation.21 | convolution fusion | flops 3221618688 | bytes 11272192 | tf_op jit(solution)/shard_map/attention/dot_general | solution.py:86
  147.3 0.7 fusion.24
  148.0 2.4 %fusion.41 = (f32[4,512]{1,0:T(4,128)S(1)}, f32[4,512,512]{1,2,0:T(8,128)S(1)}) fusion(f32[512,512,4]{1,0,2:T(8,128)S(1)} %fusion.24, pred[512,512]{0,1:T(8,128)(4,1)S(1)} %compare_and_fusion), kind=kOutput, calls=%fused_computation.82 | output fusion | flops 7340543 | bytes 8658944 | tf_op jit(solution)/shard_map/attention/sub | solution.py:25
  151.6 3.6 %convolution_convert_fusion.1 = bf16[256,4096]{1,0:T(8,128)(2,1)S(1)} fusion(bf16[256,512]{1,0:T(8,128)(2,1)S(1)} %bitcast.38, bf16[4096,1280]{1,0:T(8,128)(2,1)} %all-gather.3.cloned.1.call-done), kind=kOutput, calls=%fused_computation.5 | convolution fusion | flops 1074790400 | bytes 6553600 | tf_op jit(solution)/shard_map/output/dot_general | solution.py:99
  155.2 2.6 %collective-permute-start.4 = (bf16[256,4096]{1,0:T(8,128)(2,1)S(1)}, bf16[256,4096]{1,0:T(8,128)(2,1)S(1)}, u32[]{:S(2)}, u32[]{:S(2)}) collective-permute-start(bf16[256,4096]{1,0:T(8,128)(2,1)S(1)} %convolution_convert_fusion.1), channel_id=1, source_target_pairs={{0,1},{1,0},{2,3},{3,2},{4,5},{5,4},{6,7},{7,6},{8,9},{9,8},{10,11... | collective-permute-start | bytes 6291464 | tf_op jit(solution)/shard_map/output/ppermute | solution.py:32
  157.8 3.8 %collective-permute-done.4 = bf16[256,4096]{1,0:T(8,128)(2,1)S(1)} collective-permute-done((bf16[256,4096]{1,0:T(8,128)(2,1)S(1)}, bf16[256,4096]{1,0:T(8,128)(2,1)S(1)}, u32[]{:S(2)}, u32[]{:S(2)}) %collective-permute-start.4) | collective-permute-done | bytes 2097184 | tf_op jit(solution)/shard_map/output/ppermute | solution.py:32
  161.5 4.9 %add_convert_fusion = bf16[256,4096]{1,0:T(8,128)(2,1)} fusion(bf16[256,4096]{1,0:T(8,128)(2,1)S(1)} %collective-permute-done.4, bf16[256,512]{1,0:T(8,128)(2,1)S(1)} %bitcast.37, bf16[4096,1280]{1,0:T(8,128)(2,1)} %all-gather.3.cloned.1.call-done), kind=kOutput, calls=%fused_computation.9 | convolution fusion | flops 1076887552 | bytes 8650752 | tf_op jit(solution)/shard_map/output/dot_general | solution.py:101
  166.5 33.0 %reduce-scatter.2.cloned.1.call-done = bf16[64,4096]{1,0:T(8,128)(2,1)} async-done(((bf16[256,4096]{1,0:T(8,128)(2,1)}), bf16[64,4096]{1,0:T(8,128)(2,1)}) %reduce-scatter.2.cloned.1.call-update) | async-done | bytes 524304 | tf_op jit(solution)/shard_map/output/reduce_scatter | solution.py:103
  (34 shorter events, 3.6 us)
Async XLA Ops:
  6.5 133.2 %all-gather.3.cloned.1.call-start = ((), (), s32[]{:S(2)}) async-start(), calls=%async_computation.2 | async-start | bytes 10649600 | tf_op jit(solution)/shard_map/weights/all_gather | solution.py:47
  10.5 50.1 %copy-start.1 = (f32[4096]{0:T(1024)S(1)}, f32[4096]{0:T(1024)}, u32[]{:S(2)}) copy-start(f32[4096]{0:T(1024)} %param.11) | copy-start | bytes 49156
  11.8 47.8 %all-to-all-start = ((bf16[64,2,4224]{2,1,0:T(2,128)(2,1)}), bf16[64,2,4224]{2,1,0:T(2,128)(2,1)S(1)}, u32[]{:S(2)}, u32[]{:S(2)}) async-start(bf16[64,2,4224]{2,1,0:T(2,128)(2,1)} %all_to_all.8), calls=%async_computation | async-start | bytes 2162688 | tf_op jit(solution)/shard_map/dispatch/all_to_all | solution.py:66
  28.9 170.6 %reduce-scatter.2.cloned.1.call-start = ((), (), s32[]{:S(2)}) async-start(), calls=%async_computation.3 | async-start | bytes 2621440 | tf_op jit(solution)/shard_map/output/reduce_scatter | solution.py:103
  60.1 40.4 %copy-start.2 = (s32[64]{0:T(128)S(1)}, s32[64]{0:T(128)}, u32[]{:S(2)}) copy-start(s32[64]{0:T(128)} %param.10) | copy-start | bytes 772
  61.6 13.0 %collective-permute-start = (bf16[64,4096]{1,0:T(8,128)(2,1)S(1)}, bf16[64,4096]{1,0:T(8,128)(2,1)S(1)}, u32[]{:S(2)}, u32[]{:S(2)}) collective-permute-start(bf16[64,4096]{1,0:T(8,128)(2,1)S(1)} %get-tuple-element.6), channel_id=1, source_target_pairs={{0,6},{2,0},{4,2},{6,4},{1,7},{3,1},{5,3},{7,5},{8,14},{10,8},{12,... | collective-permute-start | bytes 1572872 | tf_op jit(solution)/shard_map/pack_rows/ppermute | solution.py:32
  66.1 12.8 %collective-permute-start.1 = (bf16[64,4096]{1,0:T(8,128)(2,1)S(1)}, bf16[64,4096]{1,0:T(8,128)(2,1)S(1)}, u32[]{:S(2)}, u32[]{:S(2)}) collective-permute-start(bf16[64,4096]{1,0:T(8,128)(2,1)S(1)} %get-tuple-element.6), channel_id=1, source_target_pairs={{0,4},{2,6},{4,0},{6,2},{1,5},{3,7},{5,1},{7,3},{8,12},{10,14},{12... | collective-permute-start | bytes 1572872 | tf_op jit(solution)/shard_map/pack_rows/ppermute | solution.py:32
  68.6 26.0 %collective-permute-start.2 = (bf16[64,4096]{1,0:T(8,128)(2,1)S(1)}, bf16[64,4096]{1,0:T(8,128)(2,1)}, u32[]{:S(2)}, u32[]{:S(2)}) collective-permute-start(bf16[64,4096]{1,0:T(8,128)(2,1)S(1)} %get-tuple-element.6), channel_id=1, source_target_pairs={{0,2},{2,4},{4,6},{6,0},{1,3},{3,5},{5,7},{7,1},{8,10},{10,12},{12... | collective-permute-start | bytes 1572872 | tf_op jit(solution)/shard_map/pack_rows/ppermute | solution.py:32
  78.9 0.8 copy-start
  95.9 16.4 %collective-permute-start.3 = (bf16[256,4096]{1,0:T(8,128)(2,1)S(1)}, bf16[256,4096]{1,0:T(8,128)(2,1)}, u32[]{:S(2)}, u32[]{:S(2)}) collective-permute-start(bf16[256,4096]{1,0:T(8,128)(2,1)S(1)} %pad_maximum_fusion), channel_id=1, source_target_pairs={{0,1},{1,0},{2,3},{3,2},{4,5},{5,4},{6,7},{7,6},{8,9},{9,8},{10,11... | collective-permute-start | bytes 6291464 | tf_op jit(solution)/shard_map/pack_rows/ppermute | solution.py:32
  155.2 6.4 %collective-permute-start.4 = (bf16[256,4096]{1,0:T(8,128)(2,1)S(1)}, bf16[256,4096]{1,0:T(8,128)(2,1)S(1)}, u32[]{:S(2)}, u32[]{:S(2)}) collective-permute-start(bf16[256,4096]{1,0:T(8,128)(2,1)S(1)} %convolution_convert_fusion.1), channel_id=1, source_target_pairs={{0,1},{1,0},{2,3},{3,2},{4,5},{5,4},{6,7},{7,6},{8,9},{9,8},{10,11... | collective-permute-start | bytes 6291464 | tf_op jit(solution)/shard_map/output/ppermute | solution.py:32
Sparse Core Ops, SparseCore 0:
  10.4 129.3 all-gather.2
  166.6 32.8 reduce-scatter.1

commit v2 on v1

--- a/solution.py
+++ b/solution.py
@@ -37,7 +37,6 @@
     row_count, width = tokens.shape
     x_count = lax.axis_size("x")
     peer_count = lax.axis_size("z") * lax.axis_size("y")
-    x_index = lax.axis_index("x")
     core_index = lax.axis_index("core")
     pack_rows = row_count * x_count * 2
     projection = w_query.shape[1] + w_key.shape[1] + w_value.shape[1]
@@ -73,12 +72,13 @@
 
     with jax.named_scope("pack_rows"):
         docs = lax.all_gather(document_ids, ("x", "core"), axis=0, tiled=False)
-        rings = [normed_own] + [shift(normed_own, "x", -k, x_count) for k in range(1, x_count)]
-        near = jnp.concatenate(rings, axis=0)
+        copies = jnp.broadcast_to(normed_own[None], (x_count,) + normed_own.shape)
+        near = lax.all_to_all(copies, "x", split_axis=0, concat_axis=0, tiled=True)
+        near = near.reshape(x_count * row_count, width)
         far = shift(near, "core", 1, 2)
         normed = jnp.concatenate([near, far], axis=0)
-        ring_of = (x_index + jnp.arange(x_count, dtype=jnp.int32)) % x_count
-        block_of = jnp.concatenate([ring_of * 2 + core_index, ring_of * 2 + 1 - core_index])
+        even = 2 * jnp.arange(x_count, dtype=jnp.int32)
+        block_of = jnp.concatenate([even + core_index, even + 1 - core_index])
         doc_rows = docs[block_of].reshape(pack_rows)
         pack_positions = (block_of[:, None] * row_count + positions[None, :]).reshape(pack_rows)
 
@@ -92,15 +92,17 @@
         )
 
     with jax.named_scope("output"):
-        halves = attended.reshape(2, x_count, row_count, -1)
-        ordered = jnp.roll(halves, x_index, axis=1).reshape(2, x_count * row_count, -1)
+        half = x_count * row_count
         out_rows = weights[:, projection:]
         dims = (((1,), (1,)), ((), ()))
-        theirs = lax.dot_general(ordered[1], out_rows, dims, preferred_element_type=jnp.float32)
+        theirs = lax.dot_general(attended[half:], out_rows, dims, preferred_element_type=jnp.float32)
         received = shift(theirs.astype(jnp.bfloat16), "core", 1, 2)
-        ours = lax.dot_general(ordered[0], out_rows, dims, preferred_element_type=jnp.float32)
-        both = (ours + received.astype(jnp.float32)).astype(jnp.bfloat16)
-        return lax.psum_scatter(both, "x", scatter_dimension=0, tiled=True)
+        ours = lax.dot_general(attended[:half], out_rows, dims, preferred_element_type=jnp.float32)
+        ours = lax.optimization_barrier(ours.astype(jnp.bfloat16))
+        both = (ours.astype(jnp.float32) + received.astype(jnp.float32)).astype(jnp.bfloat16)
+        parts = lax.all_to_all(both, "x", split_axis=0, concat_axis=0, tiled=True)
+        parts = parts.reshape(x_count, row_count, -1).astype(jnp.float32)
+        return jnp.sum(parts, axis=0).astype(jnp.bfloat16)
 
 
 def solution(mesh):

time: 207 us -> 198 us (0.957)
  blocking collectives: 5.79 us -> 61.4 us
  waiting for transfers between devices: 114 us -> 68.9 us
  local copies, waits for them, and re-layouts: 13.1 us -> 5.77 us
  matrix products: 19.1 us -> 12.6 us
  starting transfers between devices: 31.7 us -> 27 us
    all_to_all x0 -> x2, blocking collectives: none -> 55.1 us  [the longest x1 29.2 us: on_device(): parts = lax.all_to_all(both, 'x', split_axis=0, concat_axis=0, tiled=True)]
    reduce_scatter x1 -> x0, waiting for transfers between devices: 33 us -> none  [on_device(): return lax.psum_scatter(both, 'x', scatter_dimension=0, tiled=True)]
    ppermute x5 -> x2, waiting for transfers between devices: 26.5 us -> 2.45 us  [shift(): lax.ppermute(array, axis, [(i, (i + step) % size) for i in range(size)])]
    all_gather x1, waiting for transfers between devices: 24.3 us -> 35.7 us  [on_device(): weights = lax.all_gather(own_weights, dp, axis=0, tiled=True)]
    dot_general x2, matrix products: 8.5 us -> 2.61 us  [the longest x1 1.31 us: on_device(): lax.dot_general(attended[half:], out_rows, dims, preferred_element_type=j...]
    ppermute x5 -> x2, starting transfers between devices: 14.6 us -> 9.83 us  [shift(): lax.ppermute(array, axis, [(i, (i + step) % size) for i in range(size)])]
    unnamed x12 -> x13, local copies, waits for them, and re-layouts: 6.9 us -> 2.95 us
    concatenate x1 -> x0, local copies, waits for them, and re-layouts: 3.15 us -> none  [on_device(): normed = jnp.concatenate([near, far], axis=0)]
  transfers between devices with their start and end apart: 8 -> 4, of which waited for: 7 -> 3; matrix products, arithmetic and copies ran while one was open for 8% -> 4% of each run, Pallas kernels for 0% -> 0%
where the time goes in v2:
time: 198 us
  waiting for transfers between devices  68.9 us (35%)
  blocking collectives  61.4 us (31%)
  starting transfers between devices  27 us (14%)
  between operations  14.3 us (7%)
  matrix products  12.6 us (6%)
  other arithmetic  7.79 us (4%)
  local copies, waits for them, and re-layouts  5.77 us (3%)
    all_gather x1, waiting for transfers between devices, on_device(): weights = lax.all_gather(own_weights, dp, axis=0, tiled=True)  35.7 us
    all_to_all x1, waiting for transfers between devices, on_device(): lax.all_to_all(outgoing, dp, split_axis=0, concat_axis=0, tiled=True)  30.7 us
    all_to_all x1, blocking collectives, on_device(): parts = lax.all_to_all(both, 'x', split_axis=0, concat_axis=0, tiled=True)  29.2 us
    all_to_all x1, blocking collectives, on_device(): near = lax.all_to_all(copies, 'x', split_axis=0, concat_axis=0, tiled=True)  25.9 us
    all_to_all x1, starting transfers between devices, on_device(): lax.all_to_all(outgoing, dp, split_axis=0, concat_axis=0, tiled=True)  17.1 us
    ppermute x2, starting transfers between devices, shift(): lax.ppermute(array, axis, [(i, (i + step) % size) for i in range(size)])  9.83 us
    dot_general x1, matrix products, on_device(): jnp.dot(normed, weights[:, :projection], preferred_element_type=jnp.float32)  6.82 us
    unnamed x1, blocking collectives  6.35 us
  transfers between devices with their start and end apart: 4, of which 3 were waited for; matrix products, arithmetic and copies ran while one was open for 4% of the time, Pallas kernels for 0%

profile of v2, /device:TPU:1, one launch (start us, length us, event | category | flops | bytes accessed | tf_op | source)
XLA Modules:
  0.0 197.7 jit_solution(18006663716016221230)
XLA Ops:
  6.5 1.6 pad_maximum_fusion
  8.1 0.7 and_select_fusion.1
  8.8 0.2 select_reduce_fusion
  9.1 1.5 convolution_convert_fusion
  10.6 1.3 all_to_all.17
  11.8 17.1 %all-to-all-start = ((bf16[64,2,4224]{2,1,0:T(2,128)(2,1)}), bf16[64,2,4224]{2,1,0:T(2,128)(2,1)S(1)}, u32[]{:S(2)}, u32[]{:S(2)}) async-start(bf16[64,2,4224]{2,1,0:T(2,128)(2,1)} %all_to_all.17), calls=%async_computation | async-start | bytes 2162688 | tf_op jit(solution)/shard_map/dispatch/all_to_all | solution.py:65
  29.0 30.7 %all-to-all-done = bf16[64,2,4224]{2,1,0:T(2,128)(2,1)S(1)} async-done(((bf16[64,2,4224]{2,1,0:T(2,128)(2,1)}), bf16[64,2,4224]{2,1,0:T(2,128)(2,1)S(1)}, u32[]{:S(2)}, u32[]{:S(2)}) %all-to-all-start) | async-done | bytes 1081376 | tf_op jit(solution)/shard_map/dispatch/all_to_all | solution.py:65
  59.6 0.4 all_to_all.19
  60.2 0.5 multiply_reduce_fusion
  60.7 0.2 multiply_convert_fusion
  60.8 0.2 broadcast_in_dim.25
  61.1 25.9 %all_to_all.26 = bf16[4,64,4096]{2,1,0:T(8,128)(2,1)S(1)} all-to-all(bf16[4,64,4096]{2,1,0:T(8,128)(2,1)S(1)} %broadcast_in_dim.25), channel_id=1, replica_groups=mesh['z'=8,'y'=8,'x'=4,'core'=2] {'x'}, dimensions={0} | all-to-all | bytes 4194304 | tf_op jit(solution)/shard_map/pack_rows/all_to_all | solution.py:76
  87.0 7.2 %collective-permute-start = (bf16[256,4096]{1,0:T(8,128)(2,1)S(1)}, bf16[256,4096]{1,0:T(8,128)(2,1)}, u32[]{:S(2)}, u32[]{:S(2)}) collective-permute-start(bf16[256,4096]{1,0:T(8,128)(2,1)S(1)} %bitcast.41), channel_id=1, source_target_pairs={{0,1},{1,0},{2,3},{3,2},{4,5},{5,4},{6,7},{7,6},{8,9},{9,8},{10,11... | collective-permute-start | bytes 6291464 | tf_op jit(solution)/shard_map/pack_rows/ppermute | solution.py:32
  94.2 1.3 dynamic-slice
  96.3 0.2 dynamic-update-slice
  96.5 6.3 %all-reduce = s32[512]{0:T(512)S(1)} all-reduce(s32[512]{0:T(512)S(1)} %dynamic-update-slice), channel_id=2, replica_groups=mesh['z'=8,'y'=8,'x'=4,'core'=2] {'x','core'}, use_global_device_ids=true, to_apply=%add | all-reduce | flops 512 | bytes 4096
  103.0 0.6 gather_fusion
  103.9 0.3 compare_and_fusion
  104.2 35.7 %all-gather.3.cloned.1.call-done = bf16[4096,1280]{1,0:T(8,128)(2,1)} async-done(((bf16[64,1280]{1,0:T(8,128)(2,1)}), bf16[4096,1280]{1,0:T(8,128)(2,1)}) %all-gather.3.cloned.1.call-update) | async-done | bytes 10485776 | tf_op jit(solution)/shard_map/weights/all_gather | solution.py:46
  139.9 6.8 %fusion.14 = bf16[512,768]{1,0:T(8,128)(2,1)S(1)} fusion(bf16[4096,1280]{1,0:T(8,128)(2,1)} %all-gather.3.cloned.1.call-done, bf16[256,4096]{1,0:T(8,128)(2,1)} %collective-permute-done, bf16[256,4096]{1,0:T(8,128)(2,1)S(1)} %bitcast.42), kind=kOutput, calls=%fused_computation.23 | convolution fusion | flops 3230007296 | bytes 11272192 | tf_op jit(solution)/shard_map/attention/dot_general | solution.py:86
  146.8 0.7 fusion.25
  147.5 2.4 %fusion.44 = (f32[4,512]{1,0:T(4,128)S(1)}, f32[4,512,512]{1,2,0:T(8,128)S(1)}) fusion(f32[512,512,4]{1,0,2:T(8,128)S(1)} %fusion.25, pred[512,512]{0,1:T(8,128)(4,1)S(1)} %compare_and_fusion), kind=kOutput, calls=%fused_computation.75 | output fusion | flops 7340543 | bytes 8658944 | tf_op jit(solution)/shard_map/attention/sub | solution.py:25
  149.9 0.5 fusion.20
  150.4 0.5 slice-done.1
  150.9 0.8 slice-done.2
  151.8 1.3 convolution_convert_fusion.1
  153.1 2.6 %collective-permute-start.1 = (bf16[256,4096]{1,0:T(8,128)(2,1)S(1)}, bf16[256,4096]{1,0:T(8,128)(2,1)S(1)}, u32[]{:S(2)}, u32[]{:S(2)}) collective-permute-start(bf16[256,4096]{1,0:T(8,128)(2,1)S(1)} %convolution_convert_fusion.1), channel_id=1, source_target_pairs={{0,1},{1,0},{2,3},{3,2},{4,5},{5,4},{6,7},{7,6},{8,9},{9,8},{10,11... | collective-permute-start | bytes 6291464 | tf_op jit(solution)/shard_map/output/ppermute | solution.py:32
  155.7 1.3 convolution_convert_fusion.2
  157.0 2.5 %collective-permute-done.1 = bf16[256,4096]{1,0:T(8,128)(2,1)S(1)} collective-permute-done((bf16[256,4096]{1,0:T(8,128)(2,1)S(1)}, bf16[256,4096]{1,0:T(8,128)(2,1)S(1)}, u32[]{:S(2)}, u32[]{:S(2)}) %collective-permute-start.1) | collective-permute-done | bytes 2097184 | tf_op jit(solution)/shard_map/output/ppermute | solution.py:32
  159.4 0.9 add_convert_fusion
  160.4 29.2 %all_to_all.27 = bf16[4,64,4096]{2,1,0:T(8,128)(2,1)S(1)} all-to-all(bf16[4,64,4096]{2,1,0:T(8,128)(2,1)S(1)} %bitcast.40), channel_id=1, replica_groups=mesh['z'=8,'y'=8,'x'=4,'core'=2] {'x'}, dimensions={0} | all-to-all | bytes 4194304 | tf_op jit(solution)/shard_map/output/all_to_all | solution.py:103
  189.6 1.3 reduce_sum.42
  (28 shorter events, 0.8 us)
Async XLA Ops:
  6.5 133.4 %all-gather.3.cloned.1.call-start = ((), (), s32[]{:S(2)}) async-start(), calls=%async_computation.3 | async-start | bytes 10649600 | tf_op jit(solution)/shard_map/weights/all_gather | solution.py:46
  10.6 50.1 %copy-start = (f32[4096]{0:T(1024)S(1)}, f32[4096]{0:T(1024)}, u32[]{:S(2)}) copy-start(f32[4096]{0:T(1024)} %param.11) | copy-start | bytes 49156
  11.8 47.8 %all-to-all-start = ((bf16[64,2,4224]{2,1,0:T(2,128)(2,1)}), bf16[64,2,4224]{2,1,0:T(2,128)(2,1)S(1)}, u32[]{:S(2)}, u32[]{:S(2)}) async-start(bf16[64,2,4224]{2,1,0:T(2,128)(2,1)} %all_to_all.17), calls=%async_computation | async-start | bytes 2162688 | tf_op jit(solution)/shard_map/dispatch/all_to_all | solution.py:65
  60.7 35.6 %copy-start.1 = (s32[64]{0:T(128)S(1)}, s32[64]{0:T(128)}, u32[]{:S(2)}) copy-start(s32[64]{0:T(128)} %param.10) | copy-start | bytes 772
  87.0 17.2 %collective-permute-start = (bf16[256,4096]{1,0:T(8,128)(2,1)S(1)}, bf16[256,4096]{1,0:T(8,128)(2,1)}, u32[]{:S(2)}, u32[]{:S(2)}) collective-permute-start(bf16[256,4096]{1,0:T(8,128)(2,1)S(1)} %bitcast.41), channel_id=1, source_target_pairs={{0,1},{1,0},{2,3},{3,2},{4,5},{5,4},{6,7},{7,6},{8,9},{9,8},{10,11... | collective-permute-start | bytes 6291464 | tf_op jit(solution)/shard_map/pack_rows/ppermute | solution.py:32
  147.5 2.9 %slice-start = ((s8[10485760]{0:T(1024)(128)(4,1)}), s8[4194304]{0:T(1024)(128)(4,1)S(1)}, s32[]{:S(2)}) async-start(s8[10485760]{0:T(1024)(128)(4,1)} %bitcast.46), calls=%async_computation.4 | async-start | bytes 8388608
  147.5 3.5 %slice-start.1 = ((s8[10485760]{0:T(1024)(128)(4,1)}), s8[4194304]{0:T(1024)(128)(4,1)S(1)}, s32[]{:S(2)}) async-start(s8[10485760]{0:T(1024)(128)(4,1)} %bitcast.46), calls=%async_computation.5 | async-start | bytes 8388608
  149.9 1.9 slice-start.2
  153.1 6.4 %collective-permute-start.1 = (bf16[256,4096]{1,0:T(8,128)(2,1)S(1)}, bf16[256,4096]{1,0:T(8,128)(2,1)S(1)}, u32[]{:S(2)}, u32[]{:S(2)}) collective-permute-start(bf16[256,4096]{1,0:T(8,128)(2,1)S(1)} %convolution_convert_fusion.1), channel_id=1, source_target_pairs={{0,1},{1,0},{2,3},{3,2},{4,5},{5,4},{6,7},{7,6},{8,9},{9,8},{10,11... | collective-permute-start | bytes 6291464 | tf_op jit(solution)/shard_map/output/ppermute | solution.py:32
Sparse Core Ops, SparseCore 0:
  10.4 129.5 all-gather.2

commit v3 on v2

--- a/solution.py
+++ b/solution.py
@@ -1,10 +1,16 @@
+import math
+
 import jax
 import jax.numpy as jnp
 from jax import lax
+from jax.experimental import pallas as pl
+from jax.experimental.pallas import tpu as pltpu
 from jax.sharding import Mesh, PartitionSpec as P
 
 HEAD_DIM = 128
 LANES = 128
+CHUNK = 512
+VMEM_BYTES = 32 * 1024 * 1024
 
 
 def rms_rows(states, norm_gain):
@@ -13,19 +19,90 @@
     return (floats * lax.rsqrt(mean_square + 1e-05) * norm_gain).astype(jnp.bfloat16)
 
 
-def attend_pack(query, key_rows, value_rows, doc_rows, positions):
-    count = query.shape[0]
-    group = query.shape[1] // HEAD_DIM
-    queries = query.reshape(count, group, HEAD_DIM)
-    scores = jnp.einsum("tgd,sd->gts", queries, key_rows, preferred_element_type=jnp.float32)
-    scores = scores / jnp.sqrt(jnp.float32(HEAD_DIM))
-    allowed = (doc_rows[:, None] == doc_rows[None, :]) & (positions[:, None] >= positions[None, :])
-    scores = jnp.where(allowed, scores, jnp.float32(-1e30))
-    highest = jnp.max(scores, axis=-1, keepdims=True)
-    weights = jnp.where(allowed, jnp.exp(scores - highest), jnp.float32(0.0))
-    probs = (weights / jnp.sum(weights, axis=-1, keepdims=True)).astype(jnp.bfloat16)
-    mixed = jnp.einsum("gts,sd->tgd", probs, value_rows, preferred_element_type=jnp.float32)
-    return mixed.reshape(count, group * HEAD_DIM).astype(jnp.bfloat16)
+def attention_kernel(
+    near,
+    far,
+    weights,
+    doc_column,
+    doc_row,
+    place_column,
+    place_row,
+    attended,
+    total,
+    held,
+    loaded,
+    arrivals,
+):
+    half, width = near.shape
+    projection = loaded.shape[1]
+    group = attended.shape[1] // HEAD_DIM
+    halves = [slice(0, half), slice(half, 2 * half)]
+    chunks = [slice(start, start + CHUNK) for start in range(0, width, CHUNK)]
+    copies = [
+        pltpu.make_async_copy(
+            weights.at[pl.ds(chunk.start, CHUNK), pl.ds(0, projection)],
+            loaded.at[pl.ds(chunk.start, CHUNK), :],
+            arrivals.at[index],
+        )
+        for index, chunk in enumerate(chunks)
+    ]
+    for copy in copies:
+        copy.start()
+    for copy, chunk in zip(copies, chunks):
+        copy.wait()
+        for here, rows in zip(halves, (near, far)):
+            term = jnp.dot(
+                rows[:, chunk], loaded[chunk, :], preferred_element_type=jnp.float32
+            )
+            if chunk.start == 0:
+                total[here, :] = term
+            elif chunk.stop < width:
+                total[here, :] += term
+            else:
+                held[here, :] = (total[here, :] + term).astype(jnp.bfloat16)
+    key_at = group * HEAD_DIM
+    keys = held[:, key_at : key_at + HEAD_DIM]
+    values = held[:, key_at + HEAD_DIM : key_at + 2 * HEAD_DIM]
+    scale = HEAD_DIM**-0.5 * math.log2(math.e)
+    for here in halves:
+        same = doc_column[here, :] == doc_row[...]
+        allowed = same & (place_column[here, :] >= place_row[...])
+        hidden = jnp.where(allowed, 0.0, -1e30)
+        for head in range(group):
+            lanes = slice(head * HEAD_DIM, (head + 1) * HEAD_DIM)
+            scores = lax.dot_general(
+                held[here, lanes], keys, (((1,), (1,)), ((), ())), preferred_element_type=jnp.float32
+            )
+            scores = scores * scale + hidden
+            weight = jnp.exp2(scores - jnp.max(scores, axis=1, keepdims=True))
+            share = 1.0 / jnp.sum(weight, axis=1, keepdims=True)
+            mixed = jnp.dot(weight.astype(jnp.bfloat16), values, preferred_element_type=jnp.float32)
+            attended[here, lanes] = (mixed * share).astype(jnp.bfloat16)
+
+
+def attention(near, far, weights, docs, places, projection, head_columns):
+    half, width = near.shape
+    rows = 2 * half
+    here = pl.BlockSpec(memory_space=pltpu.VMEM)
+    return pl.pallas_call(
+        attention_kernel,
+        out_shape=jax.ShapeDtypeStruct((rows, head_columns), jnp.bfloat16),
+        in_specs=[here, here, pl.BlockSpec(memory_space=pl.ANY), here, here, here, here],
+        out_specs=here,
+        scratch_shapes=[
+            pltpu.VMEM((rows, projection), jnp.float32),
+            pltpu.VMEM((rows, projection), jnp.bfloat16),
+            pltpu.VMEM((width, projection), jnp.bfloat16),
+            pltpu.SemaphoreType.DMA((width // CHUNK,)),
+        ],
+        compiler_params=pltpu.CompilerParams(vmem_limit_bytes=VMEM_BYTES),
+        cost_estimate=pl.CostEstimate(
+            flops=2 * rows * width * projection + 4 * rows * rows * head_columns,
+            bytes_accessed=2 * width * (rows + projection) + 2 * rows * head_columns,
+            transcendentals=rows * rows * head_columns // HEAD_DIM,
+        ),
+        name="attention",
+    )(near, far, weights, docs[:, None], docs[None, :], places[:, None], places[None, :])
 
 
 def shift(array, axis, step, size):
@@ -76,19 +153,14 @@
         near = lax.all_to_all(copies, "x", split_axis=0, concat_axis=0, tiled=True)
         near = near.reshape(x_count * row_count, width)
         far = shift(near, "core", 1, 2)
-        normed = jnp.concatenate([near, far], axis=0)
         even = 2 * jnp.arange(x_count, dtype=jnp.int32)
         block_of = jnp.concatenate([even + core_index, even + 1 - core_index])
         doc_rows = docs[block_of].reshape(pack_rows)
         pack_positions = (block_of[:, None] * row_count + positions[None, :]).reshape(pack_rows)
 
     with jax.named_scope("attention"):
-        sums = jnp.dot(normed, weights[:, :projection], preferred_element_type=jnp.float32)
-        sums = sums.astype(jnp.bfloat16)
-        q_end = w_query.shape[1]
-        k_end = q_end + w_key.shape[1]
-        attended = attend_pack(
-            sums[:, :q_end], sums[:, q_end:k_end], sums[:, k_end:], doc_rows, pack_positions
+        attended = attention(
+            near, far, weights, doc_rows, pack_positions, projection, w_query.shape[1]
         )
 
     with jax.named_scope("output"):

time: 198 us -> 199 us (level)
  Pallas kernels: 0 us -> 8.54 us
  matrix products: 12.6 us -> 4.51 us
  local copies, waits for them, and re-layouts: 5.77 us -> 8.71 us
  other arithmetic: 7.79 us -> 5.04 us
    pallas_call x0 -> x1, Pallas kernels: none -> 8.54 us  [attention(): pl.pallas_call(attention_kernel, out_shape=jax.ShapeDtypeStruct((rows, he...]
    dot_general x3 -> x0, matrix products: 8.02 us -> none  [the longest x1 6.82 us: on_device(): jnp.dot(normed, weights[:, :projection], preferred_element_type=jnp.float32)]
    unnamed x13 -> x9, local copies, waits for them, and re-layouts: 2.95 us -> 5.53 us
    sub x1 -> x0, other arithmetic: 2.36 us -> none  [attend_pack(): weights = jnp.where(allowed, jnp.exp(scores - highest), jnp.float32(0.0))]
where the time goes in v3:
time: 199 us; the launch traced here: 198 us
  waiting for transfers between devices  68.8 us (35%)
  blocking collectives  61.2 us (31%)
  starting transfers between devices  27.2 us (14%)
  between operations  14.2 us (7%)
  local copies, waits for them, and re-layouts  8.71 us (4%)
  Pallas kernels  8.54 us (4%)
  other arithmetic  5.04 us (3%)
  matrix products  4.51 us (2%)
    all_gather x1, waiting for transfers between devices, on_device(): weights = lax.all_gather(own_weights, dp, axis=0, tiled=True)  35.8 us
    all_to_all x1, waiting for transfers between devices, on_device(): lax.all_to_all(outgoing, dp, split_axis=0, concat_axis=0, tiled=True)  30.8 us
    all_to_all x1, blocking collectives, on_device(): parts = lax.all_to_all(both, 'x', split_axis=0, concat_axis=0, tiled=True)  29.2 us
    all_to_all x1, blocking collectives, on_device(): near = lax.all_to_all(copies, 'x', split_axis=0, concat_axis=0, tiled=True)  25.6 us
    all_to_all x1, starting transfers between devices, on_device(): lax.all_to_all(outgoing, dp, split_axis=0, concat_axis=0, tiled=True)  17.1 us
    ppermute x2, starting transfers between devices, shift(): lax.ppermute(array, axis, [(i, (i + step) % size) for i in range(size)])  10 us
    pallas_call x1, Pallas kernels, attention(): pl.pallas_call(attention_kernel, out_shape=jax.ShapeDtypeStruct((rows, he...  8.54 us
    unnamed x1, blocking collectives  6.35 us
  transfers between devices with their start and end apart: 4, of which 3 were waited for; matrix products, arithmetic and copies ran while one was open for 4% of the time, Pallas kernels for 0%

profile of v3, /device:TPU:1, one launch (start us, length us, event | category | flops | bytes accessed | tf_op | source)
XLA Modules:
  0.0 198.2 jit_solution(11651383322506343468)
XLA Ops:
  6.5 1.6 pad_maximum_fusion
  8.1 0.7 and_select_fusion.1
  8.8 0.2 select_reduce_fusion
  9.1 1.5 convolution_convert_fusion
  10.6 1.2 all_to_all.17
  11.8 17.1 %all-to-all-start = ((bf16[64,2,4224]{2,1,0:T(2,128)(2,1)}), bf16[64,2,4224]{2,1,0:T(2,128)(2,1)S(1)}, u32[]{:S(2)}, u32[]{:S(2)}) async-start(bf16[64,2,4224]{2,1,0:T(2,128)(2,1)} %all_to_all.17), calls=%async_computation | async-start | bytes 2162688 | tf_op jit(solution)/shard_map/dispatch/all_to_all | solution.py:142
  29.0 30.8 %all-to-all-done = bf16[64,2,4224]{2,1,0:T(2,128)(2,1)S(1)} async-done(((bf16[64,2,4224]{2,1,0:T(2,128)(2,1)}), bf16[64,2,4224]{2,1,0:T(2,128)(2,1)S(1)}, u32[]{:S(2)}, u32[]{:S(2)}) %all-to-all-start) | async-done | bytes 1081376 | tf_op jit(solution)/shard_map/dispatch/all_to_all | solution.py:142
  59.7 0.4 all_to_all.19
  60.2 0.1 convert_reduce_fusion
  60.3 0.5 multiply_reduce_fusion
  60.8 0.2 multiply_convert_fusion
  60.9 0.2 broadcast_in_dim.15
  61.2 25.6 %all_to_all.26 = bf16[4,64,4096]{2,1,0:T(8,128)(2,1)S(1)} all-to-all(bf16[4,64,4096]{2,1,0:T(8,128)(2,1)S(1)} %broadcast_in_dim.15), channel_id=1, replica_groups=mesh['z'=8,'y'=8,'x'=4,'core'=2] {'x'}, dimensions={0} | all-to-all | bytes 4194304 | tf_op jit(solution)/shard_map/pack_rows/all_to_all | solution.py:153
  86.8 7.3 %collective-permute-start = (bf16[256,4096]{1,0:T(8,128)(2,1)S(1)}, bf16[256,4096]{1,0:T(8,128)(2,1)}, u32[]{:S(2)}, u32[]{:S(2)}) collective-permute-start(bf16[256,4096]{1,0:T(8,128)(2,1)S(1)} %bitcast.10), channel_id=1, source_target_pairs={{0,1},{1,0},{2,3},{3,2},{4,5},{5,4},{6,7},{7,6},{8,9},{9,8},{10,11... | collective-permute-start | bytes 6291464 | tf_op jit(solution)/shard_map/pack_rows/ppermute | solution.py:109
  94.1 1.3 dynamic-slice
  96.1 0.2 dynamic-update-slice
  96.3 6.3 %all-reduce = s32[512]{0:T(512)S(1)} all-reduce(s32[512]{0:T(512)S(1)} %dynamic-update-slice), channel_id=2, replica_groups=mesh['z'=8,'y'=8,'x'=4,'core'=2] {'x','core'}, use_global_device_ids=true, to_apply=%add | all-reduce | flops 512 | bytes 4096
  102.7 0.1 reshape.164
  102.8 0.6 gather_fusion
  103.5 0.2 reshape.170.doc_column
  103.8 0.1 add.129.place_row
  103.9 0.2 add.133.place_column
  104.1 35.8 %all-gather.3.cloned.1.call-done.weights = bf16[4096,1280]{1,0:T(8,128)(2,1)} async-done(((bf16[64,1280]{1,0:T(8,128)(2,1)}), bf16[4096,1280]{1,0:T(8,128)(2,1)}) %all-gather.3.cloned.1.call-update) | async-done | bytes 10485776 | tf_op jit(solution)/shard_map/weights/all_gather | solution.py:123
  139.9 4.0 %copy-done = bf16[4096,1280]{1,0:T(8,128)(2,1)S(1)} copy-done((bf16[4096,1280]{1,0:T(8,128)(2,1)S(1)}, bf16[4096,1280]{1,0:T(8,128)(2,1)}, u32[]{:S(2)}) %copy-start) | copy-done | bytes 10485784
  143.9 8.5 %attention.1 = bf16[512,512]{1,0:T(8,128)(2,1)S(1)} custom-call(bf16[256,4096]{1,0:T(8,128)(2,1)S(1)} %bitcast.11, bf16[256,4096]{1,0:T(8,128)(2,1)} %collective-permute-done.far, bf16[4096,1280]{1,0:T(8,128)(2,1)S(1)} %copy-done, s32[512,1]{1,0:T(8,128)S(1)} %reshape.170.doc_column, s32[1,512]{1,0:T(1,128)S(1)} %reshape.154.doc_row, ...), custom_call_target="tpu_custom_call" | custom-call | flops 3758096384 | bytes 11010048 | tf_op jit(solution)/shard_map/attention/attention/pallas_call | solution.py:87
  152.4 1.3 convolution_convert_fusion.1
  153.7 2.7 %collective-permute-start.1 = (bf16[256,4096]{1,0:T(8,128)(2,1)S(1)}, bf16[256,4096]{1,0:T(8,128)(2,1)S(1)}, u32[]{:S(2)}, u32[]{:S(2)}) collective-permute-start(bf16[256,4096]{1,0:T(8,128)(2,1)S(1)} %convolution_convert_fusion.1), channel_id=1, source_target_pairs={{0,1},{1,0},{2,3},{3,2},{4,5},{5,4},{6,7},{7,6},{8,9},{9,8},{10,11... | collective-permute-start | bytes 6291464 | tf_op jit(solution)/shard_map/output/ppermute | solution.py:109
  156.5 1.3 convolution_convert_fusion.2
  157.8 2.3 %collective-permute-done.1 = bf16[256,4096]{1,0:T(8,128)(2,1)S(1)} collective-permute-done((bf16[256,4096]{1,0:T(8,128)(2,1)S(1)}, bf16[256,4096]{1,0:T(8,128)(2,1)S(1)}, u32[]{:S(2)}, u32[]{:S(2)}) %collective-permute-start.1) | collective-permute-done | bytes 2097184 | tf_op jit(solution)/shard_map/output/ppermute | solution.py:109
  160.0 0.8 add_convert_fusion
  160.9 29.2 %all_to_all.27 = bf16[4,64,4096]{2,1,0:T(8,128)(2,1)S(1)} all-to-all(bf16[4,64,4096]{2,1,0:T(8,128)(2,1)S(1)} %bitcast.12), channel_id=1, replica_groups=mesh['z'=8,'y'=8,'x'=4,'core'=2] {'x'}, dimensions={0} | all-to-all | bytes 4194304 | tf_op jit(solution)/shard_map/output/all_to_all | solution.py:175
  190.1 1.3 reduce_sum.32
  (20 shorter events, 0.5 us)
Async XLA Ops:
  6.5 133.4 %all-gather.3.cloned.1.call-start = ((), (), s32[]{:S(2)}) async-start(), calls=%async_computation.3 | async-start | bytes 10649600 | tf_op jit(solution)/shard_map/weights/all_gather | solution.py:123
  11.8 47.9 %all-to-all-start = ((bf16[64,2,4224]{2,1,0:T(2,128)(2,1)}), bf16[64,2,4224]{2,1,0:T(2,128)(2,1)S(1)}, u32[]{:S(2)}, u32[]{:S(2)}) async-start(bf16[64,2,4224]{2,1,0:T(2,128)(2,1)} %all_to_all.17), calls=%async_computation | async-start | bytes 2162688 | tf_op jit(solution)/shard_map/dispatch/all_to_all | solution.py:142
  29.0 31.8 %copy-start.1 = (f32[4096]{0:T(1024)S(1)}, f32[4096]{0:T(1024)}, u32[]{:S(2)}) copy-start(f32[4096]{0:T(1024)} %param.11) | copy-start | bytes 49156
  61.2 34.9 %copy-start.2 = (s32[64]{0:T(128)S(1)}, s32[64]{0:T(128)}, u32[]{:S(2)}) copy-start(s32[64]{0:T(128)} %param.10) | copy-start | bytes 772
  86.8 17.3 %collective-permute-start = (bf16[256,4096]{1,0:T(8,128)(2,1)S(1)}, bf16[256,4096]{1,0:T(8,128)(2,1)}, u32[]{:S(2)}, u32[]{:S(2)}) collective-permute-start(bf16[256,4096]{1,0:T(8,128)(2,1)S(1)} %bitcast.10), channel_id=1, source_target_pairs={{0,1},{1,0},{2,3},{3,2},{4,5},{5,4},{6,7},{7,6},{8,9},{9,8},{10,11... | collective-permute-start | bytes 6291464 | tf_op jit(solution)/shard_map/pack_rows/ppermute | solution.py:109
  139.9 4.0 %copy-start = (bf16[4096,1280]{1,0:T(8,128)(2,1)S(1)}, bf16[4096,1280]{1,0:T(8,128)(2,1)}, u32[]{:S(2)}) copy-start(bf16[4096,1280]{1,0:T(8,128)(2,1)} %all-gather.3.cloned.1.call-done.weights) | copy-start | bytes 31457284
  153.7 6.3 %collective-permute-start.1 = (bf16[256,4096]{1,0:T(8,128)(2,1)S(1)}, bf16[256,4096]{1,0:T(8,128)(2,1)S(1)}, u32[]{:S(2)}, u32[]{:S(2)}) collective-permute-start(bf16[256,4096]{1,0:T(8,128)(2,1)S(1)} %convolution_convert_fusion.1), channel_id=1, source_target_pairs={{0,1},{1,0},{2,3},{3,2},{4,5},{5,4},{6,7},{7,6},{8,9},{9,8},{10,11... | collective-permute-start | bytes 6291464 | tf_op jit(solution)/shard_map/output/ppermute | solution.py:109
Sparse Core Ops, SparseCore 0:
  10.4 129.4 all-gather.2

commit v4 on v2

v4 whole, which is shorter than its diff:
```python
import functools
import math

import jax
import jax.numpy as jnp
from jax import lax
from jax.experimental import pallas as pl
from jax.experimental.pallas import tpu as pltpu
from jax.sharding import Mesh, PartitionSpec as P

HEAD_DIM = 128
LANES = 128
SIDE = 8
ROWS = 64
VMEM_BYTES = 16 * 1024 * 1024
PLANE = ("z", "y", "core")


def rms_rows(states, norm_gain):
    floats = states.astype(jnp.float32)
    mean_square = jnp.mean(floats * floats, axis=-1, keepdims=True)
    return (floats * lax.rsqrt(mean_square + 1e-05) * norm_gain).astype(jnp.bfloat16)


def shift(array, axis, step):
    size = lax.axis_size(axis)
    return lax.ppermute(array, axis, [(i, (i + step) % size) for i in range(size)])


def spread(block, axis):
    size = lax.axis_size(axis)
    copies = jnp.broadcast_to(block[None], (size,) + block.shape)
    return lax.all_to_all(copies, axis, split_axis=0, concat_axis=0, tiled=True)


def member(z, y, core):
    return ((z % SIDE) * SIDE + y % SIDE) * 2 + core


def spread_lines(block):
    groups = [[member(z, y, 0) for y in range(SIDE)] for z in range(SIDE)]
    groups += [[member(z, y, 1) for z in range(SIDE)] for y in range(SIDE)]
    copies = jnp.broadcast_to(block[None], (SIDE,) + block.shape)
    return lax.all_to_all(
        copies, PLANE, split_axis=0, concat_axis=0, axis_index_groups=groups, tiled=True
    )


def across(array, step):
    pairs = []
    for z in range(SIDE):
        for y in range(SIDE):
            pairs.append((member(z, y, 0), member(z + step, y, 0)))
            pairs.append((member(z, y, 1), member(z, y + step, 1)))
    return lax.ppermute(array, PLANE, pairs)


def ring_step(blocks):
    return across(blocks[0], -1), across(blocks[1], 1)


HERE = pl.BlockSpec(memory_space=pltpu.VMEM)
SCALAR = pl.BlockSpec(memory_space=pltpu.SMEM)
PARAMS = pltpu.CompilerParams(vmem_limit_bytes=VMEM_BYTES)


def turn(load, out, width):
    half = LANES // 2
    rows = out.shape[0]
    lower = lax.broadcasted_iota(jnp.int32, (rows, LANES), 1) < half
    for p in range(0, SIDE, 2):
        for q in range(0, SIDE, 2):
            left = load((p * SIDE + q) * half)
            right = load(((p + 1) * SIDE + q) * half)
            first = jnp.where(lower, left, pltpu.roll(right, half, 1))
            second = jnp.where(lower, pltpu.roll(left, half, 1), right)
            for offset, value in ((0, first), (1, second)):
                at = ((q + offset) * SIDE + p) * half
                out[:, at : at + LANES] = value.astype(out.dtype)


def keep(load, out, width):
    for at in range(0, width, LANES):
        out[:, at : at + LANES] = load(at).astype(out.dtype)


def turn_kernel(turned, rows, out):
    width = SIDE * SIDE * LANES // 2

    def load(at):
        return rows[:, at : at + LANES].astype(jnp.float32)

    @pl.when(turned[0] == 1)
    def _():
        turn(load, out, width)

    @pl.when(turned[0] == 0)
    def _():
        keep(load, out, width)

    out[:, width:] = rows[:, width:]


def turn_rows(rows, turned):
    return pl.pallas_call(
        turn_kernel,
        out_shape=jax.ShapeDtypeStruct(rows.shape, rows.dtype),
        in_specs=[SCALAR, HERE],
        out_specs=HERE,
        compiler_params=PARAMS,
        name="turn_rows",
    )(turned, rows)


def add_products(ring_at, near, far, total, blocks, steps, projection, first):
    half = near.shape[0]
    span = SIDE * ROWS
    for index, (block, step) in enumerate(zip(blocks, steps)):
        place = lax.rem(ring_at[0] + step, SIDE) * span
        chunk = pl.ds(pl.multiple_of(place, span), span)
        for part, rows in enumerate((near, far)):
            here = slice(part * half, (part + 1) * half)
            term = jnp.dot(
                rows[:, chunk], block[:, :projection], preferred_element_type=jnp.float32
            )
            if first and index == 0:
                total[here, :] = term
            else:
                total[here, :] += term


def collect(blocks, out_rows, projection):
    start = 0
    for block in blocks:
        out_rows[start : start + block.shape[0], :] = block[:, projection:]
        start += block.shape[0]


def project_kernel(steps, ring_at, near, far, *rest):
    blocks, total, out_rows = rest[: len(steps)], rest[-2], rest[-1]
    projection = total.shape[1]
    first = len(rest) == len(steps) + 2
    collect(blocks, out_rows, projection)
    if not first:
        total[...] = rest[-3][...]
    add_products(ring_at, near, far, total, blocks, steps, projection, first)


def project(ring_at, near, far, blocks, steps, projection, so_far=None):
    rows, depth = 2 * near.shape[0], sum(block.shape[0] for block in blocks)
    columns = blocks[0].shape[1]
    operands = (ring_at, near, far, *blocks) + (() if so_far is None else (so_far,))
    return pl.pallas_call(
        functools.partial(project_kernel, steps),
        out_shape=[
            jax.ShapeDtypeStruct((rows, projection), jnp.float32),
            jax.ShapeDtypeStruct((depth, columns - projection), jnp.bfloat16),
        ],
        in_specs=[SCALAR] + [HERE] * (len(operands) - 1),
        out_specs=[HERE, HERE],
        compiler_params=PARAMS,
        cost_estimate=pl.CostEstimate(
            flops=2 * rows * depth * projection,
            bytes_accessed=2 * depth * (rows + columns),
            transcendentals=0,
        ),
        name="project",
    )(*operands)


def attention_kernel(
    steps, ring_at, near, far, doc_column, doc_row, place_column, place_row, so_far, *rest
):
    blocks, (attended, out_rows, total, held) = rest[: len(steps)], rest[len(steps) :]
    half = near.shape[0]
    projection = held.shape[1]
    group = attended.shape[1] // HEAD_DIM
    halves = [slice(0, half), slice(half, 2 * half)]
    collect(blocks, out_rows, projection)
    total[...] = so_far[...]
    add_products(ring_at, near, far, total, blocks, steps, projection, False)
    held[...] = total[...].astype(jnp.bfloat16)
    key_at = group * HEAD_DIM
    keys = held[:, key_at : key_at + HEAD_DIM]
    values = held[:, key_at + HEAD_DIM : key_at + 2 * HEAD_DIM]
    scale = HEAD_DIM**-0.5 * math.log2(math.e)
    for here in halves:
        same = doc_column[here, :] == doc_row[...]
        allowed = same & (place_column[here, :] >= place_row[...])
        hidden = jnp.where(allowed, 0.0, -1e30)
        for head in range(group):
            lanes = slice(head * HEAD_DIM, (head + 1) * HEAD_DIM)
            scores = lax.dot_general(
                held[here, lanes], keys, (((1,), (1,)), ((), ())), preferred_element_type=jnp.float32
            )
            scores = scores * scale + hidden
            weight = jnp.exp2(scores - jnp.max(scores, axis=1, keepdims=True))
            share = 1.0 / jnp.sum(weight, axis=1, keepdims=True)
            mixed = jnp.dot(weight.astype(jnp.bfloat16), values, preferred_element_type=jnp.float32)
            attended[here, lanes] = (mixed * share).astype(jnp.bfloat16)


def attention(ring_at, near, far, docs, places, so_far, blocks, steps, head_columns):
    rows, projection = so_far.shape
    depth = sum(block.shape[0] for block in blocks)
    columns = blocks[0].shape[1]
    masks = (docs[:, None], docs[None, :], places[:, None], places[None, :])
    return pl.pallas_call(
        functools.partial(attention_kernel, steps),
        out_shape=[
            jax.ShapeDtypeStruct((rows, head_columns), jnp.bfloat16),
            jax.ShapeDtypeStruct((depth, columns - projection), jnp.bfloat16),
        ],
        in_specs=[SCALAR] + [HERE] * (7 + len(blocks)),
        out_specs=[HERE, HERE],
        scratch_shapes=[
            pltpu.VMEM((rows, projection), jnp.float32),
            pltpu.VMEM((rows, projection), jnp.bfloat16),
        ],
        compiler_params=PARAMS,
        cost_estimate=pl.CostEstimate(
            flops=2 * rows * depth * projection + 4 * rows * rows * head_columns,
            bytes_accessed=2 * depth * columns + 8 * rows * projection,
            transcendentals=rows * rows * head_columns // HEAD_DIM,
        ),
        name="attention",
    )(ring_at, near, far, *masks, so_far, *blocks)


def output_kernel(first, turned, steps, ring_at, attended, *rest):
    pieces, out, held = rest[:-2], rest[-2], rest[-1]
    rows = out.shape[0]
    span = SIDE * ROWS
    result = held if turned else out
    index = 0
    for piece in pieces:
        for start in range(0, piece.shape[0], span):
            term = lax.dot_general(
                attended[first : first + rows, :],
                piece[start : start + span, :],
                (((1,), (1,)), ((), ())),
                preferred_element_type=jnp.float32,
            )
            place = lax.rem(ring_at[0] + steps[index], SIDE) * span
            result[:, pl.ds(pl.multiple_of(place, span), span)] = term.astype(result.dtype)
            index += 1
    if turned:
        turn(lambda at: held[:, at : at + LANES], out, out.shape[1])


def output_half(first, rows, turned, ring_at, attended, pieces, steps):
    columns = sum(piece.shape[0] for piece in pieces)
    held = pltpu.VMEM((rows, columns) if turned else (8, LANES), jnp.float32)
    return pl.pallas_call(
        functools.partial(output_kernel, first, turned, steps),
        out_shape=jax.ShapeDtypeStruct((rows, columns), jnp.bfloat16),
        in_specs=[SCALAR] + [HERE] * (1 + len(pieces)),
        out_specs=HERE,
        scratch_shapes=[held],
        compiler_params=PARAMS,
        cost_estimate=pl.CostEstimate(
            flops=2 * rows * columns * attended.shape[1],
            bytes_accessed=2 * columns * (rows + attended.shape[1]),
            transcendentals=0,
        ),
        name="output_product",
    )(ring_at, attended, *pieces)


def finish_kernel(turned, parts, out):
    count = parts.shape[0]

    def load(at):
        total = parts[0, :, at : at + LANES].astype(jnp.float32)
        for part in range(1, count):
            total = total + parts[part, :, at : at + LANES].astype(jnp.float32)
        return total

    @pl.when(turned[0] == 1)
    def _():
        turn(load, out, out.shape[1])

    @pl.when(turned[0] == 0)
    def _():
        keep(load, out, out.shape[1])


def finish(parts, turned):
    return pl.pallas_call(
        finish_kernel,
        out_shape=jax.ShapeDtypeStruct(parts.shape[1:], jnp.bfloat16),
        in_specs=[SCALAR, HERE],
        out_specs=HERE,
        compiler_params=PARAMS,
        name="finish",
    )(turned, parts)


def on_device(tokens, repack_plan, document_ids, norm_gain, w_query, w_key, w_value, w_out):
    row_count, width = tokens.shape
    x_count = lax.axis_size("x")
    peer_count = SIDE * SIDE
    core_index = lax.axis_index("core").astype(jnp.int32)
    ring_at = jnp.where(core_index == 0, lax.axis_index("z"), lax.axis_index("y"))
    ring_at = ring_at.astype(jnp.int32).reshape(1)
    turned = core_index.reshape(1)
    pack_rows = row_count * x_count * 2
    projection = w_query.shape[1] + w_key.shape[1] + w_value.shape[1]
    positions = jnp.arange(row_count, dtype=jnp.int32)

    with jax.named_scope("weights_spread"):
        own_weights = jnp.concatenate([w_query, w_key, w_value, w_out.T], axis=1)
        line = spread_lines(own_weights).reshape(SIDE * row_count, -1)

    with jax.named_scope("dispatch"):
        capacity = 2
        slot_count = peer_count * capacity
        target = repack_plan // pack_rows
        landing = repack_plan % row_count
        same_pack = target[:, None] == target[None, :]
        earlier = positions[None, :] < positions[:, None]
        slot_rank = jnp.sum(jnp.where(same_pack & earlier, 1, 0), axis=1).astype(jnp.int32)
        slot_of = target * capacity + slot_rank
        selector = slot_of[None, :] == jnp.arange(slot_count, dtype=jnp.int32)[:, None]
        marks = jnp.broadcast_to((landing + 1)[:, None], (row_count, LANES)).astype(jnp.bfloat16)
        outgoing = jnp.dot(
            selector.astype(jnp.bfloat16),
            jnp.concatenate([tokens, marks], axis=1),
            preferred_element_type=jnp.float32,
        ).astype(jnp.bfloat16)
        line, outgoing = lax.optimization_barrier((line, outgoing))
        line_1 = ring_step((line, line))
        arrived = lax.all_to_all(outgoing, ("z", "y"), split_axis=0, concat_axis=0, tiled=True)
        arrived_marks = arrived[:, width].astype(jnp.int32)
        settle = arrived_marks[None, :] == positions[:, None] + 1
        owned = jnp.dot(
            settle.astype(jnp.bfloat16), arrived[:, :width], preferred_element_type=jnp.float32
        ).astype(jnp.bfloat16)
        normed_own = rms_rows(owned, norm_gain)

    with jax.named_scope("pack_rows"):
        doc_columns = jnp.broadcast_to(document_ids[:, None], (row_count, LANES))
        labelled = jnp.concatenate([normed_own, doc_columns.astype(jnp.bfloat16)], axis=1)
        labelled = turn_rows(labelled, turned)
        line_1, _ = lax.optimization_barrier((line_1, labelled))
        line_2 = ring_step(line_1)
        line_3 = ring_step(line_2)
        near = spread(labelled, "x").reshape(x_count * row_count, -1)
        near, _ = lax.optimization_barrier((near, line_2[0]))
        far = shift(turn_rows(near, jnp.ones((1,), jnp.int32)), "core", 1)
        line_4 = (across(line_3[0], -1),)
        far, _ = lax.optimization_barrier((far, line_3))
        docs = jnp.concatenate([near[:, width], far[:, width]]).astype(jnp.int32)
        even = 2 * jnp.arange(x_count, dtype=jnp.int32)
        block_of = jnp.concatenate([even + core_index, even + 1 - core_index])
        places = (block_of[:, None] * row_count + positions[None, :]).reshape(pack_rows)

    with jax.named_scope("attention"):
        early, early_steps = [line, *line_1, *line_2], (0, 1, 7, 2, 6)
        so_far, pieces = project(ring_at, near, far, early, early_steps, projection)
        so_far, pieces_3 = project(ring_at, near, far, line_3, (3, 5), projection, so_far)
        attended, pieces_4 = attention(
            ring_at, near, far, docs, places, so_far, line_4, (4,), w_query.shape[1]
        )

    with jax.named_scope("output"):
        half = x_count * row_count
        pieces = (pieces, pieces_3, pieces_4)
        steps = early_steps + (3, 5, 4)
        theirs = output_half(half, half, True, ring_at, attended, pieces, steps)
        received = shift(theirs, "core", 1)
        ours = output_half(0, half, False, ring_at, attended, pieces, steps)
        both = (ours.astype(jnp.float32) + received.astype(jnp.float32)).astype(jnp.bfloat16)
        parts = lax.all_to_all(both, "x", split_axis=0, concat_axis=0, tiled=True)
        return finish(parts.reshape(x_count, row_count, -1), turned)


def solution(mesh):
    grid = Mesh(mesh.devices.reshape(SIDE, SIDE, 4, 2), ("z", "y", "x", "core"))
    dp, tensor, rows = ("z", "y"), ("x", "core"), ("z", "y", "x", "core")
    return jax.shard_map(
        on_device,
        mesh=grid,
        in_specs=(
            P(rows, None),
            P(rows),
            P(rows),
            P(),
            P(dp, tensor),
            P(dp, tensor),
            P(dp, tensor),
            P(tensor, dp),
        ),
        out_specs=P(rows, None),
        check_vma=False,
    )
```

time: 198 us -> 196 us (0.990)
  blocking collectives: 61.4 us -> 29.3 us
  starting transfers between devices: 27 us -> 53.8 us
  Pallas kernels: 0 us -> 21.2 us
  between operations: 14.3 us -> 0.31 us
  matrix products: 12.6 us -> 0.89 us
  waiting for transfers between devices: 68.9 us -> 80.5 us
  other arithmetic: 7.79 us -> 2.42 us
    ppermute x0 -> x7, waiting for transfers between devices: none -> 37.9 us  [across(): return lax.ppermute(array, PLANE, pairs)]
    all_gather x1 -> x0, waiting for transfers between devices: 35.7 us -> none  [on_device(): weights = lax.all_gather(own_weights, dp, axis=0, tiled=True)]
    all_to_all x1 -> x0, blocking collectives: 25.9 us -> none  [on_device(): near = lax.all_to_all(copies, 'x', split_axis=0, concat_axis=0, tiled=True)]
    ppermute x0 -> x7, starting transfers between devices: none -> 21.3 us  [across(): return lax.ppermute(array, PLANE, pairs)]
    pallas_call x0 -> x8, Pallas kernels: none -> 21.2 us  [the longest x2 9.01 us: project(): pl.pallas_call(functools.partial(project_kernel, steps), out_shape=[jax.S...]
    dot_general x5 -> x0, matrix products: 10.6 us -> none  [the longest x1 6.82 us: on_device(): jnp.dot(normed, weights[:, :projection], preferred_element_type=jnp.float32)]
    all_to_all x1 -> x3, waiting for transfers between devices: 30.7 us -> 40.2 us  [the longest x1 20.1 us: spread_lines(): lax.all_to_all(copies, PLANE, split_axis=0, concat_axis=0, axis_index_gro...]
    unnamed x1 -> x0, blocking collectives: 6.35 us -> none
  transfers between devices with their start and end apart: 4 -> 12, of which waited for: 3 -> 8; matrix products, arithmetic and copies ran while one was open for 4% -> 3% of each run, Pallas kernels for 0% -> 7%
where the time goes in v4:
time: 196 us; the launch traced here: 195 us
  waiting for transfers between devices  80.5 us (41%)
  starting transfers between devices  53.8 us (27%)
  blocking collectives  29.3 us (15%)
  Pallas kernels  21.2 us (11%)
  local copies, waits for them, and re-layouts  6.67 us (3%)
  other arithmetic  2.42 us (1%)
    ppermute x7, waiting for transfers between devices, across(): return lax.ppermute(array, PLANE, pairs)  37.9 us
    all_to_all x1, blocking collectives, on_device(): parts = lax.all_to_all(both, 'x', split_axis=0, concat_axis=0, tiled=True)  29.3 us
    ppermute x7, starting transfers between devices, across(): return lax.ppermute(array, PLANE, pairs)  21.3 us
    all_to_all x1, waiting for transfers between devices, spread_lines(): lax.all_to_all(copies, PLANE, split_axis=0, concat_axis=0, axis_index_gro...  20.1 us
    all_to_all x1, waiting for transfers between devices, on_device(): lax.all_to_all(outgoing, ('z', 'y'), split_axis=0, concat_axis=0, tiled=T...  20.1 us
    all_to_all x1, starting transfers between devices, spread_lines(): lax.all_to_all(copies, PLANE, split_axis=0, concat_axis=0, axis_index_gro...  11 us
    ppermute x2, starting transfers between devices, shift(): lax.ppermute(array, axis, [(i, (i + step) % size) for i in range(size)])  9.51 us
    pallas_call x2, Pallas kernels, project(): pl.pallas_call(functools.partial(project_kernel, steps), out_shape=[jax.S...  9.01 us
  transfers between devices with their start and end apart: 12, of which 8 were waited for; matrix products, arithmetic and copies ran while one was open for 3% of the time, Pallas kernels for 7%

profile of v4, /device:TPU:1, one launch (start us, length us, event | category | flops | bytes accessed | tf_op | source)
XLA Modules:
  0.0 195.1 jit_solution(1359935709577989790)
XLA Ops:
  0.9 1.2 broadcast_in_dim.16
  2.1 11.0 %all-to-all-start = ((bf16[8,64,1280]{2,1,0:T(8,128)(2,1)}), bf16[8,64,1280]{2,1,0:T(8,128)(2,1)S(1)}, u32[]{:S(2)}, u32[]{:S(2)}) async-start(bf16[8,64,1280]{2,1,0:T(8,128)(2,1)} %broadcast_in_dim.16), calls=%async_computation | async-start | bytes 2621440 | tf_op jit(solution)/shard_map/weights_spread/all_to_all | solution.py:44
  13.8 20.1 %all-to-all-done = bf16[8,64,1280]{2,1,0:T(8,128)(2,1)S(1)} async-done(((bf16[8,64,1280]{2,1,0:T(8,128)(2,1)}), bf16[8,64,1280]{2,1,0:T(8,128)(2,1)S(1)}, u32[]{:S(2)}, u32[]{:S(2)}) %all-to-all-start) | async-done | bytes 1310752 | tf_op jit(solution)/shard_map/weights_spread/all_to_all | solution.py:44
  34.0 1.2 all_to_all.21
  35.2 8.0 %all-to-all-start.1 = ((bf16[64,2,4224]{2,1,0:T(2,128)(2,1)}), bf16[64,2,4224]{2,1,0:T(2,128)(2,1)S(1)}, u32[]{:S(2)}, u32[]{:S(2)}) async-start(bf16[64,2,4224]{2,1,0:T(2,128)(2,1)} %all_to_all.21), calls=%async_computation.1 | async-start | bytes 2162688 | tf_op jit(solution)/shard_map/dispatch/all_to_all | solution.py:333
  43.2 4.1 %collective-permute-start = (bf16[512,1280]{1,0:T(8,128)(2,1)S(1)}, bf16[512,1280]{1,0:T(8,128)(2,1)}, u32[]{:S(2)}, u32[]{:S(2)}) collective-permute-start(bf16[512,1280]{1,0:T(8,128)(2,1)S(1)} %bitcast.11), channel_id=1, source_target_pairs={{0,448},{1,57},{8,456},{9,1},{16,464},{17,9},{24,472},{25,17},{32,... | collective-permute-start | bytes 3932168 | tf_op jit(solution)/shard_map/dispatch/ppermute | solution.py:55
  47.3 1.9 collective-permute-start.1
  49.3 20.1 %all-to-all-done.1 = bf16[64,2,4224]{2,1,0:T(2,128)(2,1)S(1)} async-done(((bf16[64,2,4224]{2,1,0:T(2,128)(2,1)}), bf16[64,2,4224]{2,1,0:T(2,128)(2,1)S(1)}, u32[]{:S(2)}, u32[]{:S(2)}) %all-to-all-start.1) | async-done | bytes 1081376 | tf_op jit(solution)/shard_map/dispatch/all_to_all | solution.py:333
  71.0 1.5 broadcast_in_dim.21
  72.5 4.0 %all-to-all-start.2 = ((bf16[4,64,4224]{2,1,0:T(8,128)(2,1)}), bf16[4,64,4224]{2,1,0:T(8,128)(2,1)S(1)}, u32[]{:S(2)}, u32[]{:S(2)}) async-start(bf16[4,64,4224]{2,1,0:T(8,128)(2,1)} %broadcast_in_dim.21), calls=%async_computation.2 | async-start | bytes 4325376 | tf_op jit(solution)/shard_map/pack_rows/all_to_all | solution.py:33
  76.5 6.0 %collective-permute-done.rest_1_ = bf16[512,1280]{1,0:T(8,128)(2,1)} collective-permute-done((bf16[512,1280]{1,0:T(8,128)(2,1)S(1)}, bf16[512,1280]{1,0:T(8,128)(2,1)}, u32[]{:S(2)}, u32[]{:S(2)}) %collective-permute-start) | collective-permute-done | bytes 1310752 | tf_op jit(solution)/shard_map/dispatch/ppermute | solution.py:55
  82.6 1.2 collective-permute-done.1.rest_2_
  83.8 3.1 %collective-permute-start.2 = (bf16[512,1280]{1,0:T(8,128)(2,1)}, bf16[512,1280]{1,0:T(8,128)(2,1)}, u32[]{:S(2)}, u32[]{:S(2)}) collective-permute-start(bf16[512,1280]{1,0:T(8,128)(2,1)} %collective-permute-done.rest_1_), channel_id=1, source_target_pairs={{0,448},{1,57},{8,456},{9,1},{16,464},{17,9},{24,472},{25,17},{32,... | collective-permute-start | bytes 3932168 | tf_op jit(solution)/shard_map/pack_rows/ppermute | solution.py:55
  86.9 2.2 %collective-permute-start.5 = (bf16[512,1280]{1,0:T(8,128)(2,1)}, bf16[512,1280]{1,0:T(8,128)(2,1)}, u32[]{:S(2)}, u32[]{:S(2)}) collective-permute-start(bf16[512,1280]{1,0:T(8,128)(2,1)} %collective-permute-done.1.rest_2_), channel_id=1, source_target_pairs={{0,64},{1,9},{8,72},{9,17},{16,80},{17,25},{24,88},{25,33},{32,96}... | collective-permute-start | bytes 3932168 | tf_op jit(solution)/shard_map/pack_rows/ppermute | solution.py:55
  89.1 13.7 %collective-permute-done.2.rest_3_ = bf16[512,1280]{1,0:T(8,128)(2,1)} collective-permute-done((bf16[512,1280]{1,0:T(8,128)(2,1)}, bf16[512,1280]{1,0:T(8,128)(2,1)}, u32[]{:S(2)}, u32[]{:S(2)}) %collective-permute-start.2) | collective-permute-done | bytes 1310752 | tf_op jit(solution)/shard_map/pack_rows/ppermute | solution.py:55
  102.7 2.2 %turn_rows.3 = bf16[256,4224]{1,0:T(8,128)(2,1)} custom-call(s32[1]{0:T(128)} %constant.60.clone.1.turned, bf16[256,4224]{1,0:T(8,128)(2,1)S(1)} %bitcast.6), custom_call_target="tpu_custom_call" | custom-call | tf_op jit(solution)/shard_map/pack_rows/turn_rows/pallas_call | solution.py:105
  104.9 5.3 %collective-permute-start.3 = (bf16[256,4224]{1,0:T(8,128)(2,1)}, bf16[256,4224]{1,0:T(8,128)(2,1)}, u32[]{:S(2)}, u32[]{:S(2)}) collective-permute-start(bf16[256,4224]{1,0:T(8,128)(2,1)} %turn_rows.3), channel_id=1, source_target_pairs={{0,1},{1,0},{2,3},{3,2},{4,5},{5,4},{6,7},{7,6},{8,9},{9,8},{10,11... | collective-permute-start | bytes 6488072 | tf_op jit(solution)/shard_map/pack_rows/ppermute | solution.py:27
  110.3 3.3 %collective-permute-start.4 = (bf16[512,1280]{1,0:T(8,128)(2,1)}, bf16[512,1280]{1,0:T(8,128)(2,1)}, u32[]{:S(2)}, u32[]{:S(2)}) collective-permute-start(bf16[512,1280]{1,0:T(8,128)(2,1)} %collective-permute-done.2.rest_3_), channel_id=1, source_target_pairs={{0,448},{1,57},{8,456},{9,1},{16,464},{17,9},{24,472},{25,17},{32,... | collective-permute-start | bytes 3932168 | tf_op jit(solution)/shard_map/pack_rows/ppermute | solution.py:55
  113.6 2.0 %collective-permute-start.6 = (bf16[512,1280]{1,0:T(8,128)(2,1)}, bf16[512,1280]{1,0:T(8,128)(2,1)}, u32[]{:S(2)}, u32[]{:S(2)}) collective-permute-start(bf16[512,1280]{1,0:T(8,128)(2,1)} %collective-permute-done.5.rest_4_), channel_id=1, source_target_pairs={{0,64},{1,9},{8,72},{9,17},{16,80},{17,25},{24,88},{25,33},{32,96}... | collective-permute-start | bytes 3932168 | tf_op jit(solution)/shard_map/pack_rows/ppermute | solution.py:55
  115.6 13.7 %collective-permute-done.4.rest_0_ = bf16[512,1280]{1,0:T(8,128)(2,1)} collective-permute-done((bf16[512,1280]{1,0:T(8,128)(2,1)}, bf16[512,1280]{1,0:T(8,128)(2,1)}, u32[]{:S(2)}, u32[]{:S(2)}) %collective-permute-start.4) | collective-permute-done | bytes 1310752 | tf_op jit(solution)/shard_map/pack_rows/ppermute | solution.py:55
  129.2 4.7 %collective-permute-start.7 = (bf16[512,1280]{1,0:T(8,128)(2,1)}, bf16[512,1280]{1,0:T(8,128)(2,1)}, u32[]{:S(2)}, u32[]{:S(2)}) collective-permute-start(bf16[512,1280]{1,0:T(8,128)(2,1)} %collective-permute-done.4.rest_0_), channel_id=1, source_target_pairs={{0,448},{1,57},{8,456},{9,1},{16,464},{17,9},{24,472},{25,17},{32,... | collective-permute-start | bytes 3932168 | tf_op jit(solution)/shard_map/pack_rows/ppermute | solution.py:55
  135.2 0.9 slice_reduce_fusion
  136.2 5.5 %project.2 = (f32[512,768]{1,0:T(8,128)S(1)}, bf16[2560,512]{1,0:T(8,128)(2,1)S(1)}) custom-call(s32[1]{0:T(128)} %bitcast.1.ring_at, bf16[256,4224]{1,0:T(8,128)(2,1)S(1)} %bitcast.8, bf16[256,4224]{1,0:T(8,128)(2,1)} %collective-permute-done.3.far, bf16[512,1280]{1,0:T(8,128)(2,1)S(1)} %bitcast.13, bf16[512,1280]{1,0:T(8,128)(2,1)} %collective-permute-done.rest_1_, ...), custom_call_target="tpu_custom_call" | custom-call | flops 2013265920 | bytes 9175040 | tf_op jit(solution)/shard_map/attention/project/pallas_call | solution.py:153
  141.7 3.5 %project.3 = (f32[512,768]{1,0:T(8,128)S(1)}, bf16[1024,512]{1,0:T(8,128)(2,1)S(1)}) custom-call(s32[1]{0:T(128)} %bitcast.1.ring_at, bf16[256,4224]{1,0:T(8,128)(2,1)S(1)} %bitcast.9, bf16[256,4224]{1,0:T(8,128)(2,1)} %collective-permute-done.3.far, bf16[512,1280]{1,0:T(8,128)(2,1)} %collective-permute-done.4.rest_0_, ...), custom_call_target="tpu_custom_call" | custom-call | flops 805306368 | bytes 3670016 | tf_op jit(solution)/shard_map/attention/project/pallas_call | solution.py:153
  145.3 3.3 %collective-permute-done.7.rest_0_ = bf16[512,1280]{1,0:T(8,128)(2,1)} collective-permute-done((bf16[512,1280]{1,0:T(8,128)(2,1)}, bf16[512,1280]{1,0:T(8,128)(2,1)}, u32[]{:S(2)}, u32[]{:S(2)}) %collective-permute-start.7) | collective-permute-done | bytes 1310752 | tf_op jit(solution)/shard_map/pack_rows/ppermute | solution.py:55
  148.6 5.2 %attention.1 = (bf16[512,512]{1,0:T(8,128)(2,1)S(1)}, bf16[512,512]{1,0:T(8,128)(2,1)S(1)}) custom-call(s32[1]{0:T(128)} %bitcast.1.ring_at, bf16[256,4224]{1,0:T(8,128)(2,1)S(1)} %bitcast.10, bf16[256,4224]{1,0:T(8,128)(2,1)} %collective-permute-done.3.far, s32[512,1]{1,0:T(8,128)S(1)} %maximum_convert_fusion.doc_column, ...), custom_call_target="tpu_custom_call" | custom-call | flops 939524096 | bytes 4456448 | tf_op jit(solution)/shard_map/attention/attention/pallas_call | solution.py:208
  153.8 2.0 %output_product.3 = bf16[256,4096]{1,0:T(8,128)(2,1)S(1)} custom-call(s32[1]{0:T(128)} %bitcast.1.ring_at, bf16[512,512]{1,0:T(8,128)(2,1)S(1)} %get-tuple-element.25.attended, bf16[2560,512]{1,0:T(8,128)(2,1)S(1)} %get-tuple-element.26.rest_0_, bf16[1024,512]{1,0:T(8,128)(2,1)S(1)} %get-tuple-element.27.rest_1_, bf16[512,512]{1,0:T(8,128)(2,1)S(1)} %get-tuple-element.28.rest_2_), custom_call_target="tpu_custom_call" | custom-call | flops 1073741824 | bytes 6291456 | tf_op jit(solution)/shard_map/output/output_product/pallas_call | solution.py:254
  155.8 4.2 %collective-permute-start.8 = (bf16[256,4096]{1,0:T(8,128)(2,1)S(1)}, bf16[256,4096]{1,0:T(8,128)(2,1)S(1)}, u32[]{:S(2)}, u32[]{:S(2)}) collective-permute-start(bf16[256,4096]{1,0:T(8,128)(2,1)S(1)} %output_product.3), channel_id=1, source_target_pairs={{0,1},{1,0},{2,3},{3,2},{4,5},{5,4},{6,7},{7,6},{8,9},{9,8},{10,11... | collective-permute-start | bytes 6291464 | tf_op jit(solution)/shard_map/output/ppermute | solution.py:27
  160.0 1.3 output_product.2
  161.3 2.5 %collective-permute-done.8 = bf16[256,4096]{1,0:T(8,128)(2,1)S(1)} collective-permute-done((bf16[256,4096]{1,0:T(8,128)(2,1)S(1)}, bf16[256,4096]{1,0:T(8,128)(2,1)S(1)}, u32[]{:S(2)}, u32[]{:S(2)}) %collective-permute-start.8) | collective-permute-done | bytes 2097184 | tf_op jit(solution)/shard_map/output/ppermute | solution.py:27
  164.6 29.3 %all_to_all.31.parts = bf16[4,64,4096]{2,1,0:T(8,128)(2,1)S(1)} all-to-all(bf16[4,64,4096]{2,1,0:T(8,128)(2,1)S(1)} %bitcast.14), channel_id=1, replica_groups=mesh['z'=8,'y'=8,'x'=4,'core'=2] {'x'}, dimensions={0} | all-to-all | bytes 4194304 | tf_op jit(solution)/shard_map/output/all_to_all | solution.py:374
  193.9 1.2 finish.1
  (41 shorter events, 5.4 us)
Async XLA Ops:
  2.1 11.0 %copy-start.3 = (s32[64]{0:T(128)S(1)}, s32[64]{0:T(128)}, u32[]{:S(2)}) copy-start(s32[64]{0:T(128)} %param.9) | copy-start | bytes 772
  2.1 11.3 %copy-start.1 = (bf16[64,4096]{1,0:T(8,128)(2,1)S(1)}, bf16[64,4096]{1,0:T(8,128)(2,1)}, u32[]{:S(2)}) copy-start(bf16[64,4096]{1,0:T(8,128)(2,1)} %param.8) | copy-start | bytes 1572868
  2.1 31.9 %all-to-all-start = ((bf16[8,64,1280]{2,1,0:T(8,128)(2,1)}), bf16[8,64,1280]{2,1,0:T(8,128)(2,1)S(1)}, u32[]{:S(2)}, u32[]{:S(2)}) async-start(bf16[8,64,1280]{2,1,0:T(8,128)(2,1)} %broadcast_in_dim.16), calls=%async_computation | async-start | bytes 2621440 | tf_op jit(solution)/shard_map/weights_spread/all_to_all | solution.py:44
  35.2 8.0 %copy-start.4 = (s32[64]{0:T(128)S(1)}, s32[64]{0:T(128)}, u32[]{:S(2)}) copy-start(s32[64]{0:T(128)} %param.10) | copy-start | bytes 772
  35.2 34.1 %all-to-all-start.1 = ((bf16[64,2,4224]{2,1,0:T(2,128)(2,1)}), bf16[64,2,4224]{2,1,0:T(2,128)(2,1)S(1)}, u32[]{:S(2)}, u32[]{:S(2)}) async-start(bf16[64,2,4224]{2,1,0:T(2,128)(2,1)} %all_to_all.21), calls=%async_computation.1 | async-start | bytes 2162688 | tf_op jit(solution)/shard_map/dispatch/all_to_all | solution.py:333
  43.2 39.4 %collective-permute-start = (bf16[512,1280]{1,0:T(8,128)(2,1)S(1)}, bf16[512,1280]{1,0:T(8,128)(2,1)}, u32[]{:S(2)}, u32[]{:S(2)}) collective-permute-start(bf16[512,1280]{1,0:T(8,128)(2,1)S(1)} %bitcast.11), channel_id=1, source_target_pairs={{0,448},{1,57},{8,456},{9,1},{16,464},{17,9},{24,472},{25,17},{32,... | collective-permute-start | bytes 3932168 | tf_op jit(solution)/shard_map/dispatch/ppermute | solution.py:55
  47.3 36.5 %collective-permute-start.1 = (bf16[512,1280]{1,0:T(8,128)(2,1)S(1)}, bf16[512,1280]{1,0:T(8,128)(2,1)}, u32[]{:S(2)}, u32[]{:S(2)}) collective-permute-start(bf16[512,1280]{1,0:T(8,128)(2,1)S(1)} %bitcast.12), channel_id=1, source_target_pairs={{0,64},{1,9},{8,72},{9,17},{16,80},{17,25},{24,88},{25,33},{32,96}... | collective-permute-start | bytes 3932168 | tf_op jit(solution)/shard_map/dispatch/ppermute | solution.py:55
  69.8 0.7 copy-start.2
  72.5 30.2 %all-to-all-start.2 = ((bf16[4,64,4224]{2,1,0:T(8,128)(2,1)}), bf16[4,64,4224]{2,1,0:T(8,128)(2,1)S(1)}, u32[]{:S(2)}, u32[]{:S(2)}) async-start(bf16[4,64,4224]{2,1,0:T(8,128)(2,1)} %broadcast_in_dim.21), calls=%async_computation.2 | async-start | bytes 4325376 | tf_op jit(solution)/shard_map/pack_rows/all_to_all | solution.py:33
  83.8 19.0 %collective-permute-start.2 = (bf16[512,1280]{1,0:T(8,128)(2,1)}, bf16[512,1280]{1,0:T(8,128)(2,1)}, u32[]{:S(2)}, u32[]{:S(2)}) collective-permute-start(bf16[512,1280]{1,0:T(8,128)(2,1)} %collective-permute-done.rest_1_), channel_id=1, source_target_pairs={{0,448},{1,57},{8,456},{9,1},{16,464},{17,9},{24,472},{25,17},{32,... | collective-permute-start | bytes 3932168 | tf_op jit(solution)/shard_map/pack_rows/ppermute | solution.py:55
  86.9 26.7 %collective-permute-start.5 = (bf16[512,1280]{1,0:T(8,128)(2,1)}, bf16[512,1280]{1,0:T(8,128)(2,1)}, u32[]{:S(2)}, u32[]{:S(2)}) collective-permute-start(bf16[512,1280]{1,0:T(8,128)(2,1)} %collective-permute-done.1.rest_2_), channel_id=1, source_target_pairs={{0,64},{1,9},{8,72},{9,17},{16,80},{17,25},{24,88},{25,33},{32,96}... | collective-permute-start | bytes 3932168 | tf_op jit(solution)/shard_map/pack_rows/ppermute | solution.py:55
  104.9 30.3 %collective-permute-start.3 = (bf16[256,4224]{1,0:T(8,128)(2,1)}, bf16[256,4224]{1,0:T(8,128)(2,1)}, u32[]{:S(2)}, u32[]{:S(2)}) collective-permute-start(bf16[256,4224]{1,0:T(8,128)(2,1)} %turn_rows.3), channel_id=1, source_target_pairs={{0,1},{1,0},{2,3},{3,2},{4,5},{5,4},{6,7},{7,6},{8,9},{9,8},{10,11... | collective-permute-start | bytes 6488072 | tf_op jit(solution)/shard_map/pack_rows/ppermute | solution.py:27
  110.3 19.0 %collective-permute-start.4 = (bf16[512,1280]{1,0:T(8,128)(2,1)}, bf16[512,1280]{1,0:T(8,128)(2,1)}, u32[]{:S(2)}, u32[]{:S(2)}) collective-permute-start(bf16[512,1280]{1,0:T(8,128)(2,1)} %collective-permute-done.2.rest_3_), channel_id=1, source_target_pairs={{0,448},{1,57},{8,456},{9,1},{16,464},{17,9},{24,472},{25,17},{32,... | collective-permute-start | bytes 3932168 | tf_op jit(solution)/shard_map/pack_rows/ppermute | solution.py:55
  113.6 21.6 %collective-permute-start.6 = (bf16[512,1280]{1,0:T(8,128)(2,1)}, bf16[512,1280]{1,0:T(8,128)(2,1)}, u32[]{:S(2)}, u32[]{:S(2)}) collective-permute-start(bf16[512,1280]{1,0:T(8,128)(2,1)} %collective-permute-done.5.rest_4_), channel_id=1, source_target_pairs={{0,64},{1,9},{8,72},{9,17},{16,80},{17,25},{24,88},{25,33},{32,96}... | collective-permute-start | bytes 3932168 | tf_op jit(solution)/shard_map/pack_rows/ppermute | solution.py:55
  129.2 19.4 %collective-permute-start.7 = (bf16[512,1280]{1,0:T(8,128)(2,1)}, bf16[512,1280]{1,0:T(8,128)(2,1)}, u32[]{:S(2)}, u32[]{:S(2)}) collective-permute-start(bf16[512,1280]{1,0:T(8,128)(2,1)} %collective-permute-done.4.rest_0_), channel_id=1, source_target_pairs={{0,448},{1,57},{8,456},{9,1},{16,464},{17,9},{24,472},{25,17},{32,... | collective-permute-start | bytes 3932168 | tf_op jit(solution)/shard_map/pack_rows/ppermute | solution.py:55
  141.7 6.9 %copy-start = (s32[512,1]{1,0:T(8,128)S(1)}, s32[512,1]{1,0:T(8,128)}, u32[]{:S(2)}) copy-start(s32[512,1]{1,0:T(8,128)} %add.98.place_column) | copy-start | bytes 6148
  155.8 8.0 %collective-permute-start.8 = (bf16[256,4096]{1,0:T(8,128)(2,1)S(1)}, bf16[256,4096]{1,0:T(8,128)(2,1)S(1)}, u32[]{:S(2)}, u32[]{:S(2)}) collective-permute-start(bf16[256,4096]{1,0:T(8,128)(2,1)S(1)} %output_product.3), channel_id=1, source_target_pairs={{0,1},{1,0},{2,3},{3,2},{4,5},{5,4},{6,7},{7,6},{8,9},{9,8},{10,11... | collective-permute-start | bytes 6291464 | tf_op jit(solution)/shard_map/output/ppermute | solution.py:27

commit v5 on v4

--- a/solution.py
+++ b/solution.py
@@ -137,27 +137,39 @@
 
 
 def project_kernel(steps, ring_at, near, far, *rest):
-    blocks, total, out_rows = rest[: len(steps)], rest[-2], rest[-1]
+    first = len(rest) == len(steps) + 2
+    blocks = rest[: len(steps)]
+    if first:
+        total, out_rows = rest[len(steps) :]
+    else:
+        so_far, total, out_rows, last_rows = rest[len(steps) :]
+        total[...] = so_far[...]
+        half, span = near.shape[0], SIDE * ROWS
+        place = lax.rem(ring_at[0] + SIDE // 2, SIDE) * span
+        chunk = pl.ds(pl.multiple_of(place, span), span)
+        last_rows[:half, :] = near[:, chunk]
+        last_rows[half:, :] = far[:, chunk]
     projection = total.shape[1]
-    first = len(rest) == len(steps) + 2
     collect(blocks, out_rows, projection)
-    if not first:
-        total[...] = rest[-3][...]
     add_products(ring_at, near, far, total, blocks, steps, projection, first)
 
 
 def project(ring_at, near, far, blocks, steps, projection, so_far=None):
     rows, depth = 2 * near.shape[0], sum(block.shape[0] for block in blocks)
     columns = blocks[0].shape[1]
-    operands = (ring_at, near, far, *blocks) + (() if so_far is None else (so_far,))
+    operands = (ring_at, near, far, *blocks)
+    results = [
+        jax.ShapeDtypeStruct((rows, projection), jnp.float32),
+        jax.ShapeDtypeStruct((depth, columns - projection), jnp.bfloat16),
+    ]
+    if so_far is not None:
+        operands += (so_far,)
+        results.append(jax.ShapeDtypeStruct((rows, SIDE * ROWS), jnp.bfloat16))
     return pl.pallas_call(
         functools.partial(project_kernel, steps),
-        out_shape=[
-            jax.ShapeDtypeStruct((rows, projection), jnp.float32),
-            jax.ShapeDtypeStruct((depth, columns - projection), jnp.bfloat16),
-        ],
+        out_shape=results,
         in_specs=[SCALAR] + [HERE] * (len(operands) - 1),
-        out_specs=[HERE, HERE],
+        out_specs=[HERE] * len(results),
         compiler_params=PARAMS,
         cost_estimate=pl.CostEstimate(
             flops=2 * rows * depth * projection,
@@ -169,17 +181,16 @@
 
 
 def attention_kernel(
-    steps, ring_at, near, far, doc_column, doc_row, place_column, place_row, so_far, *rest
+    rows, doc_column, doc_row, place_column, place_row, so_far, block, attended, held
 ):
-    blocks, (attended, out_rows, total, held) = rest[: len(steps)], rest[len(steps) :]
-    half = near.shape[0]
-    projection = held.shape[1]
+    half = rows.shape[0] // 2
     group = attended.shape[1] // HEAD_DIM
     halves = [slice(0, half), slice(half, 2 * half)]
-    collect(blocks, out_rows, projection)
-    total[...] = so_far[...]
-    add_products(ring_at, near, far, total, blocks, steps, projection, False)
-    held[...] = total[...].astype(jnp.bfloat16)
+    for here in halves:
+        term = jnp.dot(
+            rows[here, :], block[...], preferred_element_type=jnp.float32
+        )
+        held[here, :] = (so_far[here, :] + term).astype(jnp.bfloat16)
     key_at = group * HEAD_DIM
     keys = held[:, key_at : key_at + HEAD_DIM]
     values = held[:, key_at + HEAD_DIM : key_at + 2 * HEAD_DIM]
@@ -200,31 +211,24 @@
             attended[here, lanes] = (mixed * share).astype(jnp.bfloat16)
 
 
-def attention(ring_at, near, far, docs, places, so_far, blocks, steps, head_columns):
+def attention(last_rows, docs, places, so_far, block, head_columns):
     rows, projection = so_far.shape
-    depth = sum(block.shape[0] for block in blocks)
-    columns = blocks[0].shape[1]
+    depth = block.shape[0]
     masks = (docs[:, None], docs[None, :], places[:, None], places[None, :])
     return pl.pallas_call(
-        functools.partial(attention_kernel, steps),
-        out_shape=[
-            jax.ShapeDtypeStruct((rows, head_columns), jnp.bfloat16),
-            jax.ShapeDtypeStruct((depth, columns - projection), jnp.bfloat16),
-        ],
-        in_specs=[SCALAR] + [HERE] * (7 + len(blocks)),
-        out_specs=[HERE, HERE],
-        scratch_shapes=[
-            pltpu.VMEM((rows, projection), jnp.float32),
-            pltpu.VMEM((rows, projection), jnp.bfloat16),
-        ],
+        attention_kernel,
+        out_shape=jax.ShapeDtypeStruct((rows, head_columns), jnp.bfloat16),
+        in_specs=[HERE] * 7,
+        out_specs=HERE,
+        scratch_shapes=[pltpu.VMEM((rows, projection), jnp.bfloat16)],
         compiler_params=PARAMS,
         cost_estimate=pl.CostEstimate(
             flops=2 * rows * depth * projection + 4 * rows * rows * head_columns,
-            bytes_accessed=2 * depth * columns + 8 * rows * projection,
+            bytes_accessed=2 * depth * projection + 8 * rows * projection,
             transcendentals=rows * rows * head_columns // HEAD_DIM,
         ),
         name="attention",
-    )(ring_at, near, far, *masks, so_far, *blocks)
+    )(last_rows, *masks, so_far, block)
 
 
 def output_kernel(first, turned, steps, ring_at, attended, *rest):
@@ -347,9 +351,7 @@
         line_3 = ring_step(line_2)
         near = spread(labelled, "x").reshape(x_count * row_count, -1)
         near, _ = lax.optimization_barrier((near, line_2[0]))
-        far = shift(turn_rows(near, jnp.ones((1,), jnp.int32)), "core", 1)
-        line_4 = (across(line_3[0], -1),)
-        far, _ = lax.optimization_barrier((far, line_3))
+        far = turn_rows(shift(near, "core", 1), jnp.ones((1,), jnp.int32))
         docs = jnp.concatenate([near[:, width], far[:, width]]).astype(jnp.int32)
         even = 2 * jnp.arange(x_count, dtype=jnp.int32)
         block_of = jnp.concatenate([even + core_index, even + 1 - core_index])
@@ -358,10 +360,13 @@
     with jax.named_scope("attention"):
         early, early_steps = [line, *line_1, *line_2], (0, 1, 7, 2, 6)
         so_far, pieces = project(ring_at, near, far, early, early_steps, projection)
-        so_far, pieces_3 = project(ring_at, near, far, line_3, (3, 5), projection, so_far)
-        attended, pieces_4 = attention(
-            ring_at, near, far, docs, places, so_far, line_4, (4,), w_query.shape[1]
+        line_3, _ = lax.optimization_barrier((line_3, so_far))
+        block_4 = across(line_3[0][:, :projection], -1)
+        pieces_4 = across(line_3[1][:, projection:], 1)
+        so_far, pieces_3, last_rows = project(
+            ring_at, near, far, line_3, (3, 5), projection, so_far
         )
+        attended = attention(last_rows, docs, places, so_far, block_4, w_query.shape[1])
 
     with jax.named_scope("output"):
         half = x_count * row_count

time: 196 us -> 193 us (0.985)
  waiting for transfers between devices: 80.5 us -> 70.8 us
  local copies, waits for them, and re-layouts: 6.67 us -> 14.8 us
  Pallas kernels: 21.2 us -> 19 us
    ppermute x7 -> x8, waiting for transfers between devices: 37.9 us -> 28.1 us  [across(): return lax.ppermute(array, PLANE, pairs)]
    unnamed x10 -> x20, local copies, waits for them, and re-layouts: 0.15 us -> 5.85 us
    slice x0 -> x2, local copies, waits for them, and re-layouts: none -> 3.14 us  [the longest x1 2.06 us: on_device(): block_4 = across(line_3[0][:, :projection], -1)]
    pallas_call x3, Pallas kernels: 14.2 us -> 11.8 us  [the longest x2 8.5 us: project(): pl.pallas_call(functools.partial(project_kernel, steps), out_shape=result...]
    ppermute x7 -> x8, starting transfers between devices: 21.3 us -> 22.1 us  [across(): return lax.ppermute(array, PLANE, pairs)]
  transfers between devices with their start and end apart: 12 -> 13, of which waited for: 8 -> 8; matrix products, arithmetic and copies ran while one was open for 3% -> 3% of each run, Pallas kernels for 7% -> 8%
where the time goes in v5:
time: 193 us; the launch traced here: 192 us
  waiting for transfers between devices  70.8 us (37%)
  starting transfers between devices  54.5 us (28%)
  blocking collectives  29.3 us (15%)
  Pallas kernels  19 us (10%)
  local copies, waits for them, and re-layouts  14.8 us (8%)
  other arithmetic  2.42 us (1%)
    all_to_all x1, blocking collectives, on_device(): parts = lax.all_to_all(both, 'x', split_axis=0, concat_axis=0, tiled=True)  29.3 us
    ppermute x8, waiting for transfers between devices, across(): return lax.ppermute(array, PLANE, pairs)  28.1 us
    ppermute x8, starting transfers between devices, across(): return lax.ppermute(array, PLANE, pairs)  22.1 us
    all_to_all x1, waiting for transfers between devices, spread_lines(): lax.all_to_all(copies, PLANE, split_axis=0, concat_axis=0, axis_index_gro...  20.1 us
    all_to_all x1, waiting for transfers between devices, on_device(): lax.all_to_all(outgoing, ('z', 'y'), split_axis=0, concat_axis=0, tiled=T...  20.1 us
    all_to_all x1, starting transfers between devices, spread_lines(): lax.all_to_all(copies, PLANE, split_axis=0, concat_axis=0, axis_index_gro...  11 us
    ppermute x2, starting transfers between devices, shift(): lax.ppermute(array, axis, [(i, (i + step) % size) for i in range(size)])  9.48 us
    pallas_call x2, Pallas kernels, project(): pl.pallas_call(functools.partial(project_kernel, steps), out_shape=result...  8.5 us
  transfers between devices with their start and end apart: 13, of which 8 were waited for; matrix products, arithmetic and copies ran while one was open for 3% of the time, Pallas kernels for 8%

profile of v5, /device:TPU:1, one launch (start us, length us, event | category | flops | bytes accessed | tf_op | source)
XLA Modules:
  0.0 192.1 jit_solution(7530685493463089918)
XLA Ops:
  2.1 11.0 %all-to-all-start = ((bf16[8,64,1280]{2,1,0:T(8,128)(2,1)}), bf16[8,64,1280]{2,1,0:T(8,128)(2,1)S(1)}, u32[]{:S(2)}, u32[]{:S(2)}) async-start(bf16[8,64,1280]{2,1,0:T(8,128)(2,1)} %broadcast_in_dim.16), calls=%async_computation | async-start | bytes 2621440 | tf_op jit(solution)/shard_map/weights_spread/all_to_all | solution.py:44
  13.8 20.1 %all-to-all-done = bf16[8,64,1280]{2,1,0:T(8,128)(2,1)S(1)} async-done(((bf16[8,64,1280]{2,1,0:T(8,128)(2,1)}), bf16[8,64,1280]{2,1,0:T(8,128)(2,1)S(1)}, u32[]{:S(2)}, u32[]{:S(2)}) %all-to-all-start) | async-done | bytes 1310752 | tf_op jit(solution)/shard_map/weights_spread/all_to_all | solution.py:44
  35.2 8.0 %all-to-all-start.1 = ((bf16[64,2,4224]{2,1,0:T(2,128)(2,1)}), bf16[64,2,4224]{2,1,0:T(2,128)(2,1)S(1)}, u32[]{:S(2)}, u32[]{:S(2)}) async-start(bf16[64,2,4224]{2,1,0:T(2,128)(2,1)} %all_to_all.21), calls=%async_computation.1 | async-start | bytes 2162688 | tf_op jit(solution)/shard_map/dispatch/all_to_all | solution.py:337
  43.2 4.1 %collective-permute-start = (bf16[512,1280]{1,0:T(8,128)(2,1)S(1)}, bf16[512,1280]{1,0:T(8,128)(2,1)}, u32[]{:S(2)}, u32[]{:S(2)}) collective-permute-start(bf16[512,1280]{1,0:T(8,128)(2,1)S(1)} %bitcast.10), channel_id=1, source_target_pairs={{0,448},{1,57},{8,456},{9,1},{16,464},{17,9},{24,472},{25,17},{32,... | collective-permute-start | bytes 3932168 | tf_op jit(solution)/shard_map/dispatch/ppermute | solution.py:55
  47.3 1.9 %collective-permute-start.1 = (bf16[512,1280]{1,0:T(8,128)(2,1)S(1)}, bf16[512,1280]{1,0:T(8,128)(2,1)}, u32[]{:S(2)}, u32[]{:S(2)}) collective-permute-start(bf16[512,1280]{1,0:T(8,128)(2,1)S(1)} %bitcast.11), channel_id=1, source_target_pairs={{0,64},{1,9},{8,72},{9,17},{16,80},{17,25},{24,88},{25,33},{32,96}... | collective-permute-start | bytes 3932168 | tf_op jit(solution)/shard_map/dispatch/ppermute | solution.py:55
  49.3 20.1 %all-to-all-done.1 = bf16[64,2,4224]{2,1,0:T(2,128)(2,1)S(1)} async-done(((bf16[64,2,4224]{2,1,0:T(2,128)(2,1)}), bf16[64,2,4224]{2,1,0:T(2,128)(2,1)S(1)}, u32[]{:S(2)}, u32[]{:S(2)}) %all-to-all-start.1) | async-done | bytes 1081376 | tf_op jit(solution)/shard_map/dispatch/all_to_all | solution.py:337
  71.0 1.5 broadcast_in_dim.21
  72.5 4.0 %all-to-all-start.2 = ((bf16[4,64,4224]{2,1,0:T(8,128)(2,1)}), bf16[4,64,4224]{2,1,0:T(8,128)(2,1)S(1)}, u32[]{:S(2)}, u32[]{:S(2)}) async-start(bf16[4,64,4224]{2,1,0:T(8,128)(2,1)} %broadcast_in_dim.21), calls=%async_computation.2 | async-start | bytes 4325376 | tf_op jit(solution)/shard_map/pack_rows/all_to_all | solution.py:33
  76.5 6.0 %collective-permute-done.rest_1_ = bf16[512,1280]{1,0:T(8,128)(2,1)} collective-permute-done((bf16[512,1280]{1,0:T(8,128)(2,1)S(1)}, bf16[512,1280]{1,0:T(8,128)(2,1)}, u32[]{:S(2)}, u32[]{:S(2)}) %collective-permute-start) | collective-permute-done | bytes 1310752 | tf_op jit(solution)/shard_map/dispatch/ppermute | solution.py:55
  83.8 3.1 %collective-permute-start.2 = (bf16[512,1280]{1,0:T(8,128)(2,1)}, bf16[512,1280]{1,0:T(8,128)(2,1)}, u32[]{:S(2)}, u32[]{:S(2)}) collective-permute-start(bf16[512,1280]{1,0:T(8,128)(2,1)} %collective-permute-done.rest_1_), channel_id=1, source_target_pairs={{0,448},{1,57},{8,456},{9,1},{16,464},{17,9},{24,472},{25,17},{32,... | collective-permute-start | bytes 3932168 | tf_op jit(solution)/shard_map/pack_rows/ppermute | solution.py:55
  86.9 2.2 %collective-permute-start.5 = (bf16[512,1280]{1,0:T(8,128)(2,1)}, bf16[512,1280]{1,0:T(8,128)(2,1)}, u32[]{:S(2)}, u32[]{:S(2)}) collective-permute-start(bf16[512,1280]{1,0:T(8,128)(2,1)} %collective-permute-done.1.rest_2_), channel_id=1, source_target_pairs={{0,64},{1,9},{8,72},{9,17},{16,80},{17,25},{24,88},{25,33},{32,96}... | collective-permute-start | bytes 3932168 | tf_op jit(solution)/shard_map/pack_rows/ppermute | solution.py:55
  89.1 13.7 %collective-permute-done.2.rest_3_ = bf16[512,1280]{1,0:T(8,128)(2,1)} collective-permute-done((bf16[512,1280]{1,0:T(8,128)(2,1)}, bf16[512,1280]{1,0:T(8,128)(2,1)}, u32[]{:S(2)}, u32[]{:S(2)}) %collective-permute-start.2) | collective-permute-done | bytes 1310752 | tf_op jit(solution)/shard_map/pack_rows/ppermute | solution.py:55
  102.8 5.3 %collective-permute-start.3 = (bf16[256,4224]{1,0:T(8,128)(2,1)S(1)}, bf16[256,4224]{1,0:T(8,128)(2,1)}, u32[]{:S(2)}, u32[]{:S(2)}) collective-permute-start(bf16[256,4224]{1,0:T(8,128)(2,1)S(1)} %bitcast.6), channel_id=1, source_target_pairs={{0,1},{1,0},{2,3},{3,2},{4,5},{5,4},{6,7},{7,6},{8,9},{9,8},{10,11... | collective-permute-start | bytes 6488072 | tf_op jit(solution)/shard_map/pack_rows/ppermute | solution.py:27
  108.1 3.3 %collective-permute-start.4 = (bf16[512,1280]{1,0:T(8,128)(2,1)}, bf16[512,1280]{1,0:T(8,128)(2,1)}, u32[]{:S(2)}, u32[]{:S(2)}) collective-permute-start(bf16[512,1280]{1,0:T(8,128)(2,1)} %collective-permute-done.2.rest_3_), channel_id=1, source_target_pairs={{0,448},{1,57},{8,456},{9,1},{16,464},{17,9},{24,472},{25,17},{32,... | collective-permute-start | bytes 3932168 | tf_op jit(solution)/shard_map/pack_rows/ppermute | solution.py:55
  111.4 2.0 %collective-permute-start.6 = (bf16[512,1280]{1,0:T(8,128)(2,1)}, bf16[512,1280]{1,0:T(8,128)(2,1)}, u32[]{:S(2)}, u32[]{:S(2)}) collective-permute-start(bf16[512,1280]{1,0:T(8,128)(2,1)} %collective-permute-done.5.rest_4_), channel_id=1, source_target_pairs={{0,64},{1,9},{8,72},{9,17},{16,80},{17,25},{24,88},{25,33},{32,96}... | collective-permute-start | bytes 3932168 | tf_op jit(solution)/shard_map/pack_rows/ppermute | solution.py:55
  113.5 2.5 %turn_rows.3.far = bf16[256,4224]{1,0:T(8,128)(2,1)S(1)} custom-call(s32[1]{0:T(128)} %constant.60.clone.1.turned, bf16[256,4224]{1,0:T(8,128)(2,1)} %collective-permute-done.3.rows), custom_call_target="tpu_custom_call" | custom-call | tf_op jit(solution)/shard_map/pack_rows/turn_rows/pallas_call | solution.py:105
  116.0 5.7 %project.2 = (f32[512,768]{1,0:T(8,128)S(1)}, bf16[2560,512]{1,0:T(8,128)(2,1)S(1)}) custom-call(s32[1]{0:T(128)} %bitcast.1.ring_at, bf16[256,4224]{1,0:T(8,128)(2,1)S(1)} %bitcast.7, bf16[256,4224]{1,0:T(8,128)(2,1)S(1)} %turn_rows.3.far, bf16[512,1280]{1,0:T(8,128)(2,1)S(1)} %bitcast.12, bf16[512,1280]{1,0:T(8,128)(2,1)} %collective-permute-done.rest_1_, ...), custom_call_target="tpu_custom_call" | custom-call | flops 2013265920 | bytes 9175040 | tf_op jit(solution)/shard_map/attention/project/pallas_call | solution.py:168
  121.7 1.5 copy-done.2
  124.4 2.7 %collective-permute-done.4.rest_0_ = bf16[512,1280]{1,0:T(8,128)(2,1)} collective-permute-done((bf16[512,1280]{1,0:T(8,128)(2,1)}, bf16[512,1280]{1,0:T(8,128)(2,1)}, u32[]{:S(2)}, u32[]{:S(2)}) %collective-permute-start.4) | collective-permute-done | bytes 1310752 | tf_op jit(solution)/shard_map/pack_rows/ppermute | solution.py:55
  127.0 4.6 %collective-permute-done.6.rest_1_ = bf16[512,1280]{1,0:T(8,128)(2,1)} collective-permute-done((bf16[512,1280]{1,0:T(8,128)(2,1)}, bf16[512,1280]{1,0:T(8,128)(2,1)}, u32[]{:S(2)}, u32[]{:S(2)}) %collective-permute-start.6) | collective-permute-done | bytes 1310752 | tf_op jit(solution)/shard_map/pack_rows/ppermute | solution.py:55
  131.6 2.1 %slice.22 = bf16[512,768]{1,0:T(8,128)(2,1)} slice(bf16[512,1280]{1,0:T(8,128)(2,1)} %collective-permute-done.4.rest_0_), slice={[0:512], [0:768]} | slice | bytes 1572864 | tf_op jit(solution)/shard_map/attention/slice | solution.py:364
  133.6 1.9 collective-permute-start.7
  137.1 3.5 %collective-permute-start.8 = (bf16[512,512]{1,0:T(8,128)(2,1)S(1)}, bf16[512,512]{1,0:T(8,128)(2,1)S(1)}, u32[]{:S(2)}, u32[]{:S(2)}) collective-permute-start(bf16[512,512]{1,0:T(8,128)(2,1)S(1)} %slice.23), channel_id=1, source_target_pairs={{0,64},{1,9},{8,72},{9,17},{16,80},{17,25},{24,88},{25,33},{32,96}... | collective-permute-start | bytes 1572872 | tf_op jit(solution)/shard_map/attention/ppermute | solution.py:55
  141.7 1.6 copy-done.1
  143.3 1.4 copy-done.5
  144.7 2.8 %project.3 = (f32[512,768]{1,0:T(8,128)S(1)}, bf16[1024,512]{1,0:T(8,128)(2,1)S(1)}, bf16[512,512]{1,0:T(8,128)(2,1)S(1)}) custom-call(s32[1]{0:T(128)} %bitcast.1.ring_at, bf16[256,4224]{1,0:T(8,128)(2,1)S(1)} %bitcast.9, bf16[256,4224]{1,0:T(8,128)(2,1)S(1)} %copy-done.1, bf16[512,1280]{1,0:T(8,128)(2,1)} %collective-permute-done.4.rest_0_, ...), custom_call_target="tpu_custom_call" | custom-call | flops 805306368 | bytes 3670016 | tf_op jit(solution)/shard_map/attention/project/pallas_call | solution.py:168
  147.6 3.3 %attention.1.attended = bf16[512,512]{1,0:T(8,128)(2,1)S(1)} custom-call(bf16[512,512]{1,0:T(8,128)(2,1)S(1)} %get-tuple-element.25.rows, s32[512,1]{1,0:T(8,128)S(1)} %maximum_convert_fusion.doc_column, s32[1,512]{1,0:T(1,128)S(1)} %maximum_convert_fusion.1.doc_row, s32[512,1]{1,0:T(8,128)S(1)} %add.98.place_column, s32[1,512]{1,0:T(1,128)S(1)} %add.96.place_row, ...), custom_call_target="tpu_custom_call" | custom-call | flops 939524096 | bytes 3932160 | tf_op jit(solution)/shard_map/attention/attention/pallas_call | solution.py:218
  150.9 2.0 %output_product.3 = bf16[256,4096]{1,0:T(8,128)(2,1)S(1)} custom-call(s32[1]{0:T(128)} %bitcast.1.ring_at, bf16[512,512]{1,0:T(8,128)(2,1)S(1)} %attention.1.attended, bf16[2560,512]{1,0:T(8,128)(2,1)S(1)} %copy-done.3, bf16[1024,512]{1,0:T(8,128)(2,1)S(1)} %get-tuple-element.28.rest_1_, bf16[512,512]{1,0:T(8,128)(2,1)S(1)} %collective-permute-done.8.rest_2_), custom_call_target="tpu_custom_call" | custom-call | flops 1073741824 | bytes 6291456 | tf_op jit(solution)/shard_map/output/output_product/pallas_call | solution.py:258
  152.9 4.2 %collective-permute-start.9 = (bf16[256,4096]{1,0:T(8,128)(2,1)S(1)}, bf16[256,4096]{1,0:T(8,128)(2,1)S(1)}, u32[]{:S(2)}, u32[]{:S(2)}) collective-permute-start(bf16[256,4096]{1,0:T(8,128)(2,1)S(1)} %output_product.3), channel_id=1, source_target_pairs={{0,1},{1,0},{2,3},{3,2},{4,5},{5,4},{6,7},{7,6},{8,9},{9,8},{10,11... | collective-permute-start | bytes 6291464 | tf_op jit(solution)/shard_map/output/ppermute | solution.py:27
  157.1 1.3 output_product.2
  158.4 2.4 %collective-permute-done.9 = bf16[256,4096]{1,0:T(8,128)(2,1)S(1)} collective-permute-done((bf16[256,4096]{1,0:T(8,128)(2,1)S(1)}, bf16[256,4096]{1,0:T(8,128)(2,1)S(1)}, u32[]{:S(2)}, u32[]{:S(2)}) %collective-permute-start.9) | collective-permute-done | bytes 2097184 | tf_op jit(solution)/shard_map/output/ppermute | solution.py:27
  161.6 29.3 %all_to_all.31.parts = bf16[4,64,4096]{2,1,0:T(8,128)(2,1)S(1)} all-to-all(bf16[4,64,4096]{2,1,0:T(8,128)(2,1)S(1)} %bitcast.13), channel_id=1, replica_groups=mesh['z'=8,'y'=8,'x'=4,'core'=2] {'x'}, dimensions={0} | all-to-all | bytes 4194304 | tf_op jit(solution)/shard_map/output/all_to_all | solution.py:379
  (55 shorter events, 12.7 us)
Async XLA Ops:
  2.1 11.0 %copy-start.8 = (s32[64]{0:T(128)S(1)}, s32[64]{0:T(128)}, u32[]{:S(2)}) copy-start(s32[64]{0:T(128)} %param.9) | copy-start | bytes 772
  2.1 11.3 %copy-start.6 = (bf16[64,4096]{1,0:T(8,128)(2,1)S(1)}, bf16[64,4096]{1,0:T(8,128)(2,1)}, u32[]{:S(2)}) copy-start(bf16[64,4096]{1,0:T(8,128)(2,1)} %param.8) | copy-start | bytes 1572868
  2.1 31.9 %all-to-all-start = ((bf16[8,64,1280]{2,1,0:T(8,128)(2,1)}), bf16[8,64,1280]{2,1,0:T(8,128)(2,1)S(1)}, u32[]{:S(2)}, u32[]{:S(2)}) async-start(bf16[8,64,1280]{2,1,0:T(8,128)(2,1)} %broadcast_in_dim.16), calls=%async_computation | async-start | bytes 2621440 | tf_op jit(solution)/shard_map/weights_spread/all_to_all | solution.py:44
  35.2 8.0 %copy-start.9 = (s32[64]{0:T(128)S(1)}, s32[64]{0:T(128)}, u32[]{:S(2)}) copy-start(s32[64]{0:T(128)} %param.10) | copy-start | bytes 772
  35.2 34.1 %all-to-all-start.1 = ((bf16[64,2,4224]{2,1,0:T(2,128)(2,1)}), bf16[64,2,4224]{2,1,0:T(2,128)(2,1)S(1)}, u32[]{:S(2)}, u32[]{:S(2)}) async-start(bf16[64,2,4224]{2,1,0:T(2,128)(2,1)} %all_to_all.21), calls=%async_computation.1 | async-start | bytes 2162688 | tf_op jit(solution)/shard_map/dispatch/all_to_all | solution.py:337
  43.2 39.4 %collective-permute-start = (bf16[512,1280]{1,0:T(8,128)(2,1)S(1)}, bf16[512,1280]{1,0:T(8,128)(2,1)}, u32[]{:S(2)}, u32[]{:S(2)}) collective-permute-start(bf16[512,1280]{1,0:T(8,128)(2,1)S(1)} %bitcast.10), channel_id=1, source_target_pairs={{0,448},{1,57},{8,456},{9,1},{16,464},{17,9},{24,472},{25,17},{32,... | collective-permute-start | bytes 3932168 | tf_op jit(solution)/shard_map/dispatch/ppermute | solution.py:55
  47.3 36.5 %collective-permute-start.1 = (bf16[512,1280]{1,0:T(8,128)(2,1)S(1)}, bf16[512,1280]{1,0:T(8,128)(2,1)}, u32[]{:S(2)}, u32[]{:S(2)}) collective-permute-start(bf16[512,1280]{1,0:T(8,128)(2,1)S(1)} %bitcast.11), channel_id=1, source_target_pairs={{0,64},{1,9},{8,72},{9,17},{16,80},{17,25},{24,88},{25,33},{32,96}... | collective-permute-start | bytes 3932168 | tf_op jit(solution)/shard_map/dispatch/ppermute | solution.py:55
  69.8 0.7 copy-start.7
  72.5 30.2 %all-to-all-start.2 = ((bf16[4,64,4224]{2,1,0:T(8,128)(2,1)}), bf16[4,64,4224]{2,1,0:T(8,128)(2,1)S(1)}, u32[]{:S(2)}, u32[]{:S(2)}) async-start(bf16[4,64,4224]{2,1,0:T(8,128)(2,1)} %broadcast_in_dim.21), calls=%async_computation.2 | async-start | bytes 4325376 | tf_op jit(solution)/shard_map/pack_rows/all_to_all | solution.py:33
  83.8 19.0 %collective-permute-start.2 = (bf16[512,1280]{1,0:T(8,128)(2,1)}, bf16[512,1280]{1,0:T(8,128)(2,1)}, u32[]{:S(2)}, u32[]{:S(2)}) collective-permute-start(bf16[512,1280]{1,0:T(8,128)(2,1)} %collective-permute-done.rest_1_), channel_id=1, source_target_pairs={{0,448},{1,57},{8,456},{9,1},{16,464},{17,9},{24,472},{25,17},{32,... | collective-permute-start | bytes 3932168 | tf_op jit(solution)/shard_map/pack_rows/ppermute | solution.py:55
  86.9 24.5 %collective-permute-start.5 = (bf16[512,1280]{1,0:T(8,128)(2,1)}, bf16[512,1280]{1,0:T(8,128)(2,1)}, u32[]{:S(2)}, u32[]{:S(2)}) collective-permute-start(bf16[512,1280]{1,0:T(8,128)(2,1)} %collective-permute-done.1.rest_2_), channel_id=1, source_target_pairs={{0,64},{1,9},{8,72},{9,17},{16,80},{17,25},{24,88},{25,33},{32,96}... | collective-permute-start | bytes 3932168 | tf_op jit(solution)/shard_map/pack_rows/ppermute | solution.py:55
  102.8 10.7 %collective-permute-start.3 = (bf16[256,4224]{1,0:T(8,128)(2,1)S(1)}, bf16[256,4224]{1,0:T(8,128)(2,1)}, u32[]{:S(2)}, u32[]{:S(2)}) collective-permute-start(bf16[256,4224]{1,0:T(8,128)(2,1)S(1)} %bitcast.6), channel_id=1, source_target_pairs={{0,1},{1,0},{2,3},{3,2},{4,5},{5,4},{6,7},{7,6},{8,9},{9,8},{10,11... | collective-permute-start | bytes 6488072 | tf_op jit(solution)/shard_map/pack_rows/ppermute | solution.py:27
  108.1 19.0 %collective-permute-start.4 = (bf16[512,1280]{1,0:T(8,128)(2,1)}, bf16[512,1280]{1,0:T(8,128)(2,1)}, u32[]{:S(2)}, u32[]{:S(2)}) collective-permute-start(bf16[512,1280]{1,0:T(8,128)(2,1)} %collective-permute-done.2.rest_3_), channel_id=1, source_target_pairs={{0,448},{1,57},{8,456},{9,1},{16,464},{17,9},{24,472},{25,17},{32,... | collective-permute-start | bytes 3932168 | tf_op jit(solution)/shard_map/pack_rows/ppermute | solution.py:55
  111.4 20.2 %collective-permute-start.6 = (bf16[512,1280]{1,0:T(8,128)(2,1)}, bf16[512,1280]{1,0:T(8,128)(2,1)}, u32[]{:S(2)}, u32[]{:S(2)}) collective-permute-start(bf16[512,1280]{1,0:T(8,128)(2,1)} %collective-permute-done.5.rest_4_), channel_id=1, source_target_pairs={{0,64},{1,9},{8,72},{9,17},{16,80},{17,25},{24,88},{25,33},{32,96}... | collective-permute-start | bytes 3932168 | tf_op jit(solution)/shard_map/pack_rows/ppermute | solution.py:55
  116.0 5.7 %copy-start = (bf16[256,4224]{1,0:T(8,128)(2,1)}, bf16[256,4224]{1,0:T(8,128)(2,1)S(1)}, u32[]{:S(2)}) copy-start(bf16[256,4224]{1,0:T(8,128)(2,1)S(1)} %turn_rows.3.far) | copy-start | bytes 6488068
  121.7 1.5 copy-start.2
  123.2 1.2 copy-start.4
  133.6 13.9 %collective-permute-start.7 = (bf16[512,768]{1,0:T(8,128)(2,1)}, bf16[512,768]{1,0:T(8,128)(2,1)S(1)}, u32[]{:S(2)}, u32[]{:S(2)}) collective-permute-start(bf16[512,768]{1,0:T(8,128)(2,1)} %slice.22), channel_id=1, source_target_pairs={{0,448},{1,57},{8,456},{9,1},{16,464},{17,9},{24,472},{25,17},{32,... | collective-permute-start | bytes 2359304 | tf_op jit(solution)/shard_map/attention/ppermute | solution.py:55
  137.1 13.7 %collective-permute-start.8 = (bf16[512,512]{1,0:T(8,128)(2,1)S(1)}, bf16[512,512]{1,0:T(8,128)(2,1)S(1)}, u32[]{:S(2)}, u32[]{:S(2)}) collective-permute-start(bf16[512,512]{1,0:T(8,128)(2,1)S(1)} %slice.23), channel_id=1, source_target_pairs={{0,64},{1,9},{8,72},{9,17},{16,80},{17,25},{24,88},{25,33},{32,96}... | collective-permute-start | bytes 1572872 | tf_op jit(solution)/shard_map/attention/ppermute | solution.py:55
  141.6 1.6 copy-start.1
  143.3 1.4 copy-start.5
  147.6 3.3 %copy-start.3 = (bf16[2560,512]{1,0:T(8,128)(2,1)S(1)}, bf16[2560,512]{1,0:T(8,128)(2,1)}, u32[]{:S(2)}) copy-start(bf16[2560,512]{1,0:T(8,128)(2,1)} %copy-done.2) | copy-start | bytes 7864324
  152.9 7.9 %collective-permute-start.9 = (bf16[256,4096]{1,0:T(8,128)(2,1)S(1)}, bf16[256,4096]{1,0:T(8,128)(2,1)S(1)}, u32[]{:S(2)}, u32[]{:S(2)}) collective-permute-start(bf16[256,4096]{1,0:T(8,128)(2,1)S(1)} %output_product.3), channel_id=1, source_target_pairs={{0,1},{1,0},{2,3},{3,2},{4,5},{5,4},{6,7},{7,6},{8,9},{9,8},{10,11... | collective-permute-start | bytes 6291464 | tf_op jit(solution)/shard_map/output/ppermute | solution.py:27

commit v6 on v5

--- a/solution.py
+++ b/solution.py
@@ -180,58 +180,81 @@
     )(*operands)
 
 
-def attention_kernel(
-    rows, doc_column, doc_row, place_column, place_row, so_far, block, attended, held
-):
-    half = rows.shape[0] // 2
+def attend(held, first, doc_column, doc_row, place_column, place_row, attended):
+    rows = attended.shape[0]
+    here = slice(first, first + rows)
     group = attended.shape[1] // HEAD_DIM
-    halves = [slice(0, half), slice(half, 2 * half)]
-    for here in halves:
-        term = jnp.dot(
-            rows[here, :], block[...], preferred_element_type=jnp.float32
-        )
-        held[here, :] = (so_far[here, :] + term).astype(jnp.bfloat16)
     key_at = group * HEAD_DIM
     keys = held[:, key_at : key_at + HEAD_DIM]
     values = held[:, key_at + HEAD_DIM : key_at + 2 * HEAD_DIM]
     scale = HEAD_DIM**-0.5 * math.log2(math.e)
-    for here in halves:
-        same = doc_column[here, :] == doc_row[...]
-        allowed = same & (place_column[here, :] >= place_row[...])
-        hidden = jnp.where(allowed, 0.0, -1e30)
-        for head in range(group):
-            lanes = slice(head * HEAD_DIM, (head + 1) * HEAD_DIM)
-            scores = lax.dot_general(
-                held[here, lanes], keys, (((1,), (1,)), ((), ())), preferred_element_type=jnp.float32
-            )
-            scores = scores * scale + hidden
-            weight = jnp.exp2(scores - jnp.max(scores, axis=1, keepdims=True))
-            share = 1.0 / jnp.sum(weight, axis=1, keepdims=True)
-            mixed = jnp.dot(weight.astype(jnp.bfloat16), values, preferred_element_type=jnp.float32)
-            attended[here, lanes] = (mixed * share).astype(jnp.bfloat16)
-
-
-def attention(last_rows, docs, places, so_far, block, head_columns):
+    same = doc_column[here, :] == doc_row[...]
+    allowed = same & (place_column[here, :] >= place_row[...])
+    hidden = jnp.where(allowed, 0.0, -1e30)
+    for head in range(group):
+        lanes = slice(head * HEAD_DIM, (head + 1) * HEAD_DIM)
+        scores = lax.dot_general(
+            held[here, lanes], keys, (((1,), (1,)), ((), ())), preferred_element_type=jnp.float32
+        )
+        scores = scores * scale + hidden
+        weight = jnp.exp2(scores - jnp.max(scores, axis=1, keepdims=True))
+        share = 1.0 / jnp.sum(weight, axis=1, keepdims=True)
+        mixed = jnp.dot(weight.astype(jnp.bfloat16), values, preferred_element_type=jnp.float32)
+        attended[:, lanes] = (mixed * share).astype(jnp.bfloat16)
+
+
+def far_attention_kernel(rows, so_far, block, *rest):
+    masks, attended, held = rest[:4], rest[4], rest[5]
+    half = rows.shape[0] // 2
+    for here in (slice(0, half), slice(half, 2 * half)):
+        term = jnp.dot(rows[here, :], block[...], preferred_element_type=jnp.float32)
+        held[here, :] = (so_far[here, :] + term).astype(jnp.bfloat16)
+    attend(held, half, *masks, attended)
+
+
+def near_attention_kernel(held, *rest):
+    attend(held, 0, *rest)
+
+
+def far_attention(last_rows, so_far, block, masks, head_columns):
     rows, projection = so_far.shape
     depth = block.shape[0]
-    masks = (docs[:, None], docs[None, :], places[:, None], places[None, :])
-    return pl.pallas_call(
-        attention_kernel,
-        out_shape=jax.ShapeDtypeStruct((rows, head_columns), jnp.bfloat16),
+    return pl.pallas_call(
+        far_attention_kernel,
+        out_shape=[
+            jax.ShapeDtypeStruct((rows // 2, head_columns), jnp.bfloat16),
+            jax.ShapeDtypeStruct((rows, projection), jnp.bfloat16),
+        ],
         in_specs=[HERE] * 7,
+        out_specs=[HERE, HERE],
+        compiler_params=PARAMS,
+        cost_estimate=pl.CostEstimate(
+            flops=2 * rows * depth * projection + 2 * rows * rows * head_columns,
+            bytes_accessed=2 * depth * projection + 8 * rows * projection,
+            transcendentals=rows * rows * head_columns // HEAD_DIM // 2,
+        ),
+        name="far_attention",
+    )(last_rows, so_far, block, *masks)
+
+
+def near_attention(held, masks, head_columns):
+    rows = held.shape[0]
+    return pl.pallas_call(
+        near_attention_kernel,
+        out_shape=jax.ShapeDtypeStruct((rows // 2, head_columns), jnp.bfloat16),
+        in_specs=[HERE] * 5,
         out_specs=HERE,
-        scratch_shapes=[pltpu.VMEM((rows, projection), jnp.bfloat16)],
         compiler_params=PARAMS,
         cost_estimate=pl.CostEstimate(
-            flops=2 * rows * depth * projection + 4 * rows * rows * head_columns,
-            bytes_accessed=2 * depth * projection + 8 * rows * projection,
-            transcendentals=rows * rows * head_columns // HEAD_DIM,
+            flops=2 * rows * rows * head_columns,
+            bytes_accessed=2 * held.size,
+            transcendentals=rows * rows * head_columns // HEAD_DIM // 2,
         ),
-        name="attention",
-    )(last_rows, *masks, so_far, block)
-
-
-def output_kernel(first, turned, steps, ring_at, attended, *rest):
+        name="near_attention",
+    )(held, *masks)
+
+
+def output_kernel(turned, steps, ring_at, attended, *rest):
     pieces, out, held = rest[:-2], rest[-2], rest[-1]
     rows = out.shape[0]
     span = SIDE * ROWS
@@ -240,7 +263,7 @@
     for piece in pieces:
         for start in range(0, piece.shape[0], span):
             term = lax.dot_general(
-                attended[first : first + rows, :],
+                attended[...],
                 piece[start : start + span, :],
                 (((1,), (1,)), ((), ())),
                 preferred_element_type=jnp.float32,
@@ -252,11 +275,11 @@
         turn(lambda at: held[:, at : at + LANES], out, out.shape[1])
 
 
-def output_half(first, rows, turned, ring_at, attended, pieces, steps):
+def output_half(rows, turned, ring_at, attended, pieces, steps):
     columns = sum(piece.shape[0] for piece in pieces)
     held = pltpu.VMEM((rows, columns) if turned else (8, LANES), jnp.float32)
     return pl.pallas_call(
-        functools.partial(output_kernel, first, turned, steps),
+        functools.partial(output_kernel, turned, steps),
         out_shape=jax.ShapeDtypeStruct((rows, columns), jnp.bfloat16),
         in_specs=[SCALAR] + [HERE] * (1 + len(pieces)),
         out_specs=HERE,
@@ -366,15 +389,20 @@
         so_far, pieces_3, last_rows = project(
             ring_at, near, far, line_3, (3, 5), projection, so_far
         )
-        attended = attention(last_rows, docs, places, so_far, block_4, w_query.shape[1])
+        masks = (docs[:, None], docs[None, :], places[:, None], places[None, :])
+        attended_far, held = far_attention(
+            last_rows, so_far, block_4, masks, w_query.shape[1]
+        )
 
     with jax.named_scope("output"):
         half = x_count * row_count
         pieces = (pieces, pieces_3, pieces_4)
         steps = early_steps + (3, 5, 4)
-        theirs = output_half(half, half, True, ring_at, attended, pieces, steps)
+        theirs = output_half(half, True, ring_at, attended_far, pieces, steps)
+        theirs, held = lax.optimization_barrier((theirs, held))
         received = shift(theirs, "core", 1)
-        ours = output_half(0, half, False, ring_at, attended, pieces, steps)
+        attended_near = near_attention(held, masks, w_query.shape[1])
+        ours = output_half(half, False, ring_at, attended_near, pieces, steps)
         both = (ours.astype(jnp.float32) + received.astype(jnp.float32)).astype(jnp.bfloat16)
         parts = lax.all_to_all(both, "x", split_axis=0, concat_axis=0, tiled=True)
         return finish(parts.reshape(x_count, row_count, -1), turned)

time: 193 us -> 192 us (level)
    pallas_call x3 -> x4, Pallas kernels: 6.57 us -> 6.76 us  [the longest x2 3.3 us: output_half(): pl.pallas_call(functools.partial(output_kernel, turned, steps), out_shape...]
where the time goes in v6:
time: 192 us; the launch traced here: 191 us
  waiting for transfers between devices  70.5 us (37%)
  starting transfers between devices  54.5 us (28%)
  blocking collectives  29.3 us (15%)
  Pallas kernels  19.2 us (10%)
  local copies, waits for them, and re-layouts  13.6 us (7%)
  other arithmetic  2.42 us (1%)
    ppermute x8, waiting for transfers between devices, across(): return lax.ppermute(array, PLANE, pairs)  29.3 us
    all_to_all x1, blocking collectives, on_device(): parts = lax.all_to_all(both, 'x', split_axis=0, concat_axis=0, tiled=True)  29.3 us
    ppermute x8, starting transfers between devices, across(): return lax.ppermute(array, PLANE, pairs)  22.1 us
    all_to_all x1, waiting for transfers between devices, spread_lines(): lax.all_to_all(copies, PLANE, split_axis=0, concat_axis=0, axis_index_gro...  20.1 us
    all_to_all x1, waiting for transfers between devices, on_device(): lax.all_to_all(outgoing, ('z', 'y'), split_axis=0, concat_axis=0, tiled=T...  20.1 us
    all_to_all x1, starting transfers between devices, spread_lines(): lax.all_to_all(copies, PLANE, split_axis=0, concat_axis=0, axis_index_gro...  11 us
    ppermute x2, starting transfers between devices, shift(): lax.ppermute(array, axis, [(i, (i + step) % size) for i in range(size)])  9.49 us
    pallas_call x2, Pallas kernels, project(): pl.pallas_call(functools.partial(project_kernel, steps), out_shape=result...  8.5 us
  transfers between devices with their start and end apart: 13, of which 8 were waited for; matrix products, arithmetic and copies ran while one was open for 3% of the time, Pallas kernels for 8%

profile of v6, /device:TPU:1, one launch (start us, length us, event | category | flops | bytes accessed | tf_op | source)
XLA Modules:
  0.0 190.9 jit_solution(2825474681524152827)
XLA Ops:
  2.1 11.0 %all-to-all-start = ((bf16[8,64,1280]{2,1,0:T(8,128)(2,1)}), bf16[8,64,1280]{2,1,0:T(8,128)(2,1)S(1)}, u32[]{:S(2)}, u32[]{:S(2)}) async-start(bf16[8,64,1280]{2,1,0:T(8,128)(2,1)} %broadcast_in_dim.16), calls=%async_computation | async-start | bytes 2621440 | tf_op jit(solution)/shard_map/weights_spread/all_to_all | solution.py:44
  13.8 20.1 %all-to-all-done = bf16[8,64,1280]{2,1,0:T(8,128)(2,1)S(1)} async-done(((bf16[8,64,1280]{2,1,0:T(8,128)(2,1)}), bf16[8,64,1280]{2,1,0:T(8,128)(2,1)S(1)}, u32[]{:S(2)}, u32[]{:S(2)}) %all-to-all-start) | async-done | bytes 1310752 | tf_op jit(solution)/shard_map/weights_spread/all_to_all | solution.py:44
  35.2 8.0 %all-to-all-start.1 = ((bf16[64,2,4224]{2,1,0:T(2,128)(2,1)}), bf16[64,2,4224]{2,1,0:T(2,128)(2,1)S(1)}, u32[]{:S(2)}, u32[]{:S(2)}) async-start(bf16[64,2,4224]{2,1,0:T(2,128)(2,1)} %all_to_all.21), calls=%async_computation.1 | async-start | bytes 2162688 | tf_op jit(solution)/shard_map/dispatch/all_to_all | solution.py:360
  43.2 4.1 %collective-permute-start = (bf16[512,1280]{1,0:T(8,128)(2,1)S(1)}, bf16[512,1280]{1,0:T(8,128)(2,1)}, u32[]{:S(2)}, u32[]{:S(2)}) collective-permute-start(bf16[512,1280]{1,0:T(8,128)(2,1)S(1)} %bitcast.10), channel_id=1, source_target_pairs={{0,448},{1,57},{8,456},{9,1},{16,464},{17,9},{24,472},{25,17},{32,... | collective-permute-start | bytes 3932168 | tf_op jit(solution)/shard_map/dispatch/ppermute | solution.py:55
  47.3 1.9 %collective-permute-start.1 = (bf16[512,1280]{1,0:T(8,128)(2,1)S(1)}, bf16[512,1280]{1,0:T(8,128)(2,1)}, u32[]{:S(2)}, u32[]{:S(2)}) collective-permute-start(bf16[512,1280]{1,0:T(8,128)(2,1)S(1)} %bitcast.11), channel_id=1, source_target_pairs={{0,64},{1,9},{8,72},{9,17},{16,80},{17,25},{24,88},{25,33},{32,96}... | collective-permute-start | bytes 3932168 | tf_op jit(solution)/shard_map/dispatch/ppermute | solution.py:55
  49.3 20.1 %all-to-all-done.1 = bf16[64,2,4224]{2,1,0:T(2,128)(2,1)S(1)} async-done(((bf16[64,2,4224]{2,1,0:T(2,128)(2,1)}), bf16[64,2,4224]{2,1,0:T(2,128)(2,1)S(1)}, u32[]{:S(2)}, u32[]{:S(2)}) %all-to-all-start.1) | async-done | bytes 1081376 | tf_op jit(solution)/shard_map/dispatch/all_to_all | solution.py:360
  71.0 1.5 broadcast_in_dim.21
  72.5 4.0 %all-to-all-start.2 = ((bf16[4,64,4224]{2,1,0:T(8,128)(2,1)}), bf16[4,64,4224]{2,1,0:T(8,128)(2,1)S(1)}, u32[]{:S(2)}, u32[]{:S(2)}) async-start(bf16[4,64,4224]{2,1,0:T(8,128)(2,1)} %broadcast_in_dim.21), calls=%async_computation.2 | async-start | bytes 4325376 | tf_op jit(solution)/shard_map/pack_rows/all_to_all | solution.py:33
  76.5 6.0 %collective-permute-done.rest_1_ = bf16[512,1280]{1,0:T(8,128)(2,1)} collective-permute-done((bf16[512,1280]{1,0:T(8,128)(2,1)S(1)}, bf16[512,1280]{1,0:T(8,128)(2,1)}, u32[]{:S(2)}, u32[]{:S(2)}) %collective-permute-start) | collective-permute-done | bytes 1310752 | tf_op jit(solution)/shard_map/dispatch/ppermute | solution.py:55
  83.8 3.1 %collective-permute-start.2 = (bf16[512,1280]{1,0:T(8,128)(2,1)}, bf16[512,1280]{1,0:T(8,128)(2,1)}, u32[]{:S(2)}, u32[]{:S(2)}) collective-permute-start(bf16[512,1280]{1,0:T(8,128)(2,1)} %collective-permute-done.rest_1_), channel_id=1, source_target_pairs={{0,448},{1,57},{8,456},{9,1},{16,464},{17,9},{24,472},{25,17},{32,... | collective-permute-start | bytes 3932168 | tf_op jit(solution)/shard_map/pack_rows/ppermute | solution.py:55
  86.9 2.2 %collective-permute-start.5 = (bf16[512,1280]{1,0:T(8,128)(2,1)}, bf16[512,1280]{1,0:T(8,128)(2,1)}, u32[]{:S(2)}, u32[]{:S(2)}) collective-permute-start(bf16[512,1280]{1,0:T(8,128)(2,1)} %collective-permute-done.1.rest_2_), channel_id=1, source_target_pairs={{0,64},{1,9},{8,72},{9,17},{16,80},{17,25},{24,88},{25,33},{32,96}... | collective-permute-start | bytes 3932168 | tf_op jit(solution)/shard_map/pack_rows/ppermute | solution.py:55
  89.1 13.7 %collective-permute-done.2.rest_3_ = bf16[512,1280]{1,0:T(8,128)(2,1)} collective-permute-done((bf16[512,1280]{1,0:T(8,128)(2,1)}, bf16[512,1280]{1,0:T(8,128)(2,1)}, u32[]{:S(2)}, u32[]{:S(2)}) %collective-permute-start.2) | collective-permute-done | bytes 1310752 | tf_op jit(solution)/shard_map/pack_rows/ppermute | solution.py:55
  102.7 5.3 %collective-permute-start.3 = (bf16[256,4224]{1,0:T(8,128)(2,1)S(1)}, bf16[256,4224]{1,0:T(8,128)(2,1)}, u32[]{:S(2)}, u32[]{:S(2)}) collective-permute-start(bf16[256,4224]{1,0:T(8,128)(2,1)S(1)} %bitcast.6), channel_id=1, source_target_pairs={{0,1},{1,0},{2,3},{3,2},{4,5},{5,4},{6,7},{7,6},{8,9},{9,8},{10,11... | collective-permute-start | bytes 6488072 | tf_op jit(solution)/shard_map/pack_rows/ppermute | solution.py:27
  108.1 3.3 %collective-permute-start.4 = (bf16[512,1280]{1,0:T(8,128)(2,1)}, bf16[512,1280]{1,0:T(8,128)(2,1)}, u32[]{:S(2)}, u32[]{:S(2)}) collective-permute-start(bf16[512,1280]{1,0:T(8,128)(2,1)} %collective-permute-done.2.rest_3_), channel_id=1, source_target_pairs={{0,448},{1,57},{8,456},{9,1},{16,464},{17,9},{24,472},{25,17},{32,... | collective-permute-start | bytes 3932168 | tf_op jit(solution)/shard_map/pack_rows/ppermute | solution.py:55
  111.4 2.0 %collective-permute-start.6 = (bf16[512,1280]{1,0:T(8,128)(2,1)}, bf16[512,1280]{1,0:T(8,128)(2,1)}, u32[]{:S(2)}, u32[]{:S(2)}) collective-permute-start(bf16[512,1280]{1,0:T(8,128)(2,1)} %collective-permute-done.5.rest_4_), channel_id=1, source_target_pairs={{0,64},{1,9},{8,72},{9,17},{16,80},{17,25},{24,88},{25,33},{32,96}... | collective-permute-start | bytes 3932168 | tf_op jit(solution)/shard_map/pack_rows/ppermute | solution.py:55
  113.5 2.5 %turn_rows.3.far = bf16[256,4224]{1,0:T(8,128)(2,1)S(1)} custom-call(s32[1]{0:T(128)} %constant.60.clone.1.turned, bf16[256,4224]{1,0:T(8,128)(2,1)} %collective-permute-done.3.rows), custom_call_target="tpu_custom_call" | custom-call | tf_op jit(solution)/shard_map/pack_rows/turn_rows/pallas_call | solution.py:105
  116.0 5.7 %project.2 = (f32[512,768]{1,0:T(8,128)S(1)}, bf16[2560,512]{1,0:T(8,128)(2,1)S(1)}) custom-call(s32[1]{0:T(128)} %bitcast.1.ring_at, bf16[256,4224]{1,0:T(8,128)(2,1)S(1)} %bitcast.7, bf16[256,4224]{1,0:T(8,128)(2,1)S(1)} %turn_rows.3.far, bf16[512,1280]{1,0:T(8,128)(2,1)S(1)} %bitcast.12, bf16[512,1280]{1,0:T(8,128)(2,1)} %collective-permute-done.rest_1_, ...), custom_call_target="tpu_custom_call" | custom-call | flops 2013265920 | bytes 9175040 | tf_op jit(solution)/shard_map/attention/project/pallas_call | solution.py:168
  121.7 1.5 copy-done.2
  123.2 3.9 %collective-permute-done.4.rest_0_ = bf16[512,1280]{1,0:T(8,128)(2,1)} collective-permute-done((bf16[512,1280]{1,0:T(8,128)(2,1)}, bf16[512,1280]{1,0:T(8,128)(2,1)}, u32[]{:S(2)}, u32[]{:S(2)}) %collective-permute-start.4) | collective-permute-done | bytes 1310752 | tf_op jit(solution)/shard_map/pack_rows/ppermute | solution.py:55
  127.0 4.6 %collective-permute-done.6.rest_1_ = bf16[512,1280]{1,0:T(8,128)(2,1)} collective-permute-done((bf16[512,1280]{1,0:T(8,128)(2,1)}, bf16[512,1280]{1,0:T(8,128)(2,1)}, u32[]{:S(2)}, u32[]{:S(2)}) %collective-permute-start.6) | collective-permute-done | bytes 1310752 | tf_op jit(solution)/shard_map/pack_rows/ppermute | solution.py:55
  131.6 2.1 %slice.20 = bf16[512,768]{1,0:T(8,128)(2,1)} slice(bf16[512,1280]{1,0:T(8,128)(2,1)} %collective-permute-done.4.rest_0_), slice={[0:512], [0:768]} | slice | bytes 1572864 | tf_op jit(solution)/shard_map/attention/slice | solution.py:387
  133.6 1.9 collective-permute-start.7
  137.1 3.5 %collective-permute-start.8 = (bf16[512,512]{1,0:T(8,128)(2,1)S(1)}, bf16[512,512]{1,0:T(8,128)(2,1)S(1)}, u32[]{:S(2)}, u32[]{:S(2)}) collective-permute-start(bf16[512,512]{1,0:T(8,128)(2,1)S(1)} %slice.23), channel_id=1, source_target_pairs={{0,64},{1,9},{8,72},{9,17},{16,80},{17,25},{24,88},{25,33},{32,96}... | collective-permute-start | bytes 1572872 | tf_op jit(solution)/shard_map/attention/ppermute | solution.py:55
  141.6 1.6 copy-done.1
  143.3 1.4 copy-done.5
  144.7 2.8 %project.3 = (f32[512,768]{1,0:T(8,128)S(1)}, bf16[1024,512]{1,0:T(8,128)(2,1)S(1)}, bf16[512,512]{1,0:T(8,128)(2,1)S(1)}) custom-call(s32[1]{0:T(128)} %bitcast.1.ring_at, bf16[256,4224]{1,0:T(8,128)(2,1)S(1)} %bitcast.9, bf16[256,4224]{1,0:T(8,128)(2,1)S(1)} %copy-done.1, bf16[512,1280]{1,0:T(8,128)(2,1)} %collective-permute-done.4.rest_0_, ...), custom_call_target="tpu_custom_call" | custom-call | flops 805306368 | bytes 3670016 | tf_op jit(solution)/shard_map/attention/project/pallas_call | solution.py:168
  147.6 2.0 %far_attention.1 = (bf16[256,512]{1,0:T(8,128)(2,1)S(1)}, bf16[512,768]{1,0:T(8,128)(2,1)S(1)}) custom-call(bf16[512,512]{1,0:T(8,128)(2,1)S(1)} %get-tuple-element.29.rows, f32[512,768]{1,0:T(8,128)S(1)} %get-tuple-element.30.so_far, bf16[512,768]{1,0:T(8,128)(2,1)S(1)} %collective-permute-done.7.block, s32[512,1]{1,0:T(8,128)S(1)} %maximum_convert_fusion.rest_0_, ...), custom_call_target="tpu_custom_call" | custom-call | flops 671088640 | bytes 3932160 | tf_op jit(solution)/shard_map/attention/far_attention/pallas_call | solution.py:222
  149.6 2.0 %output_product.2 = bf16[256,4096]{1,0:T(8,128)(2,1)S(1)} custom-call(s32[1]{0:T(128)} %bitcast.1.ring_at, bf16[256,512]{1,0:T(8,128)(2,1)S(1)} %get-tuple-element.31.attended, bf16[2560,512]{1,0:T(8,128)(2,1)S(1)} %copy-done.3, bf16[1024,512]{1,0:T(8,128)(2,1)S(1)} %get-tuple-element.33.rest_1_, bf16[512,512]{1,0:T(8,128)(2,1)S(1)} %collective-permute-done.8.rest_2_), custom_call_target="tpu_custom_call" | custom-call | flops 1073741824 | bytes 6291456 | tf_op jit(solution)/shard_map/output/output_product/pallas_call | solution.py:281
  151.6 4.2 %collective-permute-start.9 = (bf16[256,4096]{1,0:T(8,128)(2,1)S(1)}, bf16[256,4096]{1,0:T(8,128)(2,1)S(1)}, u32[]{:S(2)}, u32[]{:S(2)}) collective-permute-start(bf16[256,4096]{1,0:T(8,128)(2,1)S(1)} %output_product.2), channel_id=1, source_target_pairs={{0,1},{1,0},{2,3},{3,2},{4,5},{5,4},{6,7},{7,6},{8,9},{9,8},{10,11... | collective-permute-start | bytes 6291464 | tf_op jit(solution)/shard_map/output/ppermute | solution.py:27
  155.8 1.4 near_attention.1.attended
  157.3 1.3 output_product.3
  160.4 29.3 %all_to_all.31.parts = bf16[4,64,4096]{2,1,0:T(8,128)(2,1)S(1)} all-to-all(bf16[4,64,4096]{2,1,0:T(8,128)(2,1)S(1)} %bitcast.13), channel_id=1, replica_groups=mesh['z'=8,'y'=8,'x'=4,'core'=2] {'x'}, dimensions={0} | all-to-all | bytes 4194304 | tf_op jit(solution)/shard_map/output/all_to_all | solution.py:407
  (56 shorter events, 12.5 us)
Async XLA Ops:
  2.1 11.0 %copy-start.8 = (s32[64]{0:T(128)S(1)}, s32[64]{0:T(128)}, u32[]{:S(2)}) copy-start(s32[64]{0:T(128)} %param.9) | copy-start | bytes 772
  2.1 11.3 %copy-start.6 = (bf16[64,4096]{1,0:T(8,128)(2,1)S(1)}, bf16[64,4096]{1,0:T(8,128)(2,1)}, u32[]{:S(2)}) copy-start(bf16[64,4096]{1,0:T(8,128)(2,1)} %param.8) | copy-start | bytes 1572868
  2.1 31.9 %all-to-all-start = ((bf16[8,64,1280]{2,1,0:T(8,128)(2,1)}), bf16[8,64,1280]{2,1,0:T(8,128)(2,1)S(1)}, u32[]{:S(2)}, u32[]{:S(2)}) async-start(bf16[8,64,1280]{2,1,0:T(8,128)(2,1)} %broadcast_in_dim.16), calls=%async_computation | async-start | bytes 2621440 | tf_op jit(solution)/shard_map/weights_spread/all_to_all | solution.py:44
  35.2 8.0 %copy-start.9 = (s32[64]{0:T(128)S(1)}, s32[64]{0:T(128)}, u32[]{:S(2)}) copy-start(s32[64]{0:T(128)} %param.10) | copy-start | bytes 772
  35.2 34.1 %all-to-all-start.1 = ((bf16[64,2,4224]{2,1,0:T(2,128)(2,1)}), bf16[64,2,4224]{2,1,0:T(2,128)(2,1)S(1)}, u32[]{:S(2)}, u32[]{:S(2)}) async-start(bf16[64,2,4224]{2,1,0:T(2,128)(2,1)} %all_to_all.21), calls=%async_computation.1 | async-start | bytes 2162688 | tf_op jit(solution)/shard_map/dispatch/all_to_all | solution.py:360
  43.2 39.4 %collective-permute-start = (bf16[512,1280]{1,0:T(8,128)(2,1)S(1)}, bf16[512,1280]{1,0:T(8,128)(2,1)}, u32[]{:S(2)}, u32[]{:S(2)}) collective-permute-start(bf16[512,1280]{1,0:T(8,128)(2,1)S(1)} %bitcast.10), channel_id=1, source_target_pairs={{0,448},{1,57},{8,456},{9,1},{16,464},{17,9},{24,472},{25,17},{32,... | collective-permute-start | bytes 3932168 | tf_op jit(solution)/shard_map/dispatch/ppermute | solution.py:55
  47.3 36.5 %collective-permute-start.1 = (bf16[512,1280]{1,0:T(8,128)(2,1)S(1)}, bf16[512,1280]{1,0:T(8,128)(2,1)}, u32[]{:S(2)}, u32[]{:S(2)}) collective-permute-start(bf16[512,1280]{1,0:T(8,128)(2,1)S(1)} %bitcast.11), channel_id=1, source_target_pairs={{0,64},{1,9},{8,72},{9,17},{16,80},{17,25},{24,88},{25,33},{32,96}... | collective-permute-start | bytes 3932168 | tf_op jit(solution)/shard_map/dispatch/ppermute | solution.py:55
  69.8 0.7 copy-start.7
  72.5 30.2 %all-to-all-start.2 = ((bf16[4,64,4224]{2,1,0:T(8,128)(2,1)}), bf16[4,64,4224]{2,1,0:T(8,128)(2,1)S(1)}, u32[]{:S(2)}, u32[]{:S(2)}) async-start(bf16[4,64,4224]{2,1,0:T(8,128)(2,1)} %broadcast_in_dim.21), calls=%async_computation.2 | async-start | bytes 4325376 | tf_op jit(solution)/shard_map/pack_rows/all_to_all | solution.py:33
  83.8 19.0 %collective-permute-start.2 = (bf16[512,1280]{1,0:T(8,128)(2,1)}, bf16[512,1280]{1,0:T(8,128)(2,1)}, u32[]{:S(2)}, u32[]{:S(2)}) collective-permute-start(bf16[512,1280]{1,0:T(8,128)(2,1)} %collective-permute-done.rest_1_), channel_id=1, source_target_pairs={{0,448},{1,57},{8,456},{9,1},{16,464},{17,9},{24,472},{25,17},{32,... | collective-permute-start | bytes 3932168 | tf_op jit(solution)/shard_map/pack_rows/ppermute | solution.py:55
  86.9 24.5 %collective-permute-start.5 = (bf16[512,1280]{1,0:T(8,128)(2,1)}, bf16[512,1280]{1,0:T(8,128)(2,1)}, u32[]{:S(2)}, u32[]{:S(2)}) collective-permute-start(bf16[512,1280]{1,0:T(8,128)(2,1)} %collective-permute-done.1.rest_2_), channel_id=1, source_target_pairs={{0,64},{1,9},{8,72},{9,17},{16,80},{17,25},{24,88},{25,33},{32,96}... | collective-permute-start | bytes 3932168 | tf_op jit(solution)/shard_map/pack_rows/ppermute | solution.py:55
  102.7 10.7 %collective-permute-start.3 = (bf16[256,4224]{1,0:T(8,128)(2,1)S(1)}, bf16[256,4224]{1,0:T(8,128)(2,1)}, u32[]{:S(2)}, u32[]{:S(2)}) collective-permute-start(bf16[256,4224]{1,0:T(8,128)(2,1)S(1)} %bitcast.6), channel_id=1, source_target_pairs={{0,1},{1,0},{2,3},{3,2},{4,5},{5,4},{6,7},{7,6},{8,9},{9,8},{10,11... | collective-permute-start | bytes 6488072 | tf_op jit(solution)/shard_map/pack_rows/ppermute | solution.py:27
  108.1 19.0 %collective-permute-start.4 = (bf16[512,1280]{1,0:T(8,128)(2,1)}, bf16[512,1280]{1,0:T(8,128)(2,1)}, u32[]{:S(2)}, u32[]{:S(2)}) collective-permute-start(bf16[512,1280]{1,0:T(8,128)(2,1)} %collective-permute-done.2.rest_3_), channel_id=1, source_target_pairs={{0,448},{1,57},{8,456},{9,1},{16,464},{17,9},{24,472},{25,17},{32,... | collective-permute-start | bytes 3932168 | tf_op jit(solution)/shard_map/pack_rows/ppermute | solution.py:55
  111.4 20.2 %collective-permute-start.6 = (bf16[512,1280]{1,0:T(8,128)(2,1)}, bf16[512,1280]{1,0:T(8,128)(2,1)}, u32[]{:S(2)}, u32[]{:S(2)}) collective-permute-start(bf16[512,1280]{1,0:T(8,128)(2,1)} %collective-permute-done.5.rest_4_), channel_id=1, source_target_pairs={{0,64},{1,9},{8,72},{9,17},{16,80},{17,25},{24,88},{25,33},{32,96}... | collective-permute-start | bytes 3932168 | tf_op jit(solution)/shard_map/pack_rows/ppermute | solution.py:55
  116.0 5.7 %copy-start = (bf16[256,4224]{1,0:T(8,128)(2,1)}, bf16[256,4224]{1,0:T(8,128)(2,1)S(1)}, u32[]{:S(2)}) copy-start(bf16[256,4224]{1,0:T(8,128)(2,1)S(1)} %turn_rows.3.far) | copy-start | bytes 6488068
  121.7 1.5 copy-start.2
  123.2 12.4 %copy-start.4 = (f32[512,768]{1,0:T(8,128)}, f32[512,768]{1,0:T(8,128)S(1)}, u32[]{:S(2)}) copy-start(f32[512,768]{1,0:T(8,128)S(1)} %get-tuple-element.26.rest_2_) | copy-start | bytes 4718596
  133.6 13.9 %collective-permute-start.7 = (bf16[512,768]{1,0:T(8,128)(2,1)}, bf16[512,768]{1,0:T(8,128)(2,1)S(1)}, u32[]{:S(2)}, u32[]{:S(2)}) collective-permute-start(bf16[512,768]{1,0:T(8,128)(2,1)} %slice.20), channel_id=1, source_target_pairs={{0,448},{1,57},{8,456},{9,1},{16,464},{17,9},{24,472},{25,17},{32,... | collective-permute-start | bytes 2359304 | tf_op jit(solution)/shard_map/attention/ppermute | solution.py:55
  137.1 12.5 %collective-permute-start.8 = (bf16[512,512]{1,0:T(8,128)(2,1)S(1)}, bf16[512,512]{1,0:T(8,128)(2,1)S(1)}, u32[]{:S(2)}, u32[]{:S(2)}) collective-permute-start(bf16[512,512]{1,0:T(8,128)(2,1)S(1)} %slice.23), channel_id=1, source_target_pairs={{0,64},{1,9},{8,72},{9,17},{16,80},{17,25},{24,88},{25,33},{32,96}... | collective-permute-start | bytes 1572872 | tf_op jit(solution)/shard_map/attention/ppermute | solution.py:55
  141.6 1.6 copy-start.1
  143.3 1.4 copy-start.5
  147.6 2.0 %copy-start.3 = (bf16[2560,512]{1,0:T(8,128)(2,1)S(1)}, bf16[2560,512]{1,0:T(8,128)(2,1)}, u32[]{:S(2)}) copy-start(bf16[2560,512]{1,0:T(8,128)(2,1)} %copy-done.2) | copy-start | bytes 7864324
  151.6 8.0 %collective-permute-start.9 = (bf16[256,4096]{1,0:T(8,128)(2,1)S(1)}, bf16[256,4096]{1,0:T(8,128)(2,1)S(1)}, u32[]{:S(2)}, u32[]{:S(2)}) collective-permute-start(bf16[256,4096]{1,0:T(8,128)(2,1)S(1)} %output_product.2), channel_id=1, source_target_pairs={{0,1},{1,0},{2,3},{3,2},{4,5},{5,4},{6,7},{7,6},{8,9},{9,8},{10,11... | collective-permute-start | bytes 6291464 | tf_op jit(solution)/shard_map/output/ppermute | solution.py:27

commit v7 on v6

--- a/solution.py
+++ b/solution.py
@@ -383,9 +383,11 @@
     with jax.named_scope("attention"):
         early, early_steps = [line, *line_1, *line_2], (0, 1, 7, 2, 6)
         so_far, pieces = project(ring_at, near, far, early, early_steps, projection)
-        line_3, _ = lax.optimization_barrier((line_3, so_far))
-        block_4 = across(line_3[0][:, :projection], -1)
-        pieces_4 = across(line_3[1][:, projection:], 1)
+        above_3, _ = lax.optimization_barrier((line_3[0], so_far))
+        above_part, below_3 = lax.optimization_barrier((above_3[:, :projection], line_3[1]))
+        block_4 = across(above_part, -1)
+        pieces_4 = across(below_3[:, projection:], 1)
+        line_3 = (above_3, below_3)
         so_far, pieces_3, last_rows = project(
             ring_at, near, far, line_3, (3, 5), projection, so_far
         )

time: 192 us -> 190 us (0.990)
  waiting for transfers between devices: 70.5 us -> 68.5 us
    ppermute x8, waiting for transfers between devices: 29.3 us -> 27.3 us  [across(): return lax.ppermute(array, PLANE, pairs)]
  transfers between devices with their start and end apart: 13 -> 13, of which waited for: 8 -> 8; matrix products, arithmetic and copies ran while one was open for 3% -> 4% of each run, Pallas kernels for 8% -> 8%
where the time goes in v7:
time: 190 us; the launch traced here: 189 us
  waiting for transfers between devices  68.5 us (36%)
  starting transfers between devices  54.5 us (29%)
  blocking collectives  29.3 us (15%)
  Pallas kernels  19.2 us (10%)
  local copies, waits for them, and re-layouts  13.6 us (7%)
  other arithmetic  2.42 us (1%)
    all_to_all x1, blocking collectives, on_device(): parts = lax.all_to_all(both, 'x', split_axis=0, concat_axis=0, tiled=True)  29.3 us
    ppermute x8, waiting for transfers between devices, across(): return lax.ppermute(array, PLANE, pairs)  27.3 us
    ppermute x8, starting transfers between devices, across(): return lax.ppermute(array, PLANE, pairs)  22.1 us
    all_to_all x1, waiting for transfers between devices, spread_lines(): lax.all_to_all(copies, PLANE, split_axis=0, concat_axis=0, axis_index_gro...  20.1 us
    all_to_all x1, waiting for transfers between devices, on_device(): lax.all_to_all(outgoing, ('z', 'y'), split_axis=0, concat_axis=0, tiled=T...  20.1 us
    all_to_all x1, starting transfers between devices, spread_lines(): lax.all_to_all(copies, PLANE, split_axis=0, concat_axis=0, axis_index_gro...  11 us
    ppermute x2, starting transfers between devices, shift(): lax.ppermute(array, axis, [(i, (i + step) % size) for i in range(size)])  9.49 us
    pallas_call x2, Pallas kernels, project(): pl.pallas_call(functools.partial(project_kernel, steps), out_shape=result...  8.5 us
  transfers between devices with their start and end apart: 13, of which 8 were waited for; matrix products, arithmetic and copies ran while one was open for 4% of the time, Pallas kernels for 8%

profile of v7, /device:TPU:1, one launch (start us, length us, event | category | flops | bytes accessed | tf_op | source)
XLA Modules:
  0.0 188.8 jit_solution(13731577509332733723)
XLA Ops:
  2.1 11.0 %all-to-all-start = ((bf16[8,64,1280]{2,1,0:T(8,128)(2,1)}), bf16[8,64,1280]{2,1,0:T(8,128)(2,1)S(1)}, u32[]{:S(2)}, u32[]{:S(2)}) async-start(bf16[8,64,1280]{2,1,0:T(8,128)(2,1)} %broadcast_in_dim.16), calls=%async_computation | async-start | bytes 2621440 | tf_op jit(solution)/shard_map/weights_spread/all_to_all | solution.py:44
  13.8 20.1 %all-to-all-done = bf16[8,64,1280]{2,1,0:T(8,128)(2,1)S(1)} async-done(((bf16[8,64,1280]{2,1,0:T(8,128)(2,1)}), bf16[8,64,1280]{2,1,0:T(8,128)(2,1)S(1)}, u32[]{:S(2)}, u32[]{:S(2)}) %all-to-all-start) | async-done | bytes 1310752 | tf_op jit(solution)/shard_map/weights_spread/all_to_all | solution.py:44
  35.2 8.0 %all-to-all-start.1 = ((bf16[64,2,4224]{2,1,0:T(2,128)(2,1)}), bf16[64,2,4224]{2,1,0:T(2,128)(2,1)S(1)}, u32[]{:S(2)}, u32[]{:S(2)}) async-start(bf16[64,2,4224]{2,1,0:T(2,128)(2,1)} %all_to_all.21), calls=%async_computation.1 | async-start | bytes 2162688 | tf_op jit(solution)/shard_map/dispatch/all_to_all | solution.py:360
  43.2 4.1 %collective-permute-start = (bf16[512,1280]{1,0:T(8,128)(2,1)S(1)}, bf16[512,1280]{1,0:T(8,128)(2,1)}, u32[]{:S(2)}, u32[]{:S(2)}) collective-permute-start(bf16[512,1280]{1,0:T(8,128)(2,1)S(1)} %bitcast.10), channel_id=1, source_target_pairs={{0,448},{1,57},{8,456},{9,1},{16,464},{17,9},{24,472},{25,17},{32,... | collective-permute-start | bytes 3932168 | tf_op jit(solution)/shard_map/dispatch/ppermute | solution.py:55
  47.3 1.9 %collective-permute-start.1 = (bf16[512,1280]{1,0:T(8,128)(2,1)S(1)}, bf16[512,1280]{1,0:T(8,128)(2,1)}, u32[]{:S(2)}, u32[]{:S(2)}) collective-permute-start(bf16[512,1280]{1,0:T(8,128)(2,1)S(1)} %bitcast.11), channel_id=1, source_target_pairs={{0,64},{1,9},{8,72},{9,17},{16,80},{17,25},{24,88},{25,33},{32,96}... | collective-permute-start | bytes 3932168 | tf_op jit(solution)/shard_map/dispatch/ppermute | solution.py:55
  49.3 20.1 %all-to-all-done.1 = bf16[64,2,4224]{2,1,0:T(2,128)(2,1)S(1)} async-done(((bf16[64,2,4224]{2,1,0:T(2,128)(2,1)}), bf16[64,2,4224]{2,1,0:T(2,128)(2,1)S(1)}, u32[]{:S(2)}, u32[]{:S(2)}) %all-to-all-start.1) | async-done | bytes 1081376 | tf_op jit(solution)/shard_map/dispatch/all_to_all | solution.py:360
  71.0 1.5 broadcast_in_dim.21
  72.5 4.0 %all-to-all-start.2 = ((bf16[4,64,4224]{2,1,0:T(8,128)(2,1)}), bf16[4,64,4224]{2,1,0:T(8,128)(2,1)S(1)}, u32[]{:S(2)}, u32[]{:S(2)}) async-start(bf16[4,64,4224]{2,1,0:T(8,128)(2,1)} %broadcast_in_dim.21), calls=%async_computation.2 | async-start | bytes 4325376 | tf_op jit(solution)/shard_map/pack_rows/all_to_all | solution.py:33
  76.5 6.0 %collective-permute-done.rest_1_ = bf16[512,1280]{1,0:T(8,128)(2,1)} collective-permute-done((bf16[512,1280]{1,0:T(8,128)(2,1)S(1)}, bf16[512,1280]{1,0:T(8,128)(2,1)}, u32[]{:S(2)}, u32[]{:S(2)}) %collective-permute-start) | collective-permute-done | bytes 1310752 | tf_op jit(solution)/shard_map/dispatch/ppermute | solution.py:55
  83.8 3.1 %collective-permute-start.2 = (bf16[512,1280]{1,0:T(8,128)(2,1)}, bf16[512,1280]{1,0:T(8,128)(2,1)}, u32[]{:S(2)}, u32[]{:S(2)}) collective-permute-start(bf16[512,1280]{1,0:T(8,128)(2,1)} %collective-permute-done.rest_1_), channel_id=1, source_target_pairs={{0,448},{1,57},{8,456},{9,1},{16,464},{17,9},{24,472},{25,17},{32,... | collective-permute-start | bytes 3932168 | tf_op jit(solution)/shard_map/pack_rows/ppermute | solution.py:55
  86.9 2.2 %collective-permute-start.5 = (bf16[512,1280]{1,0:T(8,128)(2,1)}, bf16[512,1280]{1,0:T(8,128)(2,1)}, u32[]{:S(2)}, u32[]{:S(2)}) collective-permute-start(bf16[512,1280]{1,0:T(8,128)(2,1)} %collective-permute-done.1.rest_2_), channel_id=1, source_target_pairs={{0,64},{1,9},{8,72},{9,17},{16,80},{17,25},{24,88},{25,33},{32,96}... | collective-permute-start | bytes 3932168 | tf_op jit(solution)/shard_map/pack_rows/ppermute | solution.py:55
  89.1 13.7 %collective-permute-done.2.rest_3_ = bf16[512,1280]{1,0:T(8,128)(2,1)} collective-permute-done((bf16[512,1280]{1,0:T(8,128)(2,1)}, bf16[512,1280]{1,0:T(8,128)(2,1)}, u32[]{:S(2)}, u32[]{:S(2)}) %collective-permute-start.2) | collective-permute-done | bytes 1310752 | tf_op jit(solution)/shard_map/pack_rows/ppermute | solution.py:55
  102.7 5.3 %collective-permute-start.3 = (bf16[256,4224]{1,0:T(8,128)(2,1)S(1)}, bf16[256,4224]{1,0:T(8,128)(2,1)}, u32[]{:S(2)}, u32[]{:S(2)}) collective-permute-start(bf16[256,4224]{1,0:T(8,128)(2,1)S(1)} %bitcast.6), channel_id=1, source_target_pairs={{0,1},{1,0},{2,3},{3,2},{4,5},{5,4},{6,7},{7,6},{8,9},{9,8},{10,11... | collective-permute-start | bytes 6488072 | tf_op jit(solution)/shard_map/pack_rows/ppermute | solution.py:27
  108.1 3.3 %collective-permute-start.4 = (bf16[512,1280]{1,0:T(8,128)(2,1)}, bf16[512,1280]{1,0:T(8,128)(2,1)}, u32[]{:S(2)}, u32[]{:S(2)}) collective-permute-start(bf16[512,1280]{1,0:T(8,128)(2,1)} %collective-permute-done.2.rest_3_), channel_id=1, source_target_pairs={{0,448},{1,57},{8,456},{9,1},{16,464},{17,9},{24,472},{25,17},{32,... | collective-permute-start | bytes 3932168 | tf_op jit(solution)/shard_map/pack_rows/ppermute | solution.py:55
  111.4 2.0 %collective-permute-start.6 = (bf16[512,1280]{1,0:T(8,128)(2,1)}, bf16[512,1280]{1,0:T(8,128)(2,1)}, u32[]{:S(2)}, u32[]{:S(2)}) collective-permute-start(bf16[512,1280]{1,0:T(8,128)(2,1)} %collective-permute-done.5.rest_4_), channel_id=1, source_target_pairs={{0,64},{1,9},{8,72},{9,17},{16,80},{17,25},{24,88},{25,33},{32,96}... | collective-permute-start | bytes 3932168 | tf_op jit(solution)/shard_map/pack_rows/ppermute | solution.py:55
  113.5 2.5 %turn_rows.3.far = bf16[256,4224]{1,0:T(8,128)(2,1)S(1)} custom-call(s32[1]{0:T(128)} %constant.60.clone.1.turned, bf16[256,4224]{1,0:T(8,128)(2,1)} %collective-permute-done.3.rows), custom_call_target="tpu_custom_call" | custom-call | tf_op jit(solution)/shard_map/pack_rows/turn_rows/pallas_call | solution.py:105
  116.0 5.7 %project.2 = (f32[512,768]{1,0:T(8,128)S(1)}, bf16[2560,512]{1,0:T(8,128)(2,1)S(1)}) custom-call(s32[1]{0:T(128)} %bitcast.1.ring_at, bf16[256,4224]{1,0:T(8,128)(2,1)S(1)} %bitcast.7, bf16[256,4224]{1,0:T(8,128)(2,1)S(1)} %turn_rows.3.far, bf16[512,1280]{1,0:T(8,128)(2,1)S(1)} %bitcast.12, bf16[512,1280]{1,0:T(8,128)(2,1)} %collective-permute-done.rest_1_, ...), custom_call_target="tpu_custom_call" | custom-call | flops 2013265920 | bytes 9175040 | tf_op jit(solution)/shard_map/attention/project/pallas_call | solution.py:168
  121.7 1.5 copy-done.2
  123.2 3.9 %collective-permute-done.4.rest_0_ = bf16[512,1280]{1,0:T(8,128)(2,1)} collective-permute-done((bf16[512,1280]{1,0:T(8,128)(2,1)}, bf16[512,1280]{1,0:T(8,128)(2,1)}, u32[]{:S(2)}, u32[]{:S(2)}) %collective-permute-start.4) | collective-permute-done | bytes 1310752 | tf_op jit(solution)/shard_map/pack_rows/ppermute | solution.py:55
  127.0 2.1 %slice.20 = bf16[512,768]{1,0:T(8,128)(2,1)} slice(bf16[512,1280]{1,0:T(8,128)(2,1)} %collective-permute-done.4.rest_0_), slice={[0:512], [0:768]} | slice | bytes 1572864 | tf_op jit(solution)/shard_map/attention/slice | solution.py:387
  129.1 2.5 %collective-permute-done.6.rest_1_ = bf16[512,1280]{1,0:T(8,128)(2,1)} collective-permute-done((bf16[512,1280]{1,0:T(8,128)(2,1)}, bf16[512,1280]{1,0:T(8,128)(2,1)}, u32[]{:S(2)}, u32[]{:S(2)}) %collective-permute-start.6) | collective-permute-done | bytes 1310752 | tf_op jit(solution)/shard_map/pack_rows/ppermute | solution.py:55
  131.6 2.0 %collective-permute-start.7 = (bf16[512,768]{1,0:T(8,128)(2,1)}, bf16[512,768]{1,0:T(8,128)(2,1)S(1)}, u32[]{:S(2)}, u32[]{:S(2)}) collective-permute-start(bf16[512,768]{1,0:T(8,128)(2,1)} %slice.20), channel_id=1, source_target_pairs={{0,448},{1,57},{8,456},{9,1},{16,464},{17,9},{24,472},{25,17},{32,... | collective-permute-start | bytes 2359304 | tf_op jit(solution)/shard_map/attention/ppermute | solution.py:55
  135.2 3.4 %collective-permute-start.8 = (bf16[512,512]{1,0:T(8,128)(2,1)S(1)}, bf16[512,512]{1,0:T(8,128)(2,1)S(1)}, u32[]{:S(2)}, u32[]{:S(2)}) collective-permute-start(bf16[512,512]{1,0:T(8,128)(2,1)S(1)} %slice.23), channel_id=1, source_target_pairs={{0,64},{1,9},{8,72},{9,17},{16,80},{17,25},{24,88},{25,33},{32,96}... | collective-permute-start | bytes 1572872 | tf_op jit(solution)/shard_map/attention/ppermute | solution.py:55
  139.6 1.6 copy-done.1
  141.2 1.4 copy-done.5
  142.6 2.8 %project.3 = (f32[512,768]{1,0:T(8,128)S(1)}, bf16[1024,512]{1,0:T(8,128)(2,1)S(1)}, bf16[512,512]{1,0:T(8,128)(2,1)S(1)}) custom-call(s32[1]{0:T(128)} %bitcast.1.ring_at, bf16[256,4224]{1,0:T(8,128)(2,1)S(1)} %bitcast.9, bf16[256,4224]{1,0:T(8,128)(2,1)S(1)} %copy-done.1, bf16[512,1280]{1,0:T(8,128)(2,1)} %collective-permute-done.4.rest_0_, ...), custom_call_target="tpu_custom_call" | custom-call | flops 805306368 | bytes 3670016 | tf_op jit(solution)/shard_map/attention/project/pallas_call | solution.py:168
  145.5 2.0 %far_attention.1 = (bf16[256,512]{1,0:T(8,128)(2,1)S(1)}, bf16[512,768]{1,0:T(8,128)(2,1)S(1)}) custom-call(bf16[512,512]{1,0:T(8,128)(2,1)S(1)} %get-tuple-element.30.rows, f32[512,768]{1,0:T(8,128)S(1)} %get-tuple-element.31.so_far, bf16[512,768]{1,0:T(8,128)(2,1)S(1)} %collective-permute-done.7.block, s32[512,1]{1,0:T(8,128)S(1)} %maximum_convert_fusion.rest_0_, ...), custom_call_target="tpu_custom_call" | custom-call | flops 671088640 | bytes 3932160 | tf_op jit(solution)/shard_map/attention/far_attention/pallas_call | solution.py:222
  147.6 2.0 %output_product.2 = bf16[256,4096]{1,0:T(8,128)(2,1)S(1)} custom-call(s32[1]{0:T(128)} %bitcast.1.ring_at, bf16[256,512]{1,0:T(8,128)(2,1)S(1)} %get-tuple-element.33.attended, bf16[2560,512]{1,0:T(8,128)(2,1)S(1)} %copy-done.3, bf16[1024,512]{1,0:T(8,128)(2,1)S(1)} %get-tuple-element.35.rest_1_, bf16[512,512]{1,0:T(8,128)(2,1)S(1)} %collective-permute-done.8.rest_2_), custom_call_target="tpu_custom_call" | custom-call | flops 1073741824 | bytes 6291456 | tf_op jit(solution)/shard_map/output/output_product/pallas_call | solution.py:281
  149.6 4.2 %collective-permute-start.9 = (bf16[256,4096]{1,0:T(8,128)(2,1)S(1)}, bf16[256,4096]{1,0:T(8,128)(2,1)S(1)}, u32[]{:S(2)}, u32[]{:S(2)}) collective-permute-start(bf16[256,4096]{1,0:T(8,128)(2,1)S(1)} %output_product.2), channel_id=1, source_target_pairs={{0,1},{1,0},{2,3},{3,2},{4,5},{5,4},{6,7},{7,6},{8,9},{9,8},{10,11... | collective-permute-start | bytes 6291464 | tf_op jit(solution)/shard_map/output/ppermute | solution.py:27
  153.8 1.4 near_attention.1.attended
  155.2 1.3 output_product.3
  158.3 29.3 %all_to_all.31.parts = bf16[4,64,4096]{2,1,0:T(8,128)(2,1)S(1)} all-to-all(bf16[4,64,4096]{2,1,0:T(8,128)(2,1)S(1)} %bitcast.13), channel_id=1, replica_groups=mesh['z'=8,'y'=8,'x'=4,'core'=2] {'x'}, dimensions={0} | all-to-all | bytes 4194304 | tf_op jit(solution)/shard_map/output/all_to_all | solution.py:409
  (56 shorter events, 12.5 us)
Async XLA Ops:
  2.1 11.0 %copy-start.8 = (s32[64]{0:T(128)S(1)}, s32[64]{0:T(128)}, u32[]{:S(2)}) copy-start(s32[64]{0:T(128)} %param.9) | copy-start | bytes 772
  2.1 11.3 %copy-start.6 = (bf16[64,4096]{1,0:T(8,128)(2,1)S(1)}, bf16[64,4096]{1,0:T(8,128)(2,1)}, u32[]{:S(2)}) copy-start(bf16[64,4096]{1,0:T(8,128)(2,1)} %param.8) | copy-start | bytes 1572868
  2.1 31.9 %all-to-all-start = ((bf16[8,64,1280]{2,1,0:T(8,128)(2,1)}), bf16[8,64,1280]{2,1,0:T(8,128)(2,1)S(1)}, u32[]{:S(2)}, u32[]{:S(2)}) async-start(bf16[8,64,1280]{2,1,0:T(8,128)(2,1)} %broadcast_in_dim.16), calls=%async_computation | async-start | bytes 2621440 | tf_op jit(solution)/shard_map/weights_spread/all_to_all | solution.py:44
  35.2 8.0 %copy-start.9 = (s32[64]{0:T(128)S(1)}, s32[64]{0:T(128)}, u32[]{:S(2)}) copy-start(s32[64]{0:T(128)} %param.10) | copy-start | bytes 772
  35.2 34.1 %all-to-all-start.1 = ((bf16[64,2,4224]{2,1,0:T(2,128)(2,1)}), bf16[64,2,4224]{2,1,0:T(2,128)(2,1)S(1)}, u32[]{:S(2)}, u32[]{:S(2)}) async-start(bf16[64,2,4224]{2,1,0:T(2,128)(2,1)} %all_to_all.21), calls=%async_computation.1 | async-start | bytes 2162688 | tf_op jit(solution)/shard_map/dispatch/all_to_all | solution.py:360
  43.2 39.4 %collective-permute-start = (bf16[512,1280]{1,0:T(8,128)(2,1)S(1)}, bf16[512,1280]{1,0:T(8,128)(2,1)}, u32[]{:S(2)}, u32[]{:S(2)}) collective-permute-start(bf16[512,1280]{1,0:T(8,128)(2,1)S(1)} %bitcast.10), channel_id=1, source_target_pairs={{0,448},{1,57},{8,456},{9,1},{16,464},{17,9},{24,472},{25,17},{32,... | collective-permute-start | bytes 3932168 | tf_op jit(solution)/shard_map/dispatch/ppermute | solution.py:55
  47.3 36.5 %collective-permute-start.1 = (bf16[512,1280]{1,0:T(8,128)(2,1)S(1)}, bf16[512,1280]{1,0:T(8,128)(2,1)}, u32[]{:S(2)}, u32[]{:S(2)}) collective-permute-start(bf16[512,1280]{1,0:T(8,128)(2,1)S(1)} %bitcast.11), channel_id=1, source_target_pairs={{0,64},{1,9},{8,72},{9,17},{16,80},{17,25},{24,88},{25,33},{32,96}... | collective-permute-start | bytes 3932168 | tf_op jit(solution)/shard_map/dispatch/ppermute | solution.py:55
  69.8 0.7 copy-start.7
  72.5 30.2 %all-to-all-start.2 = ((bf16[4,64,4224]{2,1,0:T(8,128)(2,1)}), bf16[4,64,4224]{2,1,0:T(8,128)(2,1)S(1)}, u32[]{:S(2)}, u32[]{:S(2)}) async-start(bf16[4,64,4224]{2,1,0:T(8,128)(2,1)} %broadcast_in_dim.21), calls=%async_computation.2 | async-start | bytes 4325376 | tf_op jit(solution)/shard_map/pack_rows/all_to_all | solution.py:33
  83.8 19.0 %collective-permute-start.2 = (bf16[512,1280]{1,0:T(8,128)(2,1)}, bf16[512,1280]{1,0:T(8,128)(2,1)}, u32[]{:S(2)}, u32[]{:S(2)}) collective-permute-start(bf16[512,1280]{1,0:T(8,128)(2,1)} %collective-permute-done.rest_1_), channel_id=1, source_target_pairs={{0,448},{1,57},{8,456},{9,1},{16,464},{17,9},{24,472},{25,17},{32,... | collective-permute-start | bytes 3932168 | tf_op jit(solution)/shard_map/pack_rows/ppermute | solution.py:55
  86.9 24.5 %collective-permute-start.5 = (bf16[512,1280]{1,0:T(8,128)(2,1)}, bf16[512,1280]{1,0:T(8,128)(2,1)}, u32[]{:S(2)}, u32[]{:S(2)}) collective-permute-start(bf16[512,1280]{1,0:T(8,128)(2,1)} %collective-permute-done.1.rest_2_), channel_id=1, source_target_pairs={{0,64},{1,9},{8,72},{9,17},{16,80},{17,25},{24,88},{25,33},{32,96}... | collective-permute-start | bytes 3932168 | tf_op jit(solution)/shard_map/pack_rows/ppermute | solution.py:55
  102.7 10.7 %collective-permute-start.3 = (bf16[256,4224]{1,0:T(8,128)(2,1)S(1)}, bf16[256,4224]{1,0:T(8,128)(2,1)}, u32[]{:S(2)}, u32[]{:S(2)}) collective-permute-start(bf16[256,4224]{1,0:T(8,128)(2,1)S(1)} %bitcast.6), channel_id=1, source_target_pairs={{0,1},{1,0},{2,3},{3,2},{4,5},{5,4},{6,7},{7,6},{8,9},{9,8},{10,11... | collective-permute-start | bytes 6488072 | tf_op jit(solution)/shard_map/pack_rows/ppermute | solution.py:27
  108.1 19.0 %collective-permute-start.4 = (bf16[512,1280]{1,0:T(8,128)(2,1)}, bf16[512,1280]{1,0:T(8,128)(2,1)}, u32[]{:S(2)}, u32[]{:S(2)}) collective-permute-start(bf16[512,1280]{1,0:T(8,128)(2,1)} %collective-permute-done.2.rest_3_), channel_id=1, source_target_pairs={{0,448},{1,57},{8,456},{9,1},{16,464},{17,9},{24,472},{25,17},{32,... | collective-permute-start | bytes 3932168 | tf_op jit(solution)/shard_map/pack_rows/ppermute | solution.py:55
  111.4 20.2 %collective-permute-start.6 = (bf16[512,1280]{1,0:T(8,128)(2,1)}, bf16[512,1280]{1,0:T(8,128)(2,1)}, u32[]{:S(2)}, u32[]{:S(2)}) collective-permute-start(bf16[512,1280]{1,0:T(8,128)(2,1)} %collective-permute-done.5.rest_4_), channel_id=1, source_target_pairs={{0,64},{1,9},{8,72},{9,17},{16,80},{17,25},{24,88},{25,33},{32,96}... | collective-permute-start | bytes 3932168 | tf_op jit(solution)/shard_map/pack_rows/ppermute | solution.py:55
  116.0 5.7 %copy-start = (bf16[256,4224]{1,0:T(8,128)(2,1)}, bf16[256,4224]{1,0:T(8,128)(2,1)S(1)}, u32[]{:S(2)}) copy-start(bf16[256,4224]{1,0:T(8,128)(2,1)S(1)} %turn_rows.3.far) | copy-start | bytes 6488068
  121.7 1.5 copy-start.2
  123.2 10.5 %copy-start.4 = (f32[512,768]{1,0:T(8,128)}, f32[512,768]{1,0:T(8,128)S(1)}, u32[]{:S(2)}) copy-start(f32[512,768]{1,0:T(8,128)S(1)} %get-tuple-element.27.rest_2_) | copy-start | bytes 4718596
  131.6 13.9 %collective-permute-start.7 = (bf16[512,768]{1,0:T(8,128)(2,1)}, bf16[512,768]{1,0:T(8,128)(2,1)S(1)}, u32[]{:S(2)}, u32[]{:S(2)}) collective-permute-start(bf16[512,768]{1,0:T(8,128)(2,1)} %slice.20), channel_id=1, source_target_pairs={{0,448},{1,57},{8,456},{9,1},{16,464},{17,9},{24,472},{25,17},{32,... | collective-permute-start | bytes 2359304 | tf_op jit(solution)/shard_map/attention/ppermute | solution.py:55
  135.2 12.4 %collective-permute-start.8 = (bf16[512,512]{1,0:T(8,128)(2,1)S(1)}, bf16[512,512]{1,0:T(8,128)(2,1)S(1)}, u32[]{:S(2)}, u32[]{:S(2)}) collective-permute-start(bf16[512,512]{1,0:T(8,128)(2,1)S(1)} %slice.23), channel_id=1, source_target_pairs={{0,64},{1,9},{8,72},{9,17},{16,80},{17,25},{24,88},{25,33},{32,96}... | collective-permute-start | bytes 1572872 | tf_op jit(solution)/shard_map/attention/ppermute | solution.py:55
  139.6 1.6 copy-start.1
  141.2 1.4 copy-start.5
  145.5 2.0 %copy-start.3 = (bf16[2560,512]{1,0:T(8,128)(2,1)S(1)}, bf16[2560,512]{1,0:T(8,128)(2,1)}, u32[]{:S(2)}) copy-start(bf16[2560,512]{1,0:T(8,128)(2,1)} %copy-done.2) | copy-start | bytes 7864324
  149.6 8.0 %collective-permute-start.9 = (bf16[256,4096]{1,0:T(8,128)(2,1)S(1)}, bf16[256,4096]{1,0:T(8,128)(2,1)S(1)}, u32[]{:S(2)}, u32[]{:S(2)}) collective-permute-start(bf16[256,4096]{1,0:T(8,128)(2,1)S(1)} %output_product.2), channel_id=1, source_target_pairs={{0,1},{1,0},{2,3},{3,2},{4,5},{5,4},{6,7},{7,6},{8,9},{9,8},{10,11... | collective-permute-start | bytes 6291464 | tf_op jit(solution)/shard_map/output/ppermute | solution.py:27
